TPU v7x, 32 devices: a whole 2x2x4 slice. The times are simulated.
32 devices in a mesh: dp: 8 (over z, x), mp: 4 (over y, core).
Axes of the slice: x: 2, y: 2, z: 4, core: 2. Of those that a mesh axis runs over, the one named last changes fastest.
Arguments:
- clean_mel: bfloat16 [2, 8, 1024, 80], P(None, 'dp'), may hold values from -6 to 6
- noise_mel: bfloat16 [2, 8, 1024, 80], P(None, 'dp'), may hold values from -6 to 6
- lengths: int32 [2, 8], P(None, 'dp'), may hold values from 128 to 1024, as said below
- span_start: int32 [2, 8], P(None, 'dp'), may hold values from 0 to 308, as said below
- span_end: int32 [2, 8], P(None, 'dp'), may hold values from 1 to 1024, as said below
- phone_ids: int32 [2, 8, 1024], P(None, 'dp'), may hold values from 0 to 127
- flow_steps: int32 [2, 8], P(None, 'dp'), may hold values from 0 to 1000
- in_table: float32 [288, 1024], P(None, ('dp', 'mp')), may hold values from -0.5 to 0.5
- channel_rows: float32 [39, 1024], P(None, ('dp', 'mp')), as said below
- attn_qkv: float32 [1024, 3072], P('dp', 'mp'), may hold values from -0.1875 to 0.1875
- attn_out: float32 [1024, 1024], P('mp', 'dp'), may hold values from -0.375 to 0.375
- ffn_up: float32 [1024, 4096], P('dp', 'mp'), may hold values from -0.1875 to 0.1875
- ffn_down: float32 [4096, 1024], P('mp', 'dp'), may hold values from -0.09375 to 0.09375
- mel_head: float32 [1024, 80], P(('dp', 'mp')), may hold values from -0.1875 to 0.1875
- table_first: float32 [288, 1024], P(None, ('dp', 'mp')), may hold values from -1.9073486e-05 to 1.9073486e-05
- channel_first: float32 [39, 1024], P(None, ('dp', 'mp')), may hold values from -1.9073486e-05 to 1.9073486e-05
- qkv_first: float32 [1024, 3072], P('dp', 'mp'), may hold values from -1.9073486e-05 to 1.9073486e-05
- merge_first: float32 [1024, 1024], P('mp', 'dp'), may hold values from -1.9073486e-05 to 1.9073486e-05
- upward_first: float32 [1024, 4096], P('dp', 'mp'), may hold values from -1.9073486e-05 to 1.9073486e-05
- downward_first: float32 [4096, 1024], P('mp', 'dp'), may hold values from -1.9073486e-05 to 1.9073486e-05
- head_first: float32 [1024, 80], P(('dp', 'mp')), may hold values from -1.9073486e-05 to 1.9073486e-05
- table_second: float32 [288, 1024], P(None, ('dp', 'mp')), may hold values from 1.1538745e-13 to 4.615498e-13
- channel_second: float32 [39, 1024], P(None, ('dp', 'mp')), may hold values from 7.692497e-13 to 3.0769987e-12
- qkv_second: float32 [1024, 3072], P('dp', 'mp'), may hold values from 7.692497e-13 to 3.0769987e-12
- merge_second: float32 [1024, 1024], P('mp', 'dp'), may hold values from 7.692497e-13 to 3.0769987e-12
- upward_second: float32 [1024, 4096], P('dp', 'mp'), may hold values from 7.692497e-13 to 3.0769987e-12
- downward_second: float32 [4096, 1024], P('mp', 'dp'), may hold values from 7.692497e-13 to 3.0769987e-12
- head_second: float32 [1024, 80], P(('dp', 'mp')), may hold values from 7.692497e-13 to 3.0769987e-12
Outputs:
- loss: float32 [], replicated
- grad_norm: float32 [], replicated
- table_new: float32 [288, 1024], P(None, ('dp', 'mp'))
- table_first_new: float32 [288, 1024], P(None, ('dp', 'mp'))
- table_second_new: float32 [288, 1024], P(None, ('dp', 'mp'))
- channel_new: float32 [39, 1024], P(None, ('dp', 'mp'))
- channel_first_new: float32 [39, 1024], P(None, ('dp', 'mp'))
- channel_second_new: float32 [39, 1024], P(None, ('dp', 'mp'))
- qkv_new: float32 [1024, 3072], P('dp', 'mp')
- qkv_first_new: float32 [1024, 3072], P('dp', 'mp')
- qkv_second_new: float32 [1024, 3072], P('dp', 'mp')
- merge_new: float32 [1024, 1024], P('mp', 'dp')
- merge_first_new: float32 [1024, 1024], P('mp', 'dp')
- merge_second_new: float32 [1024, 1024], P('mp', 'dp')
- upward_new: float32 [1024, 4096], P('dp', 'mp')
- upward_first_new: float32 [1024, 4096], P('dp', 'mp')
- upward_second_new: float32 [1024, 4096], P('dp', 'mp')
- downward_new: float32 [4096, 1024], P('mp', 'dp')
- downward_first_new: float32 [4096, 1024], P('mp', 'dp')
- downward_second_new: float32 [4096, 1024], P('mp', 'dp')
- head_new: float32 [1024, 80], P(('dp', 'mp'))
- head_first_new: float32 [1024, 80], P(('dp', 'mp'))
- head_second_new: float32 [1024, 80], P(('dp', 'mp'))
Inputs may be any that keep to these rules, and one draw needn't show every extreme that they name: `lengths`: in every draw some utterance has exactly 1024 frames. `span_start`: the span lies inside its utterance and covers about 70 to 100 percent of its frames. span_end is greater than span_start and at most the utterance's length. `channel_rows`: taps are of order one over the square root of 31; gains are near one.
All inputs are finite; a program needn't handle non-finite values.
Results may differ from a plain program's by a relative error of at most 0.015.
Values may be sent and summed in bfloat16 or wider, within the bound.
A program may use at most 512 MiB of HBM per device.

v0:
```python
import jax
import jax.numpy as jnp
from jax import lax
from jax.sharding import PartitionSpec as P

HEADS = 16
HEAD_DIM = 64
PHONES = 128
KERNEL = 31
LEN = 1024
MICRO = 2
TSTEPS = 1000
STEP = 10


SIGMA = 1e-05
BETA_ONE = 0.9
BETA_TWO = 0.999
EPSILON = 1e-08
DECAY = 0.01
RATE = 0.15
CLIP_AT = 0.1
NORM_EPS = 1e-05


def gelu(v):
    return jax.nn.gelu(v, approximate=True)


def layer_norm(v, gain, bias):
    centered = v - jnp.mean(v, axis=-1, keepdims=True)
    spread = jnp.mean(centered * centered, axis=-1, keepdims=True)
    return centered * lax.rsqrt(spread + NORM_EPS) * gain + bias


def conv_mix(hidden, taps, bias, valid):
    masked = hidden * valid[..., None]
    half = taps.shape[0] // 2
    length = hidden.shape[-2]
    widths = [(0, 0)] * (hidden.ndim - 2) + [(half, half), (0, 0)]
    padded = jnp.pad(masked, widths)
    total = jnp.zeros_like(hidden) + bias
    for offset in range(taps.shape[0]):
        total = total + taps[offset] * padded[..., offset : offset + length, :]
    return total


def front(hidden, channel, valid):
    vecs = channel[KERNEL:]
    inner = hidden + gelu(conv_mix(hidden, channel[:KERNEL], vecs[7], valid))
    return (inner, layer_norm(inner, vecs[0], vecs[1]))


def adam_update(weight, first, second, grad, factor):
    clipped = grad * factor
    first_new = BETA_ONE * first + (1.0 - BETA_ONE) * clipped
    second_new = BETA_TWO * second + (1.0 - BETA_TWO) * clipped * clipped
    first_hat = first_new / (1.0 - BETA_ONE**STEP)
    second_hat = second_new / (1.0 - BETA_TWO**STEP)
    weight_new = weight - RATE * (first_hat / (jnp.sqrt(second_hat) + EPSILON) + DECAY * weight)
    return (weight_new, first_new, second_new)


def tdot(left, right):
    return lax.dot_general(
        left, right, (((0,), (0,)), ((), ())), preferred_element_type=jnp.float32
    )


def rdot(left, right):
    return lax.dot_general(
        left, right, (((1,), (1,)), ((), ())), preferred_element_type=jnp.float32
    )


def scores_of(query, key, slopes, distance, valid):
    raw = jnp.einsum("uqhd,ukhd->uhqk", query, key, preferred_element_type=jnp.float32)
    score = raw * query.shape[-1] ** (-0.5) - slopes[None, :, None, None] * distance
    return jnp.where(valid[:, None, None, :] > 0, score, -1000000000.0)


def reduce_grads(grads):
    shares = (
        lax.psum_scatter(
            grads[0].astype(jnp.bfloat16), "dp", scatter_dimension=0, tiled=True
        ).astype(jnp.float32),
        lax.psum_scatter(
            grads[1].astype(jnp.bfloat16), "dp", scatter_dimension=1, tiled=True
        ).astype(jnp.float32),
        lax.psum_scatter(
            grads[2].astype(jnp.bfloat16), "dp", scatter_dimension=0, tiled=True
        ).astype(jnp.float32),
        lax.psum_scatter(
            grads[3].astype(jnp.bfloat16), "dp", scatter_dimension=1, tiled=True
        ).astype(jnp.float32),
        lax.psum_scatter(
            grads[4].astype(jnp.bfloat16), "dp", scatter_dimension=1, tiled=True
        ).astype(jnp.float32),
        lax.psum_scatter(
            grads[5].astype(jnp.bfloat16), "dp", scatter_dimension=1, tiled=True
        ).astype(jnp.float32),
        lax.psum_scatter(
            grads[6].astype(jnp.bfloat16), "dp", scatter_dimension=0, tiled=True
        ).astype(jnp.float32),
    )
    place = lax.axis_index("mp")
    part = shares[4].shape[1] // lax.axis_size("mp")
    small = tuple(
        (
            lax.dynamic_slice_in_dim(x, place * part, part, dim)
            for x, dim in zip(shares[4:], (1, 1, 0))
        )
    )
    return tuple(shares[:4]) + small


def shards(
    clean_mel,
    noise_mel,
    lengths,
    span_start,
    span_end,
    phone_ids,
    flow_steps,
    in_table,
    channel_rows,
    attn_qkv,
    attn_out,
    ffn_up,
    ffn_down,
    mel_head,
    table_first,
    channel_first,
    qkv_first,
    merge_first,
    upward_first,
    downward_first,
    head_first,
    table_second,
    channel_second,
    qkv_second,
    merge_second,
    upward_second,
    downward_second,
    head_second,
):
    bf = jnp.bfloat16
    w_in, w_channel, w_head = (
        lax.all_gather(in_table.astype(bf), ("dp", "mp"), axis=1, tiled=True),
        lax.all_gather(channel_rows.astype(bf), ("dp", "mp"), axis=1, tiled=True),
        lax.all_gather(mel_head.astype(bf), ("dp", "mp"), axis=0, tiled=True),
    )
    w_qkv, w_out, w_up, w_down = (
        lax.all_gather(attn_qkv.astype(bf), "dp", axis=0, tiled=True),
        lax.all_gather(attn_out.astype(bf), "dp", axis=1, tiled=True),
        lax.all_gather(ffn_up.astype(bf), "dp", axis=0, tiled=True),
        lax.all_gather(ffn_down.astype(bf), "dp", axis=1, tiled=True),
    )
    channel = w_channel.astype(jnp.float32)
    place = jnp.arange(LEN)
    valid = (place[None, None, :] < lengths[:, :, None]).astype(jnp.float32)
    masked = (
        (place[None, None, :] >= span_start[:, :, None])
        & (place[None, None, :] < span_end[:, :, None])
    ).astype(jnp.float32)
    counts = lax.psum(jnp.sum(masked, axis=(1, 2)), "dp")
    inverse = 1.0 / counts
    heads_dev = w_qkv.shape[1] // (3 * HEAD_DIM)
    slopes = jnp.exp2(
        -8.0
        * (lax.axis_index("mp") * heads_dev + jnp.arange(heads_dev) + 1).astype(jnp.float32)
        / HEADS
    )
    distance = jnp.abs(place[:, None] - place[None, :]).astype(jnp.float32)
    units = lengths.shape[1]
    rows = units * LEN
    loss_local = jnp.zeros((), jnp.float32)
    totals = None
    for batch in range(MICRO):
        valid_b = valid[batch]
        tau = (flow_steps[batch].astype(jnp.float32) / TSTEPS)[:, None, None]
        clean = clean_mel[batch].astype(jnp.float32)
        noise = noise_mel[batch].astype(jnp.float32)
        noisy = (1.0 - (1.0 - SIGMA) * tau) * noise + tau * clean
        context = clean * (valid_b * (1.0 - masked[batch]))[..., None]
        target = (clean - (1.0 - SIGMA) * noise).reshape(rows, -1)
        onehot = (phone_ids[batch][..., None] == jnp.arange(PHONES)).astype(bf)
        features = jnp.concatenate([noisy.astype(bf), context.astype(bf), onehot], axis=-1).reshape(
            rows, -1
        )
        start = jnp.dot(features, w_in, preferred_element_type=jnp.float32) + channel[KERNEL + 6]
        (inner, normed), front_back = jax.vjp(
            lambda h, c: front(h, c, valid_b), start.reshape(units, LEN, -1), channel
        )
        act_one = normed.reshape(rows, -1).astype(bf)
        packed = (
            jnp.dot(act_one, w_qkv, preferred_element_type=jnp.float32)
            .astype(bf)
            .reshape(units, LEN, heads_dev, 3, HEAD_DIM)
        )
        query, key, value = (packed[:, :, :, 0], packed[:, :, :, 1], packed[:, :, :, 2])
        score = scores_of(query, key, slopes, distance, valid_b)
        top = jnp.max(score, axis=-1, keepdims=True)
        total = top + jnp.log(jnp.sum(jnp.exp(score - top), axis=-1, keepdims=True))
        prob = jnp.exp(score - total)
        mixed = (
            jnp.einsum(
                "uhqk,ukhd->uqhd", prob.astype(bf), value, preferred_element_type=jnp.float32
            )
            .astype(bf)
            .reshape(rows, -1)
        )
        attn = lax.psum(
            jnp.dot(mixed, w_out, preferred_element_type=jnp.float32).astype(jnp.bfloat16), "mp"
        ).astype(jnp.float32)
        second = inner.reshape(rows, -1) + attn
        normed_two, middle_back = jax.vjp(
            lambda h, c: layer_norm(h, c[KERNEL + 2], c[KERNEL + 3]), second, channel
        )
        act_two = normed_two.astype(bf)
        hidden = jnp.dot(act_two, w_up, preferred_element_type=jnp.float32)
        activated = gelu(hidden).astype(bf)
        third = second + lax.psum(
            jnp.dot(activated, w_down, preferred_element_type=jnp.float32).astype(jnp.bfloat16),
            "mp",
        ).astype(jnp.float32)
        normed_three, tail_back = jax.vjp(
            lambda h, c: layer_norm(h, c[KERNEL + 4], c[KERNEL + 5]), third, channel
        )
        act_three = normed_three.astype(bf)
        pred = jnp.dot(act_three, w_head, preferred_element_type=jnp.float32)
        error = pred - target
        weight_rows = masked[batch].reshape(rows, 1) * inverse[batch]
        loss_local = loss_local + jnp.sum(weight_rows * error * error)
        dpred = (2.0 * weight_rows * error).astype(bf)
        g_head = tdot(act_three, dpred)
        dthird, dchan_three = tail_back(rdot(dpred, w_head))
        dffn = dthird.astype(bf)
        g_down = tdot(activated, dffn)
        dact = rdot(dffn, w_down)
        dhidden = jax.vjp(gelu, hidden)[1](dact)[0].astype(bf)
        g_up = tdot(act_two, dhidden)
        da2 = lax.psum(rdot(dhidden, w_up).astype(jnp.bfloat16), "mp").astype(jnp.float32)
        dnorm_two, dchan_two = middle_back(da2)
        dsecond = dthird + dnorm_two
        dattn = dsecond.astype(bf)
        g_out = tdot(mixed, dattn)
        dmixed = rdot(dattn, w_out).astype(bf).reshape(units, LEN, heads_dev, HEAD_DIM)
        prob = jnp.exp(scores_of(query, key, slopes, distance, valid_b) - total)
        dvalue = jnp.einsum(
            "uhqk,uqhd->ukhd", prob.astype(bf), dmixed, preferred_element_type=jnp.float32
        )
        dprob = jnp.einsum("uqhd,ukhd->uhqk", dmixed, value, preferred_element_type=jnp.float32)
        dscore = prob * (dprob - jnp.sum(prob * dprob, axis=-1, keepdims=True))
        draw = (dscore * HEAD_DIM ** (-0.5)).astype(bf)
        dquery = jnp.einsum("uhqk,ukhd->uqhd", draw, key, preferred_element_type=jnp.float32)
        dkey = jnp.einsum("uhqk,uqhd->ukhd", draw, query, preferred_element_type=jnp.float32)
        dpacked = jnp.stack([dquery, dkey, dvalue], axis=3).astype(bf).reshape(rows, -1)
        g_qkv = tdot(act_one, dpacked)
        da1 = lax.psum(rdot(dpacked, w_qkv).astype(jnp.bfloat16), "mp").astype(jnp.float32)
        dstart, dchan_one = front_back(
            (dsecond.reshape(units, LEN, -1), da1.reshape(units, LEN, -1))
        )
        dstart = dstart.reshape(rows, -1)
        g_in = tdot(features, dstart.astype(bf))
        bias_row = jnp.zeros_like(channel).at[KERNEL + 6].set(jnp.sum(dstart, axis=0))
        g_chan = dchan_one + dchan_two + dchan_three + bias_row
        grads = (g_qkv, g_out, g_up, g_down, g_in, g_chan, g_head)
        grads = reduce_grads(grads)
        totals = grads if totals is None else tuple((a + b for a, b in zip(totals, grads)))
    squares = sum((jnp.sum(x * x) for x in totals))
    loss = lax.psum(loss_local, "dp")
    norm_sq = lax.psum(squares, ("dp", "mp"))
    grad_norm = jnp.sqrt(norm_sq)
    factor = CLIP_AT / jnp.maximum(grad_norm, CLIP_AT)
    qw, qm, qv = adam_update(attn_qkv, qkv_first, qkv_second, totals[0], factor)
    ow, om, ov = adam_update(attn_out, merge_first, merge_second, totals[1], factor)
    uw, um, uv = adam_update(ffn_up, upward_first, upward_second, totals[2], factor)
    dw, dm, dv = adam_update(ffn_down, downward_first, downward_second, totals[3], factor)
    tw, tm, tv = adam_update(in_table, table_first, table_second, totals[4], factor)
    cw, cm, cv = adam_update(channel_rows, channel_first, channel_second, totals[5], factor)
    hw, hm, hv = adam_update(mel_head, head_first, head_second, totals[6], factor)
    return (
        loss,
        grad_norm,
        tw,
        tm,
        tv,
        cw,
        cm,
        cv,
        qw,
        qm,
        qv,
        ow,
        om,
        ov,
        uw,
        um,
        uv,
        dw,
        dm,
        dv,
        hw,
        hm,
        hv,
    )


def solution(mesh):
    return jax.shard_map(
        shards,
        mesh=mesh,
        in_specs=(
            P(None, "dp", None, None),
            P(None, "dp", None, None),
            P(None, "dp"),
            P(None, "dp"),
            P(None, "dp"),
            P(None, "dp", None),
            P(None, "dp"),
            P(None, ("dp", "mp")),
            P(None, ("dp", "mp")),
            P("dp", "mp"),
            P("mp", "dp"),
            P("dp", "mp"),
            P("mp", "dp"),
            P(("dp", "mp"), None),
            P(None, ("dp", "mp")),
            P(None, ("dp", "mp")),
            P("dp", "mp"),
            P("mp", "dp"),
            P("dp", "mp"),
            P("mp", "dp"),
            P(("dp", "mp"), None),
            P(None, ("dp", "mp")),
            P(None, ("dp", "mp")),
            P("dp", "mp"),
            P("mp", "dp"),
            P("dp", "mp"),
            P("mp", "dp"),
            P(("dp", "mp"), None),
        ),
        out_specs=(
            P(),
            P(),
            P(None, ("dp", "mp")),
            P(None, ("dp", "mp")),
            P(None, ("dp", "mp")),
            P(None, ("dp", "mp")),
            P(None, ("dp", "mp")),
            P(None, ("dp", "mp")),
            P("dp", "mp"),
            P("dp", "mp"),
            P("dp", "mp"),
            P("mp", "dp"),
            P("mp", "dp"),
            P("mp", "dp"),
            P("dp", "mp"),
            P("dp", "mp"),
            P("dp", "mp"),
            P("mp", "dp"),
            P("mp", "dp"),
            P("mp", "dp"),
            P(("dp", "mp"), None),
            P(("dp", "mp"), None),
            P(("dp", "mp"), None),
        ),
        check_vma=False,
    )
```

profile of v0, /device:TPU:0, one launch (start us, length us, event | category | flops | bytes accessed | tf_op | source)
XLA Modules:
  0.0 1992.0 jit_solution(1002403422240108166)
XLA Ops:
  13.2 44.6 %all_gather.22 = bf16[39,1024]{0,1:T(8,128)(2,1)S(1)} all-gather(bf16[39,32]{0,1:T(8,128)(2,1)S(1)} %convert_element_type.515), channel_id=1, replica_groups=mesh['dp'=8,'mp'=4] {'dp','mp'}, dimensions={1}, use_global_device_ids=true | all-gather | bytes 82368 | tf_op jit(solution)/shard_map/all_gather | solution.py:150
  89.1 38.8 %all_gather.21 = bf16[288,1024]{0,1:T(8,128)(2,1)S(1)} all-gather(bf16[288,32]{0,1:T(8,128)(2,1)S(1)} %convert_element_type.514), channel_id=1, replica_groups=mesh['dp'=8,'mp'=4] {'dp','mp'}, dimensions={1}, use_global_device_ids=true | all-gather | bytes 608256 | tf_op jit(solution)/shard_map/all_gather | solution.py:149
  134.2 34.4 %fusion.244 = (f32[1024]{0:T(1024)S(1)}, f32[1,1024,1024]{2,1,0:T(8,128)}, f32[1,1024,1024]{2,1,0:T(8,128)}) fusion(f32[1024,1024]{1,0:T(8,128)S(1)} %fusion.186, f32[1024]{0:T(1024)S(1)} %get-tuple-element.263, f32[1024]{0:T(1024)S(1)} %get-tuple-element.250, f32[1024]{0:T(1024)S(1)} %get-tuple-element.251, f32[1024]{0:T(1024)S(1)} %get-tuple-element.252, ...), kind=kLoop, calls=%fused_computation.576 | loop fusion | flops 77593600 | bytes 16920576 | tf_op jit(solution)/shard_map/jvp()/reduce_sum | solution.py:31
  168.9 34.3 %fusion.246 = (f32[1024]{0:T(1024)S(1)}, f32[1,1024,1024]{2,1,0:T(8,128)}, f32[1,1024,1024]{2,1,0:T(8,128)}) fusion(f32[1024,1024]{1,0:T(8,128)S(1)} %fusion.187, f32[1024]{0:T(1024)S(1)} %get-tuple-element.263, f32[1024]{0:T(1024)S(1)} %get-tuple-element.250, f32[1024]{0:T(1024)S(1)} %get-tuple-element.251, f32[1024]{0:T(1024)S(1)} %get-tuple-element.252, ...), kind=kLoop, calls=%fused_computation.577 | loop fusion | flops 77593600 | bytes 16920576 | tf_op jit(solution)/shard_map/jvp()/reduce_sum | solution.py:31
  207.2 27.7 %all_gather.24 = bf16[256,1024]{1,0:T(8,128)(2,1)S(1)} all-gather(bf16[256,128]{1,0:T(8,128)(2,1)S(1)} %convert_element_type.527), channel_id=1, replica_groups=mesh['dp'=8,'mp'=4] {'dp'}, dimensions={1}, use_global_device_ids=true | all-gather | bytes 589824 | tf_op jit(solution)/shard_map/all_gather | solution.py:155
  308.7 81.5 %all-reduce.159.cloned.1.call-done = (bf16[1024,1024]{1,0:T(8,128)(2,1)}, bf16[1024,1024]{1,0:T(8,128)(2,1)}) async-done(((bf16[1024,1024]{1,0:T(8,128)(2,1)}, bf16[1024,1024]{1,0:T(8,128)(2,1)}), (bf16[1024,1024]{1,0:T(8,128)(2,1)}, bf16[1024,1024]{1,0:T(8,128)(2,1)})) %all-reduce.159.cloned.1.call-update) | async-done | bytes 4194320 | tf_op jit(solution)/shard_map/psum | solution.py:213
  400.4 42.2 %all-gather.6.cloned.1.call-done = bf16[1024,1024]{1,0:T(8,128)(2,1)} async-done(((bf16[128,1024]{1,0:T(8,128)(2,1)}), bf16[1024,1024]{1,0:T(8,128)(2,1)}) %all-gather.6.cloned.1.call-update) | async-done | bytes 2097168 | tf_op jit(solution)/shard_map/all_gather | solution.py:156
  455.0 39.8 %all-gather.8.cloned.1.call-done = bf16[1024,1024]{1,0:T(8,128)(2,1)} async-done(((bf16[1024,128]{1,0:T(8,128)(2,1)}), bf16[1024,1024]{1,0:T(8,128)(2,1)}) %all-gather.8.cloned.1.call-update) | async-done | bytes 2097168 | tf_op jit(solution)/shard_map/all_gather | solution.py:157
  506.5 40.2 %all_gather.27 = bf16[1024,80]{1,0:T(8,128)(2,1)S(1)} all-gather(bf16[32,80]{1,0:T(8,128)(2,1)S(1)} %convert_element_type.537), channel_id=1, replica_groups=mesh['dp'=8,'mp'=4] {'dp','mp'}, dimensions={0}, use_global_device_ids=true | all-gather | bytes 168960 | tf_op jit(solution)/shard_map/all_gather | solution.py:151
  546.7 45.4 %all-reduce.157.cloned.1.call-done = (bf16[1024,1024]{1,0:T(8,128)(2,1)}, bf16[1024,1024]{1,0:T(8,128)(2,1)}) async-done(((bf16[1024,1024]{1,0:T(8,128)(2,1)}, bf16[1024,1024]{1,0:T(8,128)(2,1)}), (bf16[1024,1024]{1,0:T(8,128)(2,1)}, bf16[1024,1024]{1,0:T(8,128)(2,1)})) %all-reduce.157.cloned.1.call-update) | async-done | bytes 4194320 | tf_op jit(solution)/shard_map/psum | solution.py:223
  633.9 85.9 %all-reduce.155.cloned.1.call-done = (bf16[1024,1024]{1,0:T(8,128)(2,1)}, bf16[1024,1024]{1,0:T(8,128)(2,1)}) async-done(((bf16[1024,1024]{1,0:T(8,128)(2,1)}, bf16[1024,1024]{1,0:T(8,128)(2,1)}), (bf16[1024,1024]{1,0:T(8,128)(2,1)}, bf16[1024,1024]{1,0:T(8,128)(2,1)})) %all-reduce.155.cloned.1.call-update) | async-done | bytes 4194320 | tf_op jit(solution)/shard_map/psum | solution.py:243
  755.9 22.5 %fusion.135 = bf16[1,1024,4,1,64]{1,4,2,3,0:T(8,128)(2,1)S(1)} fusion(f32[4,1024,1024]{1,2,0:T(8,128)} %fusion.167, f32[4,1024,1024]{1,2,0:T(8,128)} %get-tuple-element.454, f32[4,1024]{1,0:T(4,128)S(1)} %log_add_fusion, bf16[1,1024,4,3,64]{1,4,3,2,0:T(8,128)(2,1)S(1)} %bitcast.481), kind=kOutput, calls=%fused_computation.340 | convolution fusion | flops 566236160 | bytes 68190208 | tf_op jit(solution)/shard_map/uhqk,uqhd->ukhd/dot_general | solution.py:257
  778.5 28.6 %fusion.132 = bf16[1,1024,4,1,64]{1,4,2,3,0:T(8,128)(2,1)} fusion(f32[4,1024,1024]{1,2,0:T(8,128)} %fusion.167, f32[4,1024,1024]{1,2,0:T(8,128)} %get-tuple-element.454, f32[4,1024]{1,0:T(4,128)S(1)} %log_add_fusion, bf16[1,1024,4,3,64]{1,4,3,2,0:T(8,128)(2,1)S(1)} %bitcast.482), kind=kOutput, calls=%fused_computation.339 | convolution fusion | flops 566236160 | bytes 68190208 | tf_op jit(solution)/shard_map/uhqk,ukhd->uqhd/dot_general | solution.py:256
  826.7 23.3 %fusion.141 = bf16[1,1024,4,1,64]{1,4,2,3,0:T(8,128)(2,1)} fusion(f32[4,1024,1024]{1,2,0:T(8,128)} %fusion.166, f32[4,1024,1024]{1,2,0:T(8,128)} %get-tuple-element.452, f32[4,1024]{1,0:T(4,128)S(1)} %copy-done.88, bf16[1,1024,4,3,64]{1,4,3,2,0:T(8,128)(2,1)S(1)} %bitcast.476), kind=kOutput, calls=%fused_computation.342 | convolution fusion | flops 566236160 | bytes 68190208 | tf_op jit(solution)/shard_map/uhqk,uqhd->ukhd/dot_general | solution.py:257
  850.0 28.8 %fusion.138 = bf16[1,1024,4,1,64]{1,4,2,3,0:T(8,128)(2,1)} fusion(f32[4,1024,1024]{1,2,0:T(8,128)} %fusion.166, f32[4,1024,1024]{1,2,0:T(8,128)} %get-tuple-element.452, f32[4,1024]{1,0:T(4,128)S(1)} %copy-done.88, bf16[1,1024,4,3,64]{1,4,3,2,0:T(8,128)(2,1)S(1)} %bitcast.477), kind=kOutput, calls=%fused_computation.341 | convolution fusion | flops 566236160 | bytes 68190208 | tf_op jit(solution)/shard_map/uhqk,ukhd->uqhd/dot_general | solution.py:256
  934.8 39.8 %all-reduce.153.cloned.1.call-done = (bf16[1024,1024]{1,0:T(8,128)(2,1)}, bf16[1024,1024]{1,0:T(8,128)(2,1)}) async-done(((bf16[1024,1024]{1,0:T(8,128)(2,1)}, bf16[1024,1024]{1,0:T(8,128)(2,1)}), (bf16[1024,1024]{1,0:T(8,128)(2,1)}, bf16[1024,1024]{1,0:T(8,128)(2,1)})) %all-reduce.153.cloned.1.call-update) | async-done | bytes 4194320 | tf_op jit(solution)/shard_map/psum | solution.py:260
  996.6 28.5 %broadcast_multiply_fusion.2 = (f32[1,1024,1024]{2,1,0:T(8,128)}, f32[1,1024,1024]{2,1,0:T(8,128)}, f32[1,1024,1024]{2,1,0:T(8,128)}, f32[1,1024,1024]{2,1,0:T(8...) fusion(f32[1,1024,1024]{2,1,0:T(8,128)} %get-tuple-element.316,, ...), kind=kLoop, calls=%fused_computation.261 | loop fusion | flops 18874368 | bytes 79765504 | tf_op jit(solution)/shard_map/transpose(jvp())/mul | solution.py:44
  1062.9 36.8 %broadcast_multiply_fusion.4 = (f32[1,1024,1024]{2,1,0:T(8,128)}, f32[1,1024,1024]{2,1,0:T(8,128)}, f32[1,1024,1024]{2,1,0:T(8,128)}, f32[1,1024,1024]{2,1,0:T(8...) fusion(f32[1,1024,1024]{2,1,0:T(8,128)} %get-tuple-element.316,, ...), kind=kLoop, calls=%fused_computation.263 | loop fusion | flops 27262976 | bytes 117493760 | tf_op jit(solution)/shard_map/transpose(jvp())/mul | solution.py:44
  1118.0 37.0 %pad_add_fusion = f32[1,1054,1024]{2,1,0:T(8,128)} fusion(f32[1,1024,1024]{2,1,0:T(8,128)} %get-tuple-element.377, f32[1,1024,1024]{2,1,0:T(8,128)} %get-tuple-element.378, f32[1,1024,1024]{2,1,0:T(8,128)} %get-tuple-element.379, f32[1,1024,1024]{2,1,0:T(8,128)} %get-tuple-element.380, f32[1,1024,1024]{2,1,0:T(8,128)} %get-tuple-element.381, ...), kind=kLoop, calls=%fused_computation.58 | loop fusion | flops 25903104 | bytes 109174784 | tf_op jit(solution)/shard_map/transpose(jvp())/add_any | solution.py:44
  1193.6 28.5 %broadcast_multiply_fusion.3 = (f32[1,1024,1024]{2,1,0:T(8,128)}, f32[1,1024,1024]{2,1,0:T(8,128)}, f32[1,1024,1024]{2,1,0:T(8,128)}, f32[1,1024,1024]{2,1,0:T(8...) fusion(f32[1,1024,1024]{2,1,0:T(8,128)} %get-tuple-element.313,, ...), kind=kLoop, calls=%fused_computation.262 | loop fusion | flops 18874368 | bytes 79765504 | tf_op jit(solution)/shard_map/transpose(jvp())/mul | solution.py:44
  1222.5 37.0 %pad_add_fusion.1 = f32[1,1054,1024]{2,1,0:T(8,128)} fusion(f32[1,1024,1024]{2,1,0:T(8,128)} %get-tuple-element.346, f32[1,1024,1024]{2,1,0:T(8,128)} %get-tuple-element.347, f32[1,1024,1024]{2,1,0:T(8,128)} %get-tuple-element.348, f32[1,1024,1024]{2,1,0:T(8,128)} %get-tuple-element.349, f32[1,1024,1024]{2,1,0:T(8,128)} %get-tuple-element.350, ...), kind=kLoop, calls=%fused_computation.59 | loop fusion | flops 25903104 | bytes 109174784 | tf_op jit(solution)/shard_map/transpose(jvp())/add_any | solution.py:44
  1304.9 69.2 %reduce-scatter.47.cloned.1.call-done = bf16[128,1024]{1,0:T(8,128)(2,1)} async-done(((bf16[1024,1024]{1,0:T(8,128)(2,1)}), bf16[128,1024]{1,0:T(8,128)(2,1)}) %reduce-scatter.47.cloned.1.call-update) | async-done | bytes 262160
  1376.0 68.3 %reduce-scatter.41.cloned.1.call-done = bf16[128,1024]{1,0:T(8,128)(2,1)} async-done(((bf16[1024,1024]{1,0:T(8,128)(2,1)}), bf16[128,1024]{1,0:T(8,128)(2,1)}) %reduce-scatter.41.cloned.1.call-update) | async-done | bytes 262160 | tf_op jit(solution)/shard_map/reduce_scatter | solution.py:90
  1444.3 69.9 %reduce-scatter.39.cloned.1.call-done = bf16[128,1024]{1,0:T(8,128)(2,1)} async-done(((bf16[1024,1024]{1,0:T(8,128)(2,1)}), bf16[128,1024]{1,0:T(8,128)(2,1)}) %reduce-scatter.39.cloned.1.call-update) | async-done | bytes 262160 | tf_op jit(solution)/shard_map/reduce_scatter | solution.py:90
  1516.0 62.2 %reduce-scatter.57.cloned.1.call-done = bf16[128,39]{1,0:T(8,128)(2,1)} async-done(((bf16[1024,39]{1,0:T(8,128)(2,1)}), bf16[128,39]{1,0:T(8,128)(2,1)}) %reduce-scatter.57.cloned.1.call-update) | async-done | bytes 10000
  1579.0 63.3 %reduce-scatter.55.cloned.1.call-done = bf16[128,39]{1,0:T(8,128)(2,1)} async-done(((bf16[1024,39]{1,0:T(8,128)(2,1)}), bf16[128,39]{1,0:T(8,128)(2,1)}) %reduce-scatter.55.cloned.1.call-update) | async-done | bytes 10000
  1643.7 65.7 %reduce-scatter.37.cloned.1.call-done = bf16[128,768]{1,0:T(8,128)(2,1)} async-done(((bf16[1024,768]{1,0:T(8,128)(2,1)}), bf16[128,768]{1,0:T(8,128)(2,1)}) %reduce-scatter.37.cloned.1.call-update) | async-done | bytes 196624 | tf_op jit(solution)/shard_map/reduce_scatter | solution.py:84
  1709.5 67.6 %reduce-scatter.35.cloned.1.call-done = bf16[128,768]{1,0:T(8,128)(2,1)} async-done(((bf16[1024,768]{1,0:T(8,128)(2,1)}), bf16[128,768]{1,0:T(8,128)(2,1)}) %reduce-scatter.35.cloned.1.call-update) | async-done | bytes 196624 | tf_op jit(solution)/shard_map/reduce_scatter | solution.py:84
  1781.4 60.2 %reduce-scatter.53.cloned.1.call-done = bf16[128,288]{1,0:T(8,128)(2,1)} async-done(((bf16[1024,288]{1,0:T(8,128)(2,1)}), bf16[128,288]{1,0:T(8,128)(2,1)}) %reduce-scatter.53.cloned.1.call-update) | async-done | bytes 73744
  1841.6 65.2 %reduce-scatter.51.cloned.1.call-done = bf16[128,288]{1,0:T(8,128)(2,1)} async-done(((bf16[1024,288]{1,0:T(8,128)(2,1)}), bf16[128,288]{1,0:T(8,128)(2,1)}) %reduce-scatter.51.cloned.1.call-update) | async-done | bytes 73744
  1910.9 19.9 psum.82
  1930.8 36.8 %psum.87 = f32[]{:T(128)} all-reduce(f32[]{:T(128)S(6)} %add.1085), channel_id=1, replica_groups=mesh['dp'=8,'mp'=4] {'dp','mp'}, use_global_device_ids=true, to_apply=%region_142.143 | all-reduce | flops 1 | bytes 8 | tf_op jit(solution)/shard_map/psum | solution.py:273
  (661 shorter events, 491.2 us)
Async XLA Ops:
  7.2 239.2 %all-gather.4.cloned.1.call-start = ((), (), s32[]{:S(2)}) async-start(), calls=%async_computation.14 | async-start | bytes 1769472 | tf_op jit(solution)/shard_map/all_gather | solution.py:154
  9.0 381.2 %all-reduce.159.cloned.1.call-start = ((), (), s32[]{:S(2)}) async-start(), calls=%async_computation.34 | async-start | bytes 8388608 | tf_op jit(solution)/shard_map/psum | solution.py:213
  306.6 135.9 %all-gather.6.cloned.1.call-start = ((), (), s32[]{:S(2)}) async-start(), calls=%async_computation.15 | async-start | bytes 2359296 | tf_op jit(solution)/shard_map/all_gather | solution.py:156
  307.5 187.4 %all-gather.8.cloned.1.call-start = ((), (), s32[]{:S(2)}) async-start(), calls=%async_computation.16 | async-start | bytes 2359296 | tf_op jit(solution)/shard_map/all_gather | solution.py:157
  308.3 283.9 %all-reduce.157.cloned.1.call-start = ((), (), s32[]{:S(2)}) async-start(), calls=%async_computation.33 | async-start | bytes 8388608 | tf_op jit(solution)/shard_map/psum | solution.py:223
  505.8 214.0 %all-reduce.155.cloned.1.call-start = ((), (), s32[]{:S(2)}) async-start(), calls=%async_computation.32 | async-start | bytes 8388608 | tf_op jit(solution)/shard_map/psum | solution.py:243
  633.8 340.8 %all-reduce.153.cloned.1.call-start = ((), (), s32[]{:S(2)}) async-start(), calls=%async_computation.31 | async-start | bytes 8388608 | tf_op jit(solution)/shard_map/psum | solution.py:260
  888.6 409.8 %reduce-scatter.61.cloned.1.call-start = ((), (), s32[]{:S(2)}) async-start(), calls=%async_computation.30 | async-start | bytes 294912 | tf_op jit(solution)/shard_map/reduce_scatter | solution.py:102
  892.5 406.0 %reduce-scatter.59.cloned.1.call-start = ((), (), s32[]{:S(2)}) async-start(), calls=%async_computation.29 | async-start | bytes 294912 | tf_op jit(solution)/shard_map/reduce_scatter | solution.py:102
  894.0 405.9 %reduce-scatter.45.cloned.1.call-start = ((), (), s32[]{:S(2)}) async-start(), calls=%async_computation.22 | async-start | bytes 589824
  898.3 402.5 %reduce-scatter.43.cloned.1.call-start = ((), (), s32[]{:S(2)}) async-start(), calls=%async_computation.21 | async-start | bytes 589824
  902.3 401.5 %reduce-scatter.49.cloned.1.call-start = ((), (), s32[]{:S(2)}) async-start(), calls=%async_computation.24 | async-start | bytes 2359296
  911.4 462.7 %reduce-scatter.47.cloned.1.call-start = ((), (), s32[]{:S(2)}) async-start(), calls=%async_computation.23 | async-start | bytes 2359296
  920.8 523.5 %reduce-scatter.41.cloned.1.call-start = ((), (), s32[]{:S(2)}) async-start(), calls=%async_computation.20 | async-start | bytes 2359296 | tf_op jit(solution)/shard_map/reduce_scatter | solution.py:90
  928.0 586.3 %reduce-scatter.39.cloned.1.call-start = ((), (), s32[]{:S(2)}) async-start(), calls=%async_computation.19 | async-start | bytes 2359296 | tf_op jit(solution)/shard_map/reduce_scatter | solution.py:90
  934.3 643.9 %reduce-scatter.57.cloned.1.call-start = ((), (), s32[]{:S(2)}) async-start(), calls=%async_computation.28 | async-start | bytes 294912
  1222.1 420.2 %reduce-scatter.55.cloned.1.call-start = ((), (), s32[]{:S(2)}) async-start(), calls=%async_computation.27 | async-start | bytes 294912
  1276.9 432.6 %reduce-scatter.37.cloned.1.call-start = ((), (), s32[]{:S(2)}) async-start(), calls=%async_computation.18 | async-start | bytes 1769472 | tf_op jit(solution)/shard_map/reduce_scatter | solution.py:84
  1282.3 494.8 %reduce-scatter.35.cloned.1.call-start = ((), (), s32[]{:S(2)}) async-start(), calls=%async_computation.17 | async-start | bytes 1769472 | tf_op jit(solution)/shard_map/reduce_scatter | solution.py:84
  1287.4 554.2 %reduce-scatter.53.cloned.1.call-start = ((), (), s32[]{:S(2)}) async-start(), calls=%async_computation.26 | async-start | bytes 884736
  1292.8 614.0 %reduce-scatter.51.cloned.1.call-start = ((), (), s32[]{:S(2)}) async-start(), calls=%async_computation.25 | async-start | bytes 884736
  1292.9 680.3 %copy-start.86 = (f32[288,32]{0,1:T(8,128)S(1)}, f32[288,32]{0,1:T(8,128)}, u32[]{:S(2)}) copy-start(f32[288,32]{0,1:T(8,128)} %param.39) | copy-start | bytes 110596
  1292.9 681.9 %copy-start.80 = (f32[256,128]{1,0:T(8,128)S(1)}, f32[256,128]{1,0:T(8,128)}, u32[]{:S(2)}) copy-start(f32[256,128]{1,0:T(8,128)} %param.42) | copy-start | bytes 393220
  1292.9 681.9 %copy-start.93 = (f32[256,128]{1,0:T(8,128)S(1)}, f32[256,128]{1,0:T(8,128)}, u32[]{:S(2)}) copy-start(f32[256,128]{1,0:T(8,128)} %param.49) | copy-start | bytes 393220
  1295.7 679.1 %copy-start.94 = (f32[256,128]{1,0:T(8,128)S(1)}, f32[256,128]{1,0:T(8,128)}, u32[]{:S(2)}) copy-start(f32[256,128]{1,0:T(8,128)} %param.56) | copy-start | bytes 393220
  1295.7 679.9 %copy-start.49 = (f32[1024,128]{1,0:T(8,128)S(1)}, f32[1024,128]{1,0:T(8,128)}, u32[]{:S(2)}) copy-start(f32[1024,128]{1,0:T(8,128)} %param.44) | copy-start | bytes 1572868
  1297.0 681.4 %copy-start.56 = (f32[128,768]{1,0:T(8,128)S(1)}, f32[128,768]{1,0:T(8,128)}, u32[]{:S(2)}) copy-start(f32[128,768]{1,0:T(8,128)} %param.41) | copy-start | bytes 1179652
  1643.7 336.9 %copy-start.51 = (f32[128,1024]{1,0:T(8,128)S(1)}, f32[128,1024]{1,0:T(8,128)}, u32[]{:S(2)}) copy-start(f32[128,1024]{1,0:T(8,128)} %param.43) | copy-start | bytes 1572868
  1643.7 336.9 %copy-start.75 = (bf16[128,1024]{1,0:T(8,128)(2,1)S(1)}, bf16[128,1024]{1,0:T(8,128)(2,1)}, u32[]{:S(2)}) copy-start(bf16[128,1024]{1,0:T(8,128)(2,1)} %reduce-scatter.41.cloned.1.call-done) | copy-start | bytes 786436
  1643.7 336.9 %copy-start.76 = (bf16[128,1024]{1,0:T(8,128)(2,1)S(1)}, bf16[128,1024]{1,0:T(8,128)(2,1)}, u32[]{:S(2)}) copy-start(bf16[128,1024]{1,0:T(8,128)(2,1)} %reduce-scatter.39.cloned.1.call-done) | copy-start | bytes 786436
  1709.5 268.8 %copy-start.77 = (bf16[128,768]{1,0:T(8,128)(2,1)S(1)}, bf16[128,768]{1,0:T(8,128)(2,1)}, u32[]{:S(2)}) copy-start(bf16[128,768]{1,0:T(8,128)(2,1)} %reduce-scatter.37.cloned.1.call-done) | copy-start | bytes 589828
  1777.0 201.3 %copy-start.78 = (bf16[128,768]{1,0:T(8,128)(2,1)S(1)}, bf16[128,768]{1,0:T(8,128)(2,1)}, u32[]{:S(2)}) copy-start(bf16[128,768]{1,0:T(8,128)(2,1)} %reduce-scatter.35.cloned.1.call-done) | copy-start | bytes 589828
  (200 other events, 5360.4 us)
Sparse Core Ops, SparseCore 0:
  10.8 46.9 all-gather.3
  306.8 83.3 all-reduce.158
  393.1 49.4 all-gather.5
  445.2 49.5 all-gather.7
  506.0 86.1 all-reduce.156
  633.9 85.7 all-reduce.154
  888.7 85.8 all-reduce.152
  978.5 61.3 reduce-scatter.60
  1043.2 60.2 reduce-scatter.58
  1107.3 60.9 reduce-scatter.44
  1172.6 60.9 reduce-scatter.42
  1236.9 66.8 reduce-scatter.48
  1307.3 66.7 reduce-scatter.46
  1377.5 66.7 reduce-scatter.40
  1447.7 66.5 reduce-scatter.38
  1518.0 60.2 reduce-scatter.56
  1582.0 60.2 reduce-scatter.54
  1645.6 63.8 reduce-scatter.36
  1713.3 63.7 reduce-scatter.34
  1780.2 61.3 reduce-scatter.52
  1845.3 61.4 reduce-scatter.50
where the time goes:
time: 2000 us; the launch traced here: 1990 us
  waiting for transfers between devices  928 us (46%)
  other arithmetic  464 us (23%)
  matrix products  290 us (14%)
  blocking collectives  225 us (11%)
  local copies, waits for them, and re-layouts  55.7 us (3%)
  between operations  26.9 us (1%)
    unnamed x29, waiting for transfers between devices  322 us
    reduce_scatter x2, waiting for transfers between devices, reduce_grads(): lax.psum_scatter(grads[2].astype(jnp.bfloat16), 'dp', scatter_dimension=0...  138 us
    reduce_scatter x2, waiting for transfers between devices, reduce_grads(): lax.psum_scatter(grads[0].astype(jnp.bfloat16), 'dp', scatter_dimension=0...  133 us
    mul x3, other arithmetic, conv_mix(): total = total + taps[offset] * padded[..., offset:offset + length, :]  93.8 us
    reduce_sum x7, other arithmetic, layer_norm(): centered = v - jnp.mean(v, axis=-1, keepdims=True)  86.3 us
    psum x1, waiting for transfers between devices, shards(): lax.psum(rdot(dhidden, w_up).astype(jnp.bfloat16), 'mp').astype(jnp.float32)  85.9 us
    reduce_sum x8, other arithmetic, conv_mix(): total = total + taps[offset] * padded[..., offset:offset + length, :]  82.5 us
    psum x1, waiting for transfers between devices, shards(): lax.psum(jnp.dot(mixed, w_out, preferred_element_type=jnp.float32).astype...  81.5 us
  transfers between devices with their start and end apart: 21, of which 16 were waited for; matrix products, arithmetic and copies ran while one was open for 25% of the time, Pallas kernels for 0%

commit v1 on v0

v1 whole, which is shorter than its diff:
```python
import jax
import jax.numpy as jnp
from jax import lax
from jax.sharding import PartitionSpec as P

HEADS = 16
HEAD_DIM = 64
PHONES = 128
KERNEL = 31
HALF = 15
PAD = 16
TSTEPS = 1000
STEP = 10

SIGMA = 1e-05
BETA_ONE = 0.9
BETA_TWO = 0.999
EPSILON = 1e-08
DECAY = 0.01
RATE = 0.15
CLIP_AT = 0.1
NORM_EPS = 1e-05
SCALE = HEAD_DIM**-0.5
bf = jnp.bfloat16
f32 = jnp.float32


def gelu(v):
    return jax.nn.gelu(v, approximate=True)


def gelu_back(v, dv):
    return jax.vjp(gelu, v)[1](dv)[0]


def dot(left, right):
    return jnp.dot(left, right, preferred_element_type=f32)


def tdot(left, right):
    return lax.dot_general(
        left, right, (((0,), (0,)), ((), ())), preferred_element_type=f32
    )


def rdot(left, right):
    return lax.dot_general(
        left, right, (((1,), (1,)), ((), ())), preferred_element_type=f32
    )


def norm_parts(v):
    centered = v - jnp.mean(v, axis=-1, keepdims=True)
    spread = jnp.mean(centered * centered, axis=-1, keepdims=True)
    r = lax.rsqrt(spread + NORM_EPS)
    return centered * r, r


def norm_back(da, xhat, r, gain):
    dgain = jnp.sum(da * xhat, axis=0)
    dbias = jnp.sum(da, axis=0)
    dx = da * gain
    dv = r * (
        dx
        - jnp.mean(dx, axis=-1, keepdims=True)
        - xhat * jnp.mean(dx * xhat, axis=-1, keepdims=True)
    )
    return dv, dgain, dbias


def adam_update(weight, first, second, grad, factor):
    clipped = grad * factor
    first_new = BETA_ONE * first + (1.0 - BETA_ONE) * clipped
    second_new = BETA_TWO * second + (1.0 - BETA_TWO) * clipped * clipped
    first_hat = first_new / (1.0 - BETA_ONE**STEP)
    second_hat = second_new / (1.0 - BETA_TWO**STEP)
    weight_new = weight - RATE * (first_hat / (jnp.sqrt(second_hat) + EPSILON) + DECAY * weight)
    return (weight_new, first_new, second_new)


def shards(
    clean_mel,
    noise_mel,
    lengths,
    span_start,
    span_end,
    phone_ids,
    flow_steps,
    in_table,
    channel_rows,
    attn_qkv,
    attn_out,
    ffn_up,
    ffn_down,
    mel_head,
    table_first,
    channel_first,
    qkv_first,
    merge_first,
    upward_first,
    downward_first,
    head_first,
    table_second,
    channel_second,
    qkv_second,
    merge_second,
    upward_second,
    downward_second,
    head_second,
):
    micro, units, length, mel = clean_mel.shape
    nmp = lax.axis_size("mp")
    seqs = nmp // micro
    rows = length // seqs
    mp = lax.axis_index("mp")
    batch = mp // seqs
    seq = mp % seqs
    base = seq * rows
    width = in_table.shape[0]
    nch = channel_rows.shape[0]

    c_qkv = attn_qkv.shape[1]
    c_out = attn_out.shape[0]
    c_up = ffn_up.shape[1]
    cuts = (c_qkv, c_qkv + c_out, c_qkv + c_out + c_up)

    thin = jnp.concatenate([in_table.T, channel_rows.T, mel_head], axis=1).astype(bf)
    thin = lax.all_gather(thin, ("dp", "mp"), axis=0, tiled=True)
    model = thin.shape[0]
    w_qkv = lax.all_gather(attn_qkv.astype(bf), ("mp", "dp"), axis=0, tiled=True)
    w_qkv = w_qkv.reshape(nmp, model, c_qkv)
    rest = jnp.concatenate([attn_out.T, ffn_up, ffn_down.T], axis=1).astype(bf)
    rest = lax.all_gather(rest, ("mp", "dp"), axis=0, tiled=True).reshape(nmp, model, -1)
    w_out = rest[:, :, :c_out]
    w_up = rest[:, :, c_out : c_out + c_up]
    w_down = rest[:, :, c_out + c_up :]
    w_in = thin[:, :width]
    channel = thin[:, width : width + nch].T.astype(f32)
    w_head = thin[:, width + nch :]
    taps = channel[:KERNEL]
    vecs = channel[KERNEL:]

    counts = lax.psum(jnp.sum((span_end - span_start).astype(f32), axis=1), "dp")
    count = lax.dynamic_index_in_dim(counts, batch, 0, keepdims=False)

    def mine(x):
        return lax.dynamic_index_in_dim(x, batch, 0, keepdims=False)[0]

    def widen(x):
        x = jnp.pad(mine(x), [(PAD, PAD)] + [(0, 0)] * (x.ndim - 3))
        return lax.dynamic_slice_in_dim(x, base, rows + 2 * PAD, 0)

    size = mine(lengths)
    first_frame = mine(span_start)
    last_frame = mine(span_end)
    place = base - PAD + jnp.arange(rows + 2 * PAD)
    valid_ext = ((place >= 0) & (place < size)).astype(f32)[:, None]
    masked_ext = ((place >= first_frame) & (place < last_frame)).astype(f32)[:, None]
    inside = slice(PAD, PAD + rows)
    valid = valid_ext[inside]
    masked = masked_ext[inside]
    tau = mine(flow_steps).astype(f32) / TSTEPS
    clean = widen(clean_mel).astype(f32)
    noise = widen(noise_mel).astype(f32)
    noisy = (1.0 - (1.0 - SIGMA) * tau) * noise + tau * clean
    context = clean * (valid_ext * (1.0 - masked_ext))
    target = (clean - (1.0 - SIGMA) * noise)[inside]
    onehot = (widen(phone_ids)[:, None] == jnp.arange(PHONES)).astype(bf)
    features_ext = jnp.concatenate([noisy.astype(bf), context.astype(bf), onehot], axis=-1)
    features = features_ext[inside]

    start_ext = rdot(features_ext, w_in) + vecs[6]
    hm = start_ext * valid_ext
    conv = jnp.zeros((rows, model), f32) + vecs[7]
    for k in range(KERNEL):
        conv = conv + taps[k] * hm[k + 1 : k + 1 + rows]
    first = start_ext[inside] + gelu(conv)
    x_one, r_one = norm_parts(first)
    act_one = (x_one * vecs[0] + vecs[1]).astype(bf)

    packed = jnp.einsum("rd,mdc->rmc", act_one, w_qkv, preferred_element_type=f32).astype(bf)
    packed = packed.reshape(rows, HEADS, 3, HEAD_DIM)
    query, key, value = packed[:, :, 0], packed[:, :, 1], packed[:, :, 2]
    groups = [[g * seqs + s for s in range(seqs)] for g in range(micro)]

    def shift(x, i):
        pairs = [(g[(s + i) % seqs], g[s]) for g in groups for s in range(seqs)]
        return lax.ppermute(x, "mp", pairs)

    def unshift(x, i):
        pairs = [(g[s], g[(s + i) % seqs]) for g in groups for s in range(seqs)]
        return lax.ppermute(x, "mp", pairs)

    both = jnp.stack([key, value])
    both = jnp.concatenate([both] + [shift(both, i) for i in range(1, seqs)], axis=1)
    keys, values = both[0], both[1]
    blocks = (seq + jnp.arange(seqs)) % seqs
    key_place = (blocks[:, None] * rows + jnp.arange(rows)).reshape(-1)
    query_place = base + jnp.arange(rows)
    slopes = jnp.exp2(-8.0 * (jnp.arange(HEADS) + 1).astype(f32) / HEADS)
    distance = jnp.abs(query_place[:, None] - key_place[None, :]).astype(f32)
    raw = jnp.einsum("qhd,khd->hqk", query, keys, preferred_element_type=f32)
    score = raw * SCALE - slopes[:, None, None] * distance
    score = jnp.where((key_place < size)[None, None, :], score, -1000000000.0)
    top = jnp.max(score, axis=-1, keepdims=True)
    prob = jnp.exp(score - top)
    prob = prob / jnp.sum(prob, axis=-1, keepdims=True)
    prob_low = prob.astype(bf)
    mixed = jnp.einsum("hqk,khd->qhd", prob_low, values, preferred_element_type=f32)
    mixed = mixed.astype(bf).reshape(rows, nmp, c_out)
    attn = jnp.zeros((rows, model), f32)
    for m in range(nmp):
        attn = attn + rdot(mixed[:, m], w_out[m])
    second = first + attn

    x_two, r_two = norm_parts(second)
    act_two = (x_two * vecs[2] + vecs[3]).astype(bf)
    ffn = jnp.zeros((rows, model), f32)
    hidden = []
    active = []
    for m in range(nmp):
        hidden.append(dot(act_two, w_up[m]))
        active.append(gelu(hidden[m]).astype(bf))
        ffn = ffn + rdot(active[m], w_down[m])
    third = second + ffn

    x_three, r_three = norm_parts(third)
    act_three = (x_three * vecs[4] + vecs[5]).astype(bf)
    error = dot(act_three, w_head) - target
    weight_rows = masked / count
    loss_local = jnp.sum(weight_rows * error * error)
    dpred = (2.0 * weight_rows * error).astype(bf)
    g_head = tdot(act_three, dpred)
    dthird, dg3, db3 = norm_back(rdot(dpred, w_head), x_three, r_three, vecs[4])

    dffn = dthird.astype(bf)
    da2 = jnp.zeros((rows, model), f32)
    g_up, g_down = [], []
    for m in range(nmp):
        dhid = gelu_back(hidden[m], dot(dffn, w_down[m])).astype(bf)
        g_down.append(tdot(dffn, active[m]).astype(bf))
        g_up.append(tdot(act_two, dhid).astype(bf))
        da2 = da2 + rdot(dhid, w_up[m])
    dnorm, dg2, db2 = norm_back(da2, x_two, r_two, vecs[2])
    dsecond = dthird + dnorm

    dattn = dsecond.astype(bf)
    g_out = [tdot(dattn, mixed[:, m]).astype(bf) for m in range(nmp)]
    dmixed = jnp.stack([dot(dattn, w_out[m]) for m in range(nmp)], axis=1)
    dmixed = dmixed.astype(bf).reshape(rows, HEADS, HEAD_DIM)
    dvalues = jnp.einsum("hqk,qhd->khd", prob_low, dmixed, preferred_element_type=f32)
    dprob = jnp.einsum("qhd,khd->hqk", dmixed, values, preferred_element_type=f32)
    dscore = prob * (dprob - jnp.sum(prob * dprob, axis=-1, keepdims=True))
    draw = (dscore * SCALE).astype(bf)
    dquery = jnp.einsum("hqk,khd->qhd", draw, keys, preferred_element_type=f32)
    dkeys = jnp.einsum("hqk,qhd->khd", draw, query, preferred_element_type=f32)
    dboth = jnp.stack([dkeys, dvalues])
    total = dboth[:, :rows]
    for i in range(1, seqs):
        total = total + unshift(dboth[:, i * rows : (i + 1) * rows].astype(bf), i).astype(f32)
    dpacked = jnp.stack([dquery, total[0], total[1]], axis=2).astype(bf)
    dpacked = dpacked.reshape(rows, nmp, c_qkv)
    g_qkv = [tdot(act_one, dpacked[:, m]).astype(bf) for m in range(nmp)]
    da1 = jnp.zeros((rows, model), f32)
    for m in range(nmp):
        da1 = da1 + rdot(dpacked[:, m], w_qkv[m])

    dnorm, dg1, db1 = norm_back(da1, x_one, r_one, vecs[0])
    dfirst = dsecond + dnorm
    dconv = gelu_back(conv, dfirst)
    right = lax.ppermute(
        dconv[:PAD], "mp", [(g[s + 1], g[s]) for g in groups for s in range(seqs - 1)]
    )
    left = lax.ppermute(
        dconv[rows - PAD :], "mp", [(g[s], g[s + 1]) for g in groups for s in range(seqs - 1)]
    )
    dconv_ext = jnp.concatenate([left, dconv, right], axis=0)
    back = jnp.zeros((rows, model), f32)
    g_taps = []
    for k in range(KERNEL):
        back = back + taps[k] * dconv_ext[2 * PAD - 1 - k : 2 * PAD - 1 - k + rows]
        g_taps.append(jnp.sum(dconv * hm[k + 1 : k + 1 + rows], axis=0))
    dstart = dfirst + valid * back
    g_in = tdot(dstart.astype(bf), features)
    g_rows = g_taps + [dg1, db1, dg2, db2, dg3, db3, jnp.sum(dstart, axis=0), jnp.sum(dconv, axis=0)]
    g_chan = jnp.stack(g_rows, axis=1)

    g_thin = jnp.concatenate([g_in, g_chan, g_head], axis=1).astype(bf)
    g_rest = jnp.stack(
        [jnp.concatenate([g_up[m], g_down[m]], axis=1) for m in range(nmp)]
    ).reshape(nmp * model, -1)
    g_near = jnp.stack(
        [jnp.concatenate([g_qkv[m], g_out[m]], axis=1) for m in range(nmp)]
    ).reshape(nmp * model, -1)
    g_rest = lax.psum_scatter(g_rest, ("mp", "dp"), scatter_dimension=0, tiled=True).astype(f32)
    g_near = lax.psum_scatter(g_near, ("mp", "dp"), scatter_dimension=0, tiled=True).astype(f32)
    g_thin = lax.psum_scatter(g_thin, ("dp", "mp"), scatter_dimension=0, tiled=True).astype(f32)
    squares = jnp.sum(g_rest * g_rest) + jnp.sum(g_near * g_near) + jnp.sum(g_thin * g_thin)
    sums = lax.psum(jnp.stack([loss_local, squares]), ("dp", "mp"))
    loss = sums[0]
    grad_norm = jnp.sqrt(sums[1])
    factor = CLIP_AT / jnp.maximum(grad_norm, CLIP_AT)

    tw, tm, tv = adam_update(in_table, table_first, table_second, g_thin[:, :width].T, factor)
    cw, cm, cv = adam_update(
        channel_rows, channel_first, channel_second, g_thin[:, width : width + nch].T, factor
    )
    hw, hm_, hv = adam_update(mel_head, head_first, head_second, g_thin[:, width + nch :], factor)
    qw, qm, qv = adam_update(attn_qkv, qkv_first, qkv_second, g_near[:, :c_qkv], factor)
    ow, om, ov = adam_update(attn_out, merge_first, merge_second, g_near[:, c_qkv:].T, factor)
    uw, um, uv = adam_update(ffn_up, upward_first, upward_second, g_rest[:, :c_up], factor)
    dw, dm, dv = adam_update(ffn_down, downward_first, downward_second, g_rest[:, c_up:].T, factor)
    return (
        loss, grad_norm,
        tw, tm, tv, cw, cm, cv, qw, qm, qv, ow, om, ov, uw, um, uv, dw, dm, dv, hw, hm_, hv,
    )


def solution(mesh):
    wide = P(None, ("dp", "mp"))
    tall = P(("dp", "mp"), None)
    down = P("dp", "mp")
    flat = P("mp", "dp")
    weights = (wide, wide, down, flat, down, flat, tall)
    pair = P(None, "dp")
    data = (P(None, "dp", None, None), P(None, "dp", None, None), pair, pair, pair)
    data = data + (P(None, "dp", None), pair)
    return jax.shard_map(
        shards,
        mesh=mesh,
        in_specs=data + weights * 3,
        out_specs=(P(), P()) + tuple(w for w in weights for _ in range(3)),
        check_vma=False,
    )
```

time: 2000 us -> 1280 us (0.64)
  other arithmetic: 464 us -> 148 us
  waiting for transfers between devices: 928 us -> 612 us
  blocking collectives: 225 us -> 104 us
  local copies, waits for them, and re-layouts: 55.7 us -> 134 us
  matrix products: 290 us -> 241 us
    reduce_scatter x6 -> x3, waiting for transfers between devices: 272 us -> 603 us  [the longest x1 358 us: shards(): lax.psum_scatter(g_rest, ('mp', 'dp'), scatter_dimension=0, tiled=True)]
    unnamed x29 -> x5, waiting for transfers between devices: 322 us -> 0.08 us
    psum x4 -> x0, waiting for transfers between devices: 253 us -> none  [the longest x1 85.9 us: shards(): lax.psum(rdot(dhidden, w_up).astype(jnp.bfloat16), 'mp').astype(jnp.float32)]
    reduce_sum x36 -> x10, other arithmetic: 222 us -> 29.7 us  [the longest x1 11.9 us: norm_parts(): centered = v - jnp.mean(v, axis=-1, keepdims=True)]
    all_gather x4 -> x1, blocking collectives: 151 us -> 47.6 us  [shards(): thin = lax.all_gather(thin, ('dp', 'mp'), axis=0, tiled=True)]
    mul x7 -> x2, other arithmetic: 95.8 us -> 1.96 us  [the longest x1 1.94 us: shards(): context = clean * (valid_ext * (1.0 - masked_ext))]
    add_any x6 -> x0, other arithmetic: 74.4 us -> none  [the longest x4 74.4 us: conv_mix(): total = total + taps[offset] * padded[..., offset:offset + length, :]]
    all_gather x3 -> x2, waiting for transfers between devices: 82 us -> 9.59 us  [the longest x1 9.57 us: shards(): lax.all_gather(rest, ('mp', 'dp'), axis=0, tiled=True)]
  transfers between devices with their start and end apart: 21 -> 9, of which waited for: 16 -> 4; matrix products, arithmetic and copies ran while one was open for 25% -> 22% of each run, Pallas kernels for 0% -> 0%
where the time goes in v1:
time: 1280 us; the launch traced here: 1270 us
  waiting for transfers between devices  612 us (48%)
  matrix products  241 us (19%)
  other arithmetic  148 us (12%)
  local copies, waits for them, and re-layouts  134 us (10%)
  blocking collectives  104 us (8%)
  between operations  22.2 us (2%)
    reduce_scatter x1, waiting for transfers between devices, shards(): lax.psum_scatter(g_rest, ('mp', 'dp'), scatter_dimension=0, tiled=True)  358 us
    reduce_scatter x1, waiting for transfers between devices, shards(): lax.psum_scatter(g_near, ('mp', 'dp'), scatter_dimension=0, tiled=True)  180 us
    reduce_scatter x1, waiting for transfers between devices, shards(): lax.psum_scatter(g_thin, ('dp', 'mp'), scatter_dimension=0, tiled=True)  64.3 us
    dot_general x1, matrix products, shards(): dkeys = jnp.einsum('hqk,qhd->khd', draw, query, preferred_element_type=f32)  54.8 us
    dot_general x1, matrix products, shards(): dquery = jnp.einsum('hqk,khd->qhd', draw, keys, preferred_element_type=f32)  52.4 us
    all_gather x1, blocking collectives, shards(): thin = lax.all_gather(thin, ('dp', 'mp'), axis=0, tiled=True)  47.6 us
    sub x1, other arithmetic, shards(): prob = jnp.exp(score - top)  40 us
    psum x1, blocking collectives, shards(): sums = lax.psum(jnp.stack([loss_local, squares]), ('dp', 'mp'))  38.6 us
  transfers between devices with their start and end apart: 9, of which 4 were waited for; matrix products, arithmetic and copies ran while one was open for 22% of the time, Pallas kernels for 0%

profile of v1, /device:TPU:0, one launch (start us, length us, event | category | flops | bytes accessed | tf_op | source)
XLA Modules:
  0.0 1267.2 jit_solution(18020802166172764333)
XLA Ops:
  18.4 47.6 %all_gather.9 = bf16[1024,407]{1,0:T(8,128)(2,1)S(1)} all-gather(bf16[32,407]{1,0:T(8,128)(2,1)S(1)} %pad_maximum_fusion.10), channel_id=1, replica_groups=mesh['dp'=8,'mp'=4] {'dp','mp'}, dimensions={0}, use_global_device_ids=true | all-gather | bytes 859584 | tf_op jit(solution)/shard_map/all_gather | solution.py:128
  66.7 5.5 slice_reduce_fusion.1
  72.3 5.1 slice_reduce_fusion.37
  78.8 11.9 fusion.257
  92.3 8.0 convolution_convert_fusion
  100.3 4.8 copy.191
  108.9 17.5 %psum.14 = f32[2]{0:T(128)S(1)} all-reduce(f32[2]{0:T(128)S(1)} %convert_bitcast_fusion.5), channel_id=1, replica_groups=mesh['dp'=8,'mp'=4] {'dp'}, use_global_device_ids=true, to_apply=%region_0.1 | all-reduce | flops 2 | bytes 16 | tf_op jit(solution)/shard_map/psum | solution.py:143
  136.5 13.5 %fusion.156 = f32[16,512,1024]{2,1,0:T(8,128)} fusion(bf16[2,1024,16,64]{1,3,2,0:T(8,128)(2,1)S(1)} %pad_maximum_fusion.3, bf16[512,16,3,64]{0,3,2,1:T(8,128)(2,1)S(1)} %bitcast.324), kind=kOutput, calls=%fused_computation.309 | convolution fusion | flops 1073741824 | bytes 36700160 | tf_op jit(solution)/shard_map/qhd,khd->hqk/dot_general | solution.py:202
  150.0 40.0 %fusion.261 = (f32[16,512]{1,0:T(8,128)S(1)}, f32[16,512,1024]{2,1,0:T(8,128)}) fusion(f32[16,512,1024]{2,1,0:T(8,128)} %fusion.156, f32[512,1024]{1,0:T(8,128)} %abs_convert_fusion, f32[16]{0:T(128)S(1)} %multiply_exponential_fusion, pred[1024]{0:T(1024)(128)(4,1)S(1)} %broadcast_compare_fusion), kind=kOutput, calls=%fused_computation.556 | output fusion | flops 83887104 | bytes 69239872 | tf_op jit(solution)/shard_map/sub | solution.py:206
  190.1 14.5 %fusion.180 = bf16[16,64,512]{2,1,0:T(8,128)(2,1)S(1)} fusion(bf16[2,1024,16,64]{1,3,2,0:T(8,128)(2,1)} %copy-done.7, f32[16,512,1024]{2,1,0:T(8,128)} %get-tuple-element.244, f32[16,512]{1,0:T(8,128)S(1)} %get-tuple-element.243), kind=kOutput, calls=%fused_computation.341 | convolution fusion | flops 1091043328 | bytes 36732928 | tf_op jit(solution)/shard_map/hqk,khd->qhd/dot_general | solution.py:209
  204.6 9.6 all-gather.5.cloned.1.call-done
  214.2 23.6 %copy.196 = bf16[4096,2304]{1,0:T(8,128)(2,1)} copy(bf16[4096,2304]{0,1:T(8,128)(2,1)} %all-gather.5.cloned.1.call-done) | data formatting | bytes 37748736 | tf_op jit(solution)/shard_map/all_gather | solution.py:133
  242.6 2.3 fusion.262
  285.7 14.9 %fusion.25 = f32[1,1024,16,64]{1,3,2,0:T(8,128)} fusion(bf16[512,16,64]{0,2,1:T(8,128)(2,1)} %bitcast.325, f32[16,512,1024]{2,1,0:T(8,128)} %get-tuple-element.244, f32[16,512]{1,0:T(8,128)S(1)} %copy-done.180), kind=kOutput, calls=%fused_computation.74 | convolution fusion | flops 1090519040 | bytes 38830080 | tf_op jit(solution)/shard_map/hqk,qhd->khd/dot_general | solution.py:251
  300.6 14.4 %fusion.155 = f32[16,512,1024]{2,1,0:T(8,128)} fusion(bf16[512,16,64]{0,2,1:T(8,128)(2,1)} %bitcast.326, bf16[2,1024,16,64]{1,3,2,0:T(8,128)(2,1)S(1)} %copy-done.8), kind=kOutput, calls=%fused_computation.308 | convolution fusion | flops 1073741824 | bytes 36700160 | tf_op jit(solution)/shard_map/qhd,khd->hqk/dot_general | solution.py:252
  315.0 54.8 %fusion.28 = f32[1,1024,16,64]{1,3,2,0:T(8,128)} fusion(f32[16,512,1024]{2,1,0:T(8,128)} %fusion.155, bf16[512,16,3,64]{0,3,2,1:T(8,128)(2,1)} %bitcast.323, f32[16,512,1024]{2,1,0:T(8,128)} %get-tuple-element.244, f32[16,512]{1,0:T(8,128)S(1)} %copy-done.180), kind=kOutput, calls=%fused_computation.75 | convolution fusion | flops 1132471296 | bytes 139526144 | tf_op jit(solution)/shard_map/hqk,qhd->khd/dot_general | solution.py:256
  369.8 3.9 fusion.24
  382.3 52.4 %fusion.186 = bf16[512,16,1,64]{0,3,1,2:T(8,128)(2,1)S(1)} fusion(f32[16,512,1024]{2,1,0:T(8,128)} %fusion.155, bf16[2,1024,16,64]{1,3,2,0:T(8,128)(2,1)} %copy-done.7, f32[16,512,1024]{2,1,0:T(8,128)} %get-tuple-element.244, f32[16,512]{1,0:T(8,128)S(1)} %copy-done.180), kind=kOutput, calls=%fused_computation.343 | convolution fusion | flops 1132995584 | bytes 137428992 | tf_op jit(solution)/shard_map/hqk,khd->qhd/dot_general | solution.py:255
  434.8 3.6 fusion.23
  450.9 7.8 multiply_reduce_fusion.4
  458.7 4.0 multiply_reduce_fusion.22
  464.0 3.3 collective-permute-start.3
  491.6 18.7 %fusion.252 = (bf16[1024]{0:T(1024)(128)(2,1)}, bf16[512,1024]{1,0:T(8,128)(2,1)}) fusion(f32[512,1024]{1,0:T(8,128)S(1)} %get-tuple-element.221, f32[512,1024]{1,0:T(8,128)S(1)} %get-tuple-element.220, f32[16,1024]{1,0:T(8,128)} %copy-done.58, f32[1024]{0:T(1024)S(1)} %copy-done.71, f32[1024]{0:T(1024)S(1)} %copy-done.73, f32[1024]{0:T(1024)S(1)} %copy-done.75, ...), kind=kLoop, calls=%fused_computation.549 | loop fusion | flops 49806336 | bytes 5505024 | tf_op jit(solution)/shard_map/reduce_sum | solution.py:285
  522.3 3.8 pad_maximum_fusion.1
  526.1 11.4 copy.203
  556.5 6.8 pad_maximum_fusion
  563.3 21.9 %copy.197 = bf16[4,1024,2048]{2,1,0:T(8,128)(2,1)} copy(bf16[4,1024,2048]{1,2,0:T(8,128)(2,1)} %pad_maximum_fusion) | data formatting | bytes 33554432 | tf_op jit(solution)/shard_map/stack | solution.py:289
  587.7 64.3 %reduce-scatter.10.cloned.1.call-done = bf16[32,407]{1,0:T(8,128)(2,1)} async-done(((bf16[1024,407]{1,0:T(8,128)(2,1)}), bf16[32,407]{1,0:T(8,128)(2,1)}) %reduce-scatter.10.cloned.1.call-update) | async-done | bytes 26064 | tf_op jit(solution)/shard_map/reduce_scatter | solution.py:297
  654.7 180.2 %reduce-scatter.8.cloned.1.call-done = bf16[128,1024]{1,0:T(8,128)(2,1)} async-done(((bf16[4096,1024]{1,0:T(8,128)(2,1)}), bf16[128,1024]{1,0:T(8,128)(2,1)}) %reduce-scatter.8.cloned.1.call-update) | async-done | bytes 262160 | tf_op jit(solution)/shard_map/reduce_scatter | solution.py:296
  836.6 358.3 %reduce-scatter.6.cloned.1.call-done = bf16[128,2048]{1,0:T(8,128)(2,1)} async-done(((bf16[4096,2048]{1,0:T(8,128)(2,1)}), bf16[128,2048]{1,0:T(8,128)(2,1)}) %reduce-scatter.6.cloned.1.call-update) | async-done | bytes 524304 | tf_op jit(solution)/shard_map/reduce_scatter | solution.py:295
  1200.5 38.6 %psum.15 = f32[2]{0:T(128)S(1)} all-reduce(f32[2]{0:T(128)S(1)} %pad_maximum_fusion.11), channel_id=1, replica_groups=mesh['dp'=8,'mp'=4] {'dp','mp'}, use_global_device_ids=true, to_apply=%region_62.63 | all-reduce | flops 2 | bytes 16 | tf_op jit(solution)/shard_map/psum | solution.py:299
  1255.2 2.7 multiply_subtract_fusion.1
  (572 shorter events, 175.2 us)
Async XLA Ops:
  7.3 85.0 %all-gather.3.cloned.1.call-start = ((), (), s32[]{:S(2)}) async-start(), calls=%async_computation.3 | async-start | bytes 6488064 | tf_op jit(solution)/shard_map/all_gather | solution.py:130
  9.2 205.0 %all-gather.5.cloned.1.call-start = ((), (), s32[]{:S(2)}) async-start(), calls=%async_computation.4 | async-start | bytes 19464192 | tf_op jit(solution)/shard_map/all_gather | solution.py:133
  12.3 639.6 %reduce-scatter.10.cloned.1.call-start = ((), (), s32[]{:S(2)}) async-start(), calls=%async_computation.7 | async-start | bytes 1081344 | tf_op jit(solution)/shard_map/reduce_scatter | solution.py:297
  17.3 60.1 %copy-start.44 = (bf16[544,80]{1,0:T(8,128)(2,1)}, bf16[544,80]{1,0:T(8,128)(2,1)S(1)}, u32[]{:S(2)}) copy-start(bf16[544,80]{1,0:T(8,128)(2,1)S(1)} %copy.189) | copy-start | bytes 261124
  17.5 60.0 %copy-start.45 = (bf16[544,80]{1,0:T(8,128)(2,1)}, bf16[544,80]{1,0:T(8,128)(2,1)S(1)}, u32[]{:S(2)}) copy-start(bf16[544,80]{1,0:T(8,128)(2,1)S(1)} %copy.190) | copy-start | bytes 261124
  18.2 59.3 %copy-start.116 = (f32[544]{0:T(1024)}, f32[544]{0:T(1024)S(1)}, u32[]{:S(2)}) copy-start(f32[544]{0:T(1024)S(1)} %fusion.234) | copy-start | bytes 6532
  72.3 18.7 %copy-start.59 = (f32[1024]{0:T(1024)}, f32[1024]{0:T(1024)S(1)}, u32[]{:S(2)}) copy-start(f32[1024]{0:T(1024)S(1)} %get-tuple-element.164) | copy-start | bytes 12292
  90.6 152.0 %copy-start.4 = (f32[512,1024]{1,0:T(8,128)}, f32[512,1024]{1,0:T(8,128)S(1)}, u32[]{:S(2)}) copy-start(f32[512,1024]{1,0:T(8,128)S(1)} %get-tuple-element.229) | copy-start | bytes 6291460
  108.5 23.9 %collective-permute-start = (bf16[2,512,16,64]{1,3,2,0:T(8,128)(2,1)}, bf16[2,512,16,64]{1,3,2,0:T(8,128)(2,1)}, u32[]{:S(2)}, u32[]{:S(2)}) collective-permute-start(bf16[2,512,16,64]{1,3,2,0:T(8,128)(2,1)} %pad_maximum_fusion.7), channel_id=1, source_target_pairs={{1,0},{0,1},{3,2},{2,3},{5,4},{4,5},{7,6},{6,7},{9,8},{8,9},{11,10... | collective-permute-start | bytes 6291464 | tf_op jit(solution)/shard_map/ppermute | solution.py:188
  204.6 38.0 %copy-start.19 = (bf16[16,64,512]{2,1,0:T(8,128)(2,1)}, bf16[16,64,512]{2,1,0:T(8,128)(2,1)S(1)}, u32[]{:S(2)}) copy-start(bf16[16,64,512]{2,1,0:T(8,128)(2,1)S(1)} %fusion.180) | copy-start | bytes 3145732
  248.9 16.1 %copy-start.26 = (f32[512,1024]{1,0:T(8,128)}, f32[512,1024]{1,0:T(8,128)S(1)}, u32[]{:S(2)}) copy-start(f32[512,1024]{1,0:T(8,128)S(1)} %fusion.170) | copy-start | bytes 6291460
  250.1 17.1 %copy-start.165 = (f32[512,1024]{1,0:T(8,128)}, f32[512,1024]{1,0:T(8,128)S(1)}, u32[]{:S(2)}) copy-start(f32[512,1024]{1,0:T(8,128)S(1)} %fusion.166) | copy-start | bytes 6291460
  285.7 14.9 %copy-start.8 = (bf16[2,1024,16,64]{1,3,2,0:T(8,128)(2,1)S(1)}, bf16[2,1024,16,64]{1,3,2,0:T(8,128)(2,1)}, u32[]{:S(2)}) copy-start(bf16[2,1024,16,64]{1,3,2,0:T(8,128)(2,1)} %copy-done.7) | copy-start | bytes 12582916
  373.7 61.1 %collective-permute-start.1 = (bf16[2,512,16,64]{1,3,2,0:T(8,128)(2,1)}, bf16[2,512,16,64]{1,3,2,0:T(8,128)(2,1)}, u32[]{:S(2)}, u32[]{:S(2)}) collective-permute-start(bf16[2,512,16,64]{1,3,2,0:T(8,128)(2,1)} %fusion.24), channel_id=1, source_target_pairs={{0,1},{1,0},{2,3},{3,2},{4,5},{5,4},{6,7},{7,6},{8,9},{9,8},{10,11... | collective-permute-start | bytes 6291464 | tf_op jit(solution)/shard_map/ppermute | solution.py:192
  462.7 28.1 %collective-permute-start.2 = (f32[16,1024]{1,0:T(8,128)S(1)}, f32[16,1024]{1,0:T(8,128)S(1)}, u32[]{:S(2)}, u32[]{:S(2)}) collective-permute-start(f32[16,1024]{1,0:T(8,128)S(1)} %get-tuple-element.233), channel_id=1, source_target_pairs={{1,0},{3,2},{5,4},{7,6},{9,8},{11,10},{13,12},{15,14},{17,16},{19,... | collective-permute-start | bytes 196616 | tf_op jit(solution)/shard_map/ppermute | solution.py:271
  464.0 26.8 %collective-permute-start.3 = (f32[16,1024]{1,0:T(8,128)S(1)}, f32[16,1024]{1,0:T(8,128)S(1)}, u32[]{:S(2)}, u32[]{:S(2)}) collective-permute-start(f32[16,1024]{1,0:T(8,128)S(1)} %get-tuple-element.234), channel_id=1, source_target_pairs={{0,1},{2,3},{4,5},{6,7},{8,9},{10,11},{12,13},{14,15},{16,17},{18,... | collective-permute-start | bytes 196616 | tf_op jit(solution)/shard_map/ppermute | solution.py:274
  469.0 22.5 %copy-start.71 = (f32[1024]{0:T(1024)S(1)}, f32[1024]{0:T(1024)}, u32[]{:S(2)}) copy-start(f32[1024]{0:T(1024)} %copy-done.70) | copy-start | bytes 12292
  469.0 22.5 %copy-start.73 = (f32[1024]{0:T(1024)S(1)}, f32[1024]{0:T(1024)}, u32[]{:S(2)}) copy-start(f32[1024]{0:T(1024)} %copy-done.72) | copy-start | bytes 12292
  469.0 22.5 %copy-start.75 = (f32[1024]{0:T(1024)S(1)}, f32[1024]{0:T(1024)}, u32[]{:S(2)}) copy-start(f32[1024]{0:T(1024)} %copy-done.74) | copy-start | bytes 12292
  469.0 22.5 %copy-start.77 = (f32[1024]{0:T(1024)S(1)}, f32[1024]{0:T(1024)}, u32[]{:S(2)}) copy-start(f32[1024]{0:T(1024)} %copy-done.76) | copy-start | bytes 12292
  469.0 22.5 %copy-start.79 = (f32[1024]{0:T(1024)S(1)}, f32[1024]{0:T(1024)}, u32[]{:S(2)}) copy-start(f32[1024]{0:T(1024)} %copy-done.78) | copy-start | bytes 12292
  469.0 22.5 %copy-start.81 = (f32[1024]{0:T(1024)S(1)}, f32[1024]{0:T(1024)}, u32[]{:S(2)}) copy-start(f32[1024]{0:T(1024)} %copy-done.80) | copy-start | bytes 12292
  469.0 22.5 %copy-start.83 = (f32[1024]{0:T(1024)S(1)}, f32[1024]{0:T(1024)}, u32[]{:S(2)}) copy-start(f32[1024]{0:T(1024)} %copy-done.82) | copy-start | bytes 12292
  469.0 22.5 %copy-start.85 = (f32[1024]{0:T(1024)S(1)}, f32[1024]{0:T(1024)}, u32[]{:S(2)}) copy-start(f32[1024]{0:T(1024)} %copy-done.84) | copy-start | bytes 12292
  469.0 22.5 %copy-start.87 = (f32[1024]{0:T(1024)S(1)}, f32[1024]{0:T(1024)}, u32[]{:S(2)}) copy-start(f32[1024]{0:T(1024)} %copy-done.86) | copy-start | bytes 12292
  469.0 22.5 %copy-start.89 = (f32[1024]{0:T(1024)S(1)}, f32[1024]{0:T(1024)}, u32[]{:S(2)}) copy-start(f32[1024]{0:T(1024)} %copy-done.88) | copy-start | bytes 12292
  469.0 22.5 %copy-start.91 = (f32[1024]{0:T(1024)S(1)}, f32[1024]{0:T(1024)}, u32[]{:S(2)}) copy-start(f32[1024]{0:T(1024)} %copy-done.90) | copy-start | bytes 12292
  469.1 22.5 %copy-start.93 = (f32[1024]{0:T(1024)S(1)}, f32[1024]{0:T(1024)}, u32[]{:S(2)}) copy-start(f32[1024]{0:T(1024)} %copy-done.92) | copy-start | bytes 12292
  469.1 22.5 %copy-start.95 = (f32[1024]{0:T(1024)S(1)}, f32[1024]{0:T(1024)}, u32[]{:S(2)}) copy-start(f32[1024]{0:T(1024)} %copy-done.94) | copy-start | bytes 12292
  491.6 19.7 %copy-start.43 = (bf16[544,128]{1,0:T(8,128)(2,1)S(1)}, bf16[544,128]{1,0:T(8,128)(2,1)}, u32[]{:S(2)}) copy-start(bf16[544,128]{1,0:T(8,128)(2,1)} %copy-done.42) | copy-start | bytes 417796
  516.2 318.7 %reduce-scatter.8.cloned.1.call-start = ((), (), s32[]{:S(2)}) async-start(), calls=%async_computation.6 | async-start | bytes 8650752 | tf_op jit(solution)/shard_map/reduce_scatter | solution.py:296
  537.6 657.3 %reduce-scatter.6.cloned.1.call-start = ((), (), s32[]{:S(2)}) async-start(), calls=%async_computation.5 | async-start | bytes 17301504 | tf_op jit(solution)/shard_map/reduce_scatter | solution.py:295
  (160 other events, 643.9 us)
Sparse Core Ops, SparseCore 0:
  11.7 73.3 all-gather.2
  86.5 127.6 all-gather.4
  516.3 135.5 reduce-scatter.9
  654.2 180.7 reduce-scatter.7
  837.2 357.6 reduce-scatter.5

commit v2 on v1

--- a/solution.py
+++ b/solution.py
@@ -1,6 +1,10 @@
+import functools
+
 import jax
 import jax.numpy as jnp
 from jax import lax
+from jax.experimental import pallas as pl
+from jax.experimental.pallas import tpu as pltpu
 from jax.sharding import PartitionSpec as P
 
 HEADS = 16
@@ -76,6 +80,396 @@
     second_hat = second_new / (1.0 - BETA_TWO**STEP)
     weight_new = weight - RATE * (first_hat / (jnp.sqrt(second_hat) + EPSILON) + DECAY * weight)
     return (weight_new, first_new, second_new)
+
+
+MESH = pl.DeviceIdType.MESH
+AXES = ("z", "x", "y", "c")
+
+
+class Wires:
+    def __init__(self, ndp, nmp):
+        self.sizes = {"z": ndp // 2, "x": 2, "y": nmp // 2, "c": 2}
+        dp = lax.axis_index("dp")
+        mp = lax.axis_index("mp")
+        self.at = {"z": dp // 2, "x": dp % 2, "y": mp // 2, "c": mp % 2}
+
+    def peer(self, axis, k):
+        at = dict(self.at)
+        at[axis] = lax.rem(at[axis] + k, self.sizes[axis])
+        return (at["z"] * 2 + at["x"], at["y"] * 2 + at["c"])
+
+    def owner_mp(self, ky, kc):
+        ny = self.sizes["y"]
+        return lax.rem(self.at["y"] + ny - ky, ny) * 2 + lax.rem(self.at["c"] + 2 - kc, 2)
+
+    def ring(self):
+        return [self.peer(a, k) for a in AXES for k in range(1, self.sizes[a])]
+
+    def near(self, k):
+        nmp = self.sizes["y"] * self.sizes["c"]
+        return (lax.axis_index("dp"), lax.rem(lax.axis_index("mp") + k, nmp))
+
+    def far(self, k):
+        ndp = self.sizes["z"] * self.sizes["x"]
+        return (lax.rem(lax.axis_index("dp") + k, ndp), lax.axis_index("mp"))
+
+    def greet(self, peers):
+        barrier = pltpu.get_barrier_semaphore()
+        for p in peers:
+            pl.semaphore_signal(barrier, inc=1, device_id=p, device_id_type=MESH)
+        pl.semaphore_wait(barrier, len(peers))
+
+
+def slot_number(sizes, k):
+    return ((k["z"] * sizes["x"] + k["x"]) * sizes["y"] + k["y"]) * sizes["c"] + k["c"]
+
+
+def spread(sizes, order):
+    slots = [(dict.fromkeys(AXES, 0), -1)]
+    for stage, axis in enumerate(order):
+        slots += [
+            ({**k, axis: n}, stage) for n in range(1, sizes[axis]) for k, _ in list(slots)
+        ]
+    return slots
+
+
+class Gather:
+    def __init__(self, wires, order, own, slot, send, recv):
+        self.wires, self.order, self.own, self.slot = wires, order, own, slot
+        self.send, self.recv = send, recv
+        self.slots = spread(wires.sizes, order)
+        self.started = []
+
+    def forward(self, source, k, stage):
+        for later in range(stage + 1, len(self.order)):
+            axis = self.order[later]
+            for n in range(1, self.wires.sizes[axis]):
+                there = {**k, axis: n}
+                number = slot_number(self.wires.sizes, there)
+                copy = pltpu.make_async_remote_copy(
+                    source, self.slot(there, k), self.send.at[number], self.recv.at[number],
+                    device_id=self.wires.peer(axis, n), device_id_type=MESH,
+                )
+                copy.start()
+                self.started.append((copy, number))
+
+    def begin(self):
+        k, stage = self.slots[0]
+        self.forward(self.own, k, stage)
+
+    def arrive(self, index):
+        k, stage = self.slots[index]
+        number = slot_number(self.wires.sizes, k)
+        here = self.slot(k, k)
+        pltpu.make_async_remote_copy(
+            here, here, self.send.at[number], self.recv.at[number],
+            device_id=self.wires.peer("c", 1), device_id_type=MESH,
+        ).wait_recv()
+        self.forward(here, k, stage)
+
+    def finish(self):
+        for copy, _ in self.started:
+            copy.wait_send()
+
+
+class Reduce:
+    def __init__(self, wires, order, source, landing, add, send, recv):
+        self.wires, self.order = wires, order
+        self.source, self.landing, self.add = source, landing, add
+        self.send, self.recv = send, recv
+        self.started = []
+        slots = [k for k, _ in spread(wires.sizes, order[::-1])]
+        self.stages = []
+        for stage, axis in enumerate(order):
+            self.stages.append([k for k in slots if k[axis]])
+            slots = [k for k in slots if not k[axis]]
+
+    def copy(self, stage, k):
+        axis = self.order[stage]
+        number = slot_number(self.wires.sizes, k)
+        n = self.wires.sizes[axis]
+        return pltpu.make_async_remote_copy(
+            self.source(k, stage), self.landing(k, stage),
+            self.send.at[number], self.recv.at[number],
+            device_id=self.wires.peer(axis, (n - k[axis]) % n), device_id_type=MESH,
+        )
+
+    def leave(self, stage, k):
+        copy = self.copy(stage, k)
+        copy.start()
+        self.started.append(copy)
+
+    def begin(self):
+        for k in self.stages[0]:
+            self.leave(0, k)
+
+    def arrive(self, stage, k):
+        self.copy(stage, k).wait_recv()
+        kept = {**k, self.order[stage]: 0}
+        self.add(k, kept)
+        last = k[self.order[stage]] == self.wires.sizes[self.order[stage]] - 1
+        if last and stage + 1 < len(self.order) and kept[self.order[stage + 1]]:
+            self.leave(stage + 1, kept)
+
+    def finish(self):
+        for copy in self.started:
+            copy.wait_send()
+
+
+FIRST = ("z", "x", "y", "c")
+OTHER = ("z", "y", "x", "c")
+
+
+def gather_kernel(ndp, nmp, *refs):
+    owns, outs = refs[:3], refs[3:6]
+    send, recv, local = refs[6:]
+    wires = Wires(ndp, nmp)
+    wires.greet(wires.ring())
+    sizes = wires.sizes
+    thin_rows = owns[0].shape[0]
+
+    def thin_slot(k, sent):
+        block = (k["z"] * sizes["x"] + k["x"]) * nmp + wires.owner_mp(sent["y"], sent["c"])
+        return outs[0].at[pl.ds(pl.multiple_of(block * thin_rows, thin_rows), thin_rows)]
+
+    def wide_slot(ref, rows, half):
+        def slot(k, sent):
+            start = (k["z"] * sizes["x"] + k["x"]) * 2 * rows + half * rows
+            return ref.at[k["y"] * sizes["c"] + k["c"], pl.ds(start, rows)]
+
+        return slot
+
+    flows = [Gather(wires, FIRST, owns[0], thin_slot, send.at[0], recv.at[0])]
+    for ref, out in zip(owns[1:], outs[1:]):
+        rows = ref.shape[0] // 2
+        for half, order in enumerate((FIRST, OTHER)):
+            number = len(flows)
+            own = ref.at[pl.ds(half * rows, rows)]
+            slot = wide_slot(out, rows, half)
+            flows.append(Gather(wires, order, own, slot, send.at[number], recv.at[number]))
+    zero = dict.fromkeys(AXES, 0)
+    kept = [pltpu.make_async_copy(f.own, f.slot(zero, zero), local.at[i]) for i, f in enumerate(flows)]
+    for copy in kept:
+        copy.start()
+    for f in flows:
+        f.begin()
+    count = len(flows[0].slots)
+    for group in (flows[:1], flows[1:3], flows[3:]):
+        for index in range(1, count):
+            for f in group:
+                f.arrive(index)
+    for copy in kept:
+        copy.wait()
+    for f in flows:
+        f.finish()
+
+
+def gather_all(thin, near, rest, ndp, nmp):
+    model = near.shape[0] * ndp
+    outs = (
+        jax.ShapeDtypeStruct((model, thin.shape[1]), bf),
+        jax.ShapeDtypeStruct((nmp, model, near.shape[1]), bf),
+        jax.ShapeDtypeStruct((nmp, model, rest.shape[1]), bf),
+    )
+    return pl.pallas_call(
+        functools.partial(gather_kernel, ndp, nmp),
+        name="gather",
+        out_shape=outs,
+        in_specs=[pl.BlockSpec(memory_space=pl.ANY)] * 3,
+        out_specs=[pl.BlockSpec(memory_space=pl.ANY)] * 3,
+        scratch_shapes=[
+            pltpu.SemaphoreType.DMA((5, ndp * nmp)),
+            pltpu.SemaphoreType.DMA((5, ndp * nmp)),
+            pltpu.SemaphoreType.DMA((5,)),
+        ],
+        compiler_params=pltpu.CompilerParams(collective_id=0, has_side_effects=True),
+    )(thin, near, rest)
+
+
+def total(ref):
+    rows = 8
+
+    def body(i, part):
+        x = ref[pl.ds(i * rows, rows)]
+        return part + x * x
+
+    part = lax.fori_loop(0, ref.shape[0] // rows, body, jnp.zeros((rows, ref.shape[1]), f32))
+    return jnp.sum(part)
+
+
+def reduce_kernel(ndp, nmp, wide, *refs):
+    count = wide + 1
+    terms, loss = refs[:count], refs[count]
+    outs, sums = refs[count + 1 : 2 * count + 1], refs[2 * count + 1]
+    rest = refs[2 * count + 2 :]
+    held, land = rest[:count], rest[count : 2 * count + wide]
+    parts, send, recv, local, near_send, near_recv, far_send, far_recv = rest[2 * count + wide :]
+    wires = Wires(ndp, nmp)
+    sizes = wires.sizes
+    nears = [wires.near(k) for k in range(1, nmp)]
+    fars = [wires.far(k) for k in range(1, ndp)]
+    wires.greet(nears + fars)
+    flows = []
+    loads = []
+
+    def tile_add(out, target, source, rows):
+        step = 16
+
+        def body(i, _):
+            here = pl.ds(pl.multiple_of(i * step, step), step)
+            target_rows = target[here].astype(f32) + source[here].astype(f32)
+            out[here] = target_rows.astype(out.dtype)
+            return 0
+
+        lax.fori_loop(0, rows // step, body, 0)
+
+    def wide_flow(i, half, order):
+        term, keep, out = terms[i], held[i], outs[i]
+        rows = term.shape[1] // ndp // 2
+        box = land[1 + 2 * (i - 1) + half]
+
+        def place(k):
+            return pl.ds((k["z"] * sizes["x"] + k["x"]) * 2 * rows + half * rows, rows)
+
+        def source(k, stage):
+            if stage == 0:
+                return term.at[k["y"] * sizes["c"] + k["c"], place(k)]
+            return keep.at[k["y"], place(k)]
+
+        def landing(k, stage):
+            return box.at[slot_number(sizes, k) - 1]
+
+        def add(k, kept):
+            target = keep.at[kept["y"], place(kept)]
+            if any(kept.values()):
+                tile_add(target, target, landing(k, 0), rows)
+            else:
+                target = out.at[pl.ds(half * rows, rows)]
+                tile_add(target, target, landing(k, 0), rows)
+
+        n = len(flows)
+        flows.append(Reduce(wires, order, source, landing, add, send.at[n], recv.at[n]))
+
+    def thin_flow(order):
+        term, keep, out, box = terms[0], held[0], outs[0], land[0]
+        rows = out.shape[0]
+
+        def source(k, stage):
+            block = (k["z"] * sizes["x"] + k["x"]) * nmp + wires.owner_mp(k["y"], k["c"])
+            ref = term if stage == 0 else keep
+            return ref.at[pl.ds(pl.multiple_of(block * rows, rows), rows)]
+
+        def landing(k, stage):
+            return box.at[slot_number(sizes, k) - 1]
+
+        def add(k, kept):
+            target = source(kept, 1)
+            if any(kept.values()):
+                tile_add(target, target, landing(k, 0), rows)
+            else:
+                tile_add(out, out, landing(k, 0), rows)
+
+        n = len(flows)
+        flows.append(Reduce(wires, order, source, landing, add, send.at[n], recv.at[n]))
+
+    thin_flow(FIRST[::-1])
+    for i in range(1, count):
+        for half, order in enumerate((FIRST[::-1], OTHER[::-1])):
+            wide_flow(i, half, order)
+    for i in range(count):
+        if i == 0:
+            loads.append(pltpu.make_async_copy(terms[0], held[0], local.at[0]))
+        else:
+            for ky in range(sizes["y"]):
+                loads.append(
+                    pltpu.make_async_copy(
+                        terms[i].at[ky * sizes["c"]], held[i].at[ky], local.at[len(loads)]
+                    )
+                )
+    for copy in loads:
+        copy.start()
+    for f in flows[1:] + flows[:1]:
+        f.begin()
+    for copy in loads:
+        copy.wait()
+    zero = dict.fromkeys(AXES, 0)
+    for i in range(count):
+        if i == 0:
+            rows = outs[0].shape[0]
+            block = wires.owner_mp(0, 0)
+            outs[0][...] = held[0][pl.ds(pl.multiple_of(block * rows, rows), rows)].astype(f32)
+        else:
+            outs[i][...] = held[i][0, : outs[i].shape[0]].astype(f32)
+    for stage in range(len(FIRST)):
+        for pos in range(len(flows[0].stages[stage])):
+            for f in flows[1:] + flows[:1]:
+                f.arrive(stage, f.stages[stage][pos])
+    for f in flows:
+        f.finish()
+
+    squares = total(outs[0])
+    for out in outs[1:]:
+        squares = squares + total(out)
+    lanes = lax.broadcasted_iota(jnp.int32, (8, 128), 1)
+    block = jnp.where(lanes == 1, squares, loss[...])
+    for peers, sends, recvs, lower in (
+        (nears, near_send, near_recv, 0),
+        (fars, far_send, far_recv, nmp),
+    ):
+        parts[lower] = block
+        copies = []
+        for i, p in enumerate(peers):
+            copy = pltpu.make_async_remote_copy(
+                parts.at[lower], parts.at[lower + 1 + i], sends.at[i], recvs.at[i],
+                device_id=p, device_id_type=MESH,
+            )
+            copy.start()
+            copies.append(copy)
+        for copy in copies:
+            copy.wait()
+        for i in range(len(peers)):
+            block = block + parts[lower + 1 + i]
+    sums[...] = block
+
+
+def reduce_all(terms, loss, ndp, nmp):
+    wide = len(terms) - 1
+    thin = terms[0]
+    slots = ndp * nmp - 1
+    outs = [jax.ShapeDtypeStruct((thin.shape[0] // (ndp * nmp), thin.shape[1]), f32)]
+    held = [pltpu.VMEM(thin.shape, bf)]
+    land = [pltpu.VMEM((slots, thin.shape[0] // (ndp * nmp), thin.shape[1]), bf)]
+    for t in terms[1:]:
+        rows = t.shape[1] // ndp
+        outs.append(jax.ShapeDtypeStruct((rows, t.shape[2]), f32))
+        held.append(pltpu.VMEM((nmp // 2, t.shape[1], t.shape[2]), bf))
+        land += [pltpu.VMEM((slots, rows // 2, t.shape[2]), bf)] * 2
+    outs.append(jax.ShapeDtypeStruct((8, 128), f32))
+    flows = 1 + 2 * wide
+    dma = pltpu.SemaphoreType.DMA
+    vmem = pl.BlockSpec(memory_space=pltpu.VMEM)
+    return pl.pallas_call(
+        functools.partial(reduce_kernel, ndp, nmp, wide),
+        name="reduce",
+        out_shape=outs,
+        in_specs=[pl.BlockSpec(memory_space=pl.ANY)] * (wide + 1) + [vmem],
+        out_specs=[vmem] * len(outs),
+        scratch_shapes=held
+        + land
+        + [
+            pltpu.VMEM((nmp + ndp, 8, 128), f32),
+            dma((flows, ndp * nmp)),
+            dma((flows, ndp * nmp)),
+            dma((1 + wide * (nmp // 2),)),
+            dma((nmp - 1,)),
+            dma((nmp - 1,)),
+            dma((ndp - 1,)),
+            dma((ndp - 1,)),
+        ],
+        compiler_params=pltpu.CompilerParams(
+            collective_id=1, has_side_effects=True, vmem_limit_bytes=60 << 20
+        ),
+    )(*terms, loss)
 
 
 def shards(
@@ -122,21 +516,31 @@
     c_qkv = attn_qkv.shape[1]
     c_out = attn_out.shape[0]
     c_up = ffn_up.shape[1]
-    cuts = (c_qkv, c_qkv + c_out, c_qkv + c_out + c_up)
-
+
+    ndp = lax.axis_size("dp")
     thin = jnp.concatenate([in_table.T, channel_rows.T, mel_head], axis=1).astype(bf)
-    thin = lax.all_gather(thin, ("dp", "mp"), axis=0, tiled=True)
+    extra = -thin.shape[1] % 128
+    thin = jnp.pad(thin, ((0, 0), (0, extra)))
+    rest = jnp.concatenate([attn_out.T, ffn_up, ffn_down.T], axis=1).astype(bf)
+    own = ndp * nmp <= 32 and seqs == 2
+    if own:
+        thin, w_qkv, rest = gather_all(thin, attn_qkv.astype(bf), rest, ndp, nmp)
+        wires = Wires(ndp, nmp)
+        owners = jnp.stack([wires.owner_mp(m // 2, m % 2) for m in range(nmp)])
+    else:
+        thin = lax.all_gather(thin, ("dp", "mp"), axis=0, tiled=True)
+        w_qkv = lax.all_gather(attn_qkv.astype(bf), ("mp", "dp"), axis=0, tiled=True)
+        w_qkv = w_qkv.reshape(nmp, -1, c_qkv)
+        rest = lax.all_gather(rest, ("mp", "dp"), axis=0, tiled=True)
+        rest = rest.reshape(nmp, -1, rest.shape[1])
+        owners = jnp.arange(nmp)
     model = thin.shape[0]
-    w_qkv = lax.all_gather(attn_qkv.astype(bf), ("mp", "dp"), axis=0, tiled=True)
-    w_qkv = w_qkv.reshape(nmp, model, c_qkv)
-    rest = jnp.concatenate([attn_out.T, ffn_up, ffn_down.T], axis=1).astype(bf)
-    rest = lax.all_gather(rest, ("mp", "dp"), axis=0, tiled=True).reshape(nmp, model, -1)
     w_out = rest[:, :, :c_out]
     w_up = rest[:, :, c_out : c_out + c_up]
     w_down = rest[:, :, c_out + c_up :]
     w_in = thin[:, :width]
     channel = thin[:, width : width + nch].T.astype(f32)
-    w_head = thin[:, width + nch :]
+    w_head = thin[:, width + nch : width + nch + mel]
     taps = channel[:KERNEL]
     vecs = channel[KERNEL:]
 
@@ -191,13 +595,20 @@
         pairs = [(g[s], g[(s + i) % seqs]) for g in groups for s in range(seqs)]
         return lax.ppermute(x, "mp", pairs)
 
+    def swap(x):
+        if not own:
+            return x
+        x = x.reshape(2, rows, nmp // 2, 2, -1)[:, :, :, ::-1]
+        return x.reshape(2, rows, HEADS, HEAD_DIM)
+
     both = jnp.stack([key, value])
-    both = jnp.concatenate([both] + [shift(both, i) for i in range(1, seqs)], axis=1)
+    both = jnp.concatenate([both] + [swap(shift(both, i)) for i in range(1, seqs)], axis=1)
     keys, values = both[0], both[1]
     blocks = (seq + jnp.arange(seqs)) % seqs
     key_place = (blocks[:, None] * rows + jnp.arange(rows)).reshape(-1)
     query_place = base + jnp.arange(rows)
-    slopes = jnp.exp2(-8.0 * (jnp.arange(HEADS) + 1).astype(f32) / HEADS)
+    heads = (owners[:, None] * (HEADS // nmp) + jnp.arange(HEADS // nmp)).reshape(-1)
+    slopes = jnp.exp2(-8.0 * (heads + 1).astype(f32) / HEADS)
     distance = jnp.abs(query_place[:, None] - key_place[None, :]).astype(f32)
     raw = jnp.einsum("qhd,khd->hqk", query, keys, preferred_element_type=f32)
     score = raw * SCALE - slopes[:, None, None] * distance
@@ -255,10 +666,11 @@
     dquery = jnp.einsum("hqk,khd->qhd", draw, keys, preferred_element_type=f32)
     dkeys = jnp.einsum("hqk,qhd->khd", draw, query, preferred_element_type=f32)
     dboth = jnp.stack([dkeys, dvalues])
-    total = dboth[:, :rows]
+    parts = [dboth[:, i * rows : (i + 1) * rows] for i in range(seqs)]
+    dboth = parts[0]
     for i in range(1, seqs):
-        total = total + unshift(dboth[:, i * rows : (i + 1) * rows].astype(bf), i).astype(f32)
-    dpacked = jnp.stack([dquery, total[0], total[1]], axis=2).astype(bf)
+        dboth = dboth + swap(unshift(parts[i].astype(bf), i).astype(f32))
+    dpacked = jnp.stack([dquery, dboth[0], dboth[1]], axis=2).astype(bf)
     dpacked = dpacked.reshape(rows, nmp, c_qkv)
     g_qkv = [tdot(act_one, dpacked[:, m]).astype(bf) for m in range(nmp)]
     da1 = jnp.zeros((rows, model), f32)
@@ -286,17 +698,24 @@
     g_chan = jnp.stack(g_rows, axis=1)
 
     g_thin = jnp.concatenate([g_in, g_chan, g_head], axis=1).astype(bf)
-    g_rest = jnp.stack(
-        [jnp.concatenate([g_up[m], g_down[m]], axis=1) for m in range(nmp)]
-    ).reshape(nmp * model, -1)
-    g_near = jnp.stack(
-        [jnp.concatenate([g_qkv[m], g_out[m]], axis=1) for m in range(nmp)]
-    ).reshape(nmp * model, -1)
-    g_rest = lax.psum_scatter(g_rest, ("mp", "dp"), scatter_dimension=0, tiled=True).astype(f32)
-    g_near = lax.psum_scatter(g_near, ("mp", "dp"), scatter_dimension=0, tiled=True).astype(f32)
-    g_thin = lax.psum_scatter(g_thin, ("dp", "mp"), scatter_dimension=0, tiled=True).astype(f32)
-    squares = jnp.sum(g_rest * g_rest) + jnp.sum(g_near * g_near) + jnp.sum(g_thin * g_thin)
-    sums = lax.psum(jnp.stack([loss_local, squares]), ("dp", "mp"))
+    g_thin = jnp.pad(g_thin, ((0, 0), (0, extra)))
+    lanes = lax.broadcasted_iota(jnp.int32, (8, 128), 1)
+    loss_block = jnp.where(lanes == 0, loss_local, 0.0)
+    terms = [g_thin, jnp.stack(g_up), jnp.stack(g_down), jnp.stack(g_qkv), jnp.stack(g_out)]
+    if own:
+        g_thin, g_up, g_down, g_qkv, g_out, sums = reduce_all(terms, loss_block, ndp, nmp)
+    else:
+        g_thin = lax.psum_scatter(g_thin, ("dp", "mp"), scatter_dimension=0, tiled=True)
+        sums = [g_thin.astype(f32)] + [
+            lax.psum_scatter(
+                t.reshape(-1, t.shape[2]), ("mp", "dp"), scatter_dimension=0, tiled=True
+            ).astype(f32)
+            for t in terms[1:]
+        ]
+        g_thin, g_up, g_down, g_qkv, g_out = sums
+        squares = sum(jnp.sum(g * g) for g in sums)
+        sums = lax.psum(jnp.stack([loss_local, squares])[None], ("dp", "mp"))
+    sums = sums[0]
     loss = sums[0]
     grad_norm = jnp.sqrt(sums[1])
     factor = CLIP_AT / jnp.maximum(grad_norm, CLIP_AT)
@@ -305,11 +724,11 @@
     cw, cm, cv = adam_update(
         channel_rows, channel_first, channel_second, g_thin[:, width : width + nch].T, factor
     )
-    hw, hm_, hv = adam_update(mel_head, head_first, head_second, g_thin[:, width + nch :], factor)
-    qw, qm, qv = adam_update(attn_qkv, qkv_first, qkv_second, g_near[:, :c_qkv], factor)
-    ow, om, ov = adam_update(attn_out, merge_first, merge_second, g_near[:, c_qkv:].T, factor)
-    uw, um, uv = adam_update(ffn_up, upward_first, upward_second, g_rest[:, :c_up], factor)
-    dw, dm, dv = adam_update(ffn_down, downward_first, downward_second, g_rest[:, c_up:].T, factor)
+    hw, hm_, hv = adam_update(mel_head, head_first, head_second, g_thin[:, width + nch : width + nch + mel], factor)
+    qw, qm, qv = adam_update(attn_qkv, qkv_first, qkv_second, g_qkv, factor)
+    ow, om, ov = adam_update(attn_out, merge_first, merge_second, g_out.T, factor)
+    uw, um, uv = adam_update(ffn_up, upward_first, upward_second, g_up, factor)
+    dw, dm, dv = adam_update(ffn_down, downward_first, downward_second, g_down.T, factor)
     return (
         loss, grad_norm,
         tw, tm, tv, cw, cm, cv, qw, qm, qv, ow, om, ov, uw, um, uv, dw, dm, dv, hw, hm_, hv,

time: 1280 us -> 858 us (0.67)
  waiting for transfers between devices: 612 us -> 0.01 us
  Pallas kernels: 0 us -> 320 us
  blocking collectives: 104 us -> 25.4 us
  local copies, waits for them, and re-layouts: 134 us -> 98.9 us
  between operations: 22.2 us -> 6.62 us
  matrix products: 241 us -> 254 us
    reduce_scatter x3 -> x0, waiting for transfers between devices: 603 us -> none  [the longest x1 358 us: shards(): lax.psum_scatter(g_rest, ('mp', 'dp'), scatter_dimension=0, tiled=True)]
    pallas_call x0 -> x2, Pallas kernels: none -> 320 us  [the longest x1 193 us: reduce_all(): pl.pallas_call(functools.partial(reduce_kernel, ndp, nmp, wide), name='re...]
    all_gather x1 -> x0, blocking collectives: 47.6 us -> none  [shards(): thin = lax.all_gather(thin, ('dp', 'mp'), axis=0, tiled=True)]
    psum x1 -> x0, blocking collectives: 38.6 us -> none  [shards(): sums = lax.psum(jnp.stack([loss_local, squares]), ('dp', 'mp'))]
    another operation x4, local copies, waits for them, and re-layouts: 33.8 us -> 1.77 us  [the longest x1 21.9 us: shards(): jnp.stack([jnp.concatenate([g_up[m], g_down[m]], axis=1) for m in range(n...]
    all_gather x1 -> x0, local copies, waits for them, and re-layouts: 23.6 us -> none  [shards(): lax.all_gather(rest, ('mp', 'dp'), axis=0, tiled=True)]
    unnamed x381 -> x337, local copies, waits for them, and re-layouts: 31.8 us -> 23.6 us
    another operation x15 -> x9, other arithmetic: 26.1 us -> 24.4 us  [the longest x1 7.61 us: shards(): jnp.stack(g_down)]
  transfers between devices with their start and end apart: 9 -> 4, of which waited for: 4 -> 0; matrix products, arithmetic and copies ran while one was open for 22% -> 8% of each run, Pallas kernels for 0% -> 0%
where the time goes in v2:
time: 858 us; the launch traced here: 847 us
  Pallas kernels  320 us (37%)
  matrix products  254 us (30%)
  other arithmetic  137 us (16%)
  local copies, waits for them, and re-layouts  98.9 us (12%)
  blocking collectives  25.4 us (3%)
    pallas_call x1, Pallas kernels, reduce_all(): pl.pallas_call(functools.partial(reduce_kernel, ndp, nmp, wide), name='re...  193 us
    pallas_call x1, Pallas kernels, gather_all(): pl.pallas_call(functools.partial(gather_kernel, ndp, nmp), name='gather',...  127 us
    dot_general x1, matrix products, shards(): dkeys = jnp.einsum('hqk,qhd->khd', draw, query, preferred_element_type=f32)  54.8 us
    dot_general x1, matrix products, shards(): dquery = jnp.einsum('hqk,khd->qhd', draw, keys, preferred_element_type=f32)  53.1 us
    sub x1, other arithmetic, shards(): prob = jnp.exp(score - top)  39.8 us
    dot_general x18, matrix products, tdot(): lax.dot_general(left, right, (((0,), (0,)), ((), ())), preferred_element_...  36.4 us
    another operation x39, local copies, waits for them, and re-layouts, shards(): g_chan = jnp.stack(g_rows, axis=1)  33.2 us
    dot_general x18, matrix products, rdot(): lax.dot_general(left, right, (((1,), (1,)), ((), ())), preferred_element_...  27.1 us
  transfers between devices with their start and end apart: 4, of which 0 were waited for; matrix products, arithmetic and copies ran while one was open for 8% of the time, Pallas kernels for 0%

profile of v2, /device:TPU:0, one launch (start us, length us, event | category | flops | bytes accessed | tf_op | source)
XLA Modules:
  0.0 847.3 jit_solution(15518409614236892907)
XLA Ops:
  5.7 126.6 %gather.1 = (bf16[1024,512]{1,0:T(8,128)(2,1)}, bf16[4,1024,768]{2,1,0:T(8,128)(2,1)}, bf16[4,1024,2304]{2,1,0:T(8,128)(2,1)}) custom-call(bf16[32,512]{1,0:T(8,128)(2,1)} %fusion.300.refs_0_, bf16[128,768]{1,0:T(8,128)(2,1)} %convert_element_type.198.refs_1_, bf16[128,2304]{1,0:T(8,128)(2,1)} %pad_maximum_fusion.11.refs_2_), custom_call_target="tpu_custom_call" | custom-call | tf_op jit(solution)/shard_map/gather/pallas_call | solution.py:274
  133.8 5.6 slice_reduce_fusion.1
  139.5 5.3 slice_reduce_fusion.37
  152.2 11.5 %fusion.338 = (f32[512]{0:T(512)S(1)}, f32[512,1024]{1,0:T(8,128)S(1)}, f32[512,1024]{1,0:T(8,128)}) fusion(f32[544,1024]{1,0:T(8,128)S(1)} %get-tuple-element.237, f32[544,1024]{1,0:T(8,128)S(1)} %get-tuple-element.236, f32[1024]{0:T(1024)S(1)} %get-tuple-element.160, f32[1024]{0:T(1024)S(1)} %get-tuple-element.161, f32[1024]{0:T(1024)S(1)} %get-tuple-element.162, ...), kind=kLoop, calls=%fused_computation.593 | loop fusion | flops 37748224 | bytes 71436288 | tf_op jit(solution)/shard_map/reduce_sum | solution.py:57
  164.9 4.9 convolution_convert_fusion
  169.7 4.7 copy.143
  178.2 25.4 %psum.7 = f32[2]{0:T(128)S(1)} all-reduce(f32[2]{0:T(128)S(1)} %convert_bitcast_fusion.13), channel_id=1, replica_groups=mesh['dp'=8,'mp'=4] {'dp'}, use_global_device_ids=true, to_apply=%region_8.9 | all-reduce | flops 2 | bytes 16 | tf_op jit(solution)/shard_map/psum | solution.py:547
  217.9 3.0 rev.6
  225.2 13.2 %fusion.188 = f32[16,512,1024]{2,1,0:T(8,128)} fusion(bf16[2,1024,16,64]{1,3,2,0:T(8,128)(2,1)S(1)} %pad_maximum_fusion.4, bf16[512,16,3,64]{0,3,2,1:T(8,128)(2,1)S(1)} %bitcast.339), kind=kOutput, calls=%fused_computation.327 | convolution fusion | flops 1073741824 | bytes 36700160 | tf_op jit(solution)/shard_map/qhd,khd->hqk/dot_general | solution.py:613
  238.4 39.8 %fusion.342 = (f32[16,512]{1,0:T(8,128)S(1)}, f32[16,512,1024]{2,1,0:T(8,128)}) fusion(f32[16,512,1024]{2,1,0:T(8,128)} %fusion.188, f32[512,1024]{1,0:T(8,128)} %abs_convert_fusion, f32[16]{0:T(128)S(1)} %reshape.322, pred[1024]{0:T(1024)(128)(4,1)S(1)} %broadcast_compare_fusion), kind=kOutput, calls=%fused_computation.597 | output fusion | flops 83887104 | bytes 69239872 | tf_op jit(solution)/shard_map/sub | solution.py:617
  278.2 14.3 %fusion.216 = bf16[16,64,512]{2,1,0:T(8,128)(2,1)S(1)} fusion(bf16[2,1024,16,64]{1,3,2,0:T(8,128)(2,1)} %copy-done.6, f32[16,512,1024]{2,1,0:T(8,128)} %get-tuple-element.239, f32[16,512]{1,0:T(8,128)S(1)} %get-tuple-element.238), kind=kOutput, calls=%fused_computation.363 | convolution fusion | flops 1091043328 | bytes 36732928 | tf_op jit(solution)/shard_map/hqk,khd->qhd/dot_general | solution.py:620
  300.2 3.6 fusion.185
  303.7 3.6 fusion.177
  349.1 13.2 %fusion.187 = f32[16,512,1024]{2,1,0:T(8,128)} fusion(bf16[512,16,64]{0,2,1:T(8,128)(2,1)S(1)} %bitcast.341, bf16[2,1024,16,64]{1,3,2,0:T(8,128)(2,1)S(1)} %copy-done.7), kind=kOutput, calls=%fused_computation.326 | convolution fusion | flops 1073741824 | bytes 36700160 | tf_op jit(solution)/shard_map/qhd,khd->hqk/dot_general | solution.py:663
  362.4 53.1 %fusion.234 = bf16[512,16,1,64]{0,3,1,2:T(8,128)(2,1)} fusion(f32[16,512,1024]{2,1,0:T(8,128)} %fusion.187, bf16[2,1024,16,64]{1,3,2,0:T(8,128)(2,1)} %copy-done.6, f32[16,512,1024]{2,1,0:T(8,128)} %get-tuple-element.239, f32[16,512]{1,0:T(8,128)S(1)} %copy-done.152), kind=kOutput, calls=%fused_computation.369 | convolution fusion | flops 1132995584 | bytes 137428992 | tf_op jit(solution)/shard_map/hqk,khd->qhd/dot_general | solution.py:666
  415.5 54.8 %fusion.28 = f32[1,1024,16,64]{1,3,2,0:T(8,128)} fusion(f32[16,512,1024]{2,1,0:T(8,128)} %fusion.187, bf16[512,16,3,64]{0,3,2,1:T(8,128)(2,1)} %bitcast.338, f32[16,512,1024]{2,1,0:T(8,128)} %get-tuple-element.239, f32[16,512]{1,0:T(8,128)S(1)} %copy-done.152), kind=kOutput, calls=%fused_computation.72 | convolution fusion | flops 1132471296 | bytes 139526144 | tf_op jit(solution)/shard_map/hqk,qhd->khd/dot_general | solution.py:667
  470.3 12.7 %fusion.25 = f32[1,1024,16,64]{1,3,2,0:T(8,128)S(1)} fusion(bf16[512,16,64]{0,2,1:T(8,128)(2,1)S(1)} %bitcast.342, f32[16,512,1024]{2,1,0:T(8,128)} %get-tuple-element.239, f32[16,512]{1,0:T(8,128)S(1)} %copy-done.152), kind=kOutput, calls=%fused_computation.71 | convolution fusion | flops 1090519040 | bytes 38830080 | tf_op jit(solution)/shard_map/hqk,qhd->khd/dot_general | solution.py:662
  483.1 5.9 convert_bitcast_fusion.3
  488.9 2.8 convert_bitcast_fusion.2
  491.7 2.7 convert_bitcast_fusion.1
  494.5 2.8 convert_bitcast_fusion
  515.1 2.9 pad_maximum_fusion.9.refs_4_
  518.0 7.6 pad_maximum_fusion.1.refs_2_
  525.7 3.9 pad_maximum_fusion.refs_1_
  532.2 4.2 fusion.23
  550.0 7.8 multiply_reduce_fusion.4
  557.8 4.0 multiply_reduce_fusion.22
  563.1 3.0 collective-permute-start.3
  566.2 3.7 pad_maximum_fusion.2.refs_3_
  600.5 20.0 %fusion.333 = (bf16[1024]{0:T(1024)(128)(2,1)}, bf16[512,1024]{1,0:T(8,128)(2,1)}) fusion(f32[512,1024]{1,0:T(8,128)S(1)} %get-tuple-element.216, f32[512,1024]{1,0:T(8,128)S(1)} %get-tuple-element.215, f32[16,1024]{1,0:T(8,128)} %copy-done.70, f32[1024]{0:T(1024)S(1)} %copy-done.83, f32[1024]{0:T(1024)S(1)} %copy-done.85, f32[1024]{0:T(1024)S(1)} %copy-done.87, ...), kind=kLoop, calls=%fused_computation.590 | loop fusion | flops 49806336 | bytes 5505024 | tf_op jit(solution)/shard_map/reduce_sum | solution.py:697
  623.9 11.7 %concatenate.63 = bf16[1024,407]{1,0:T(8,128)(2,1)S(1)} concatenate(bf16[1024,288]{1,0:T(8,128)(2,1)S(1)} %copy.152, bf16[1024,1]{1,0:T(8,128)(2,1)S(1)} %stack.346, bf16[1024,1]{1,0:T(8,128)(2,1)S(1)} %stack.347, bf16[1024,1]{1,0:T(8,128)(2,1)} %stack.348, bf16[1024,1]{1,0:T(8,128)(2,1)} %stack.349, bf16[1024,1]{1,0:T(8,128)(2,1)} %stack.350, bf16[1024,1]{1,0:T(8,128)(2,1)} %stack.351, ...), dimensions={1} | concatenate | bytes 1667072 | tf_op jit(solution)/shard_map/concatenate | solution.py:700
  637.3 193.3 %reduce.79 = (f32[32,512]{1,0:T(8,128)}, f32[128,1024]{1,0:T(8,128)}, f32[128,1024]{1,0:T(8,128)}, f32[128,768]{1,0:T(8,128)}, f32[128,256]{1,0:T(8,128)}, /*index=5*/f32[8,128]{1,0:T(8,128)}) custom-call(bf16[1024,512]{1,0:T(8,128)(2,1)} %pad.23.refs_0_, bf16[4,1024,1024]{2,1,0:T(8,128)(2,1)} %pad_maximum_fusion.refs_1_, ...), custom_call_target="tpu_custom_call" | custom-call | tf_op jit(solution)/shard_map/reduce/pallas_call | solution.py:451
  (509 shorter events, 169.2 us)
Async XLA Ops:
  0.7 150.0 %copy-start = (s32[2,1,1024]{2,1,0:T(1,128)S(1)}, s32[2,1,1024]{2,1,0:T(1,128)}, u32[]{:S(2)}) copy-start(s32[2,1,1024]{2,1,0:T(1,128)} %param.33) | copy-start | bytes 24580
  2.1 130.2 %copy-start.16 = (f32[1024,128]{0,1:T(8,128)}, f32[1024,128]{0,1:T(8,128)S(1)}, u32[]{:S(2)}) copy-start(f32[1024,128]{0,1:T(8,128)S(1)} %copy.142) | copy-start | bytes 1572868
  3.3 130.1 %copy-start.35 = (f32[256,128]{0,1:T(8,128)}, f32[256,128]{0,1:T(8,128)S(1)}, u32[]{:S(2)}) copy-start(f32[256,128]{0,1:T(8,128)S(1)} %copy.141) | copy-start | bytes 393220
  139.3 12.6 %copy-start.92 = (f32[1024]{0:T(1024)}, f32[1024]{0:T(1024)S(1)}, u32[]{:S(2)}) copy-start(f32[1024]{0:T(1024)S(1)} %get-tuple-element.165) | copy-start | bytes 12292
  139.3 12.6 %copy-start.93 = (f32[1024]{0:T(1024)}, f32[1024]{0:T(1024)S(1)}, u32[]{:S(2)}) copy-start(f32[1024]{0:T(1024)S(1)} %get-tuple-element.166) | copy-start | bytes 12292
  139.4 12.6 %copy-start.94 = (f32[1024]{0:T(1024)}, f32[1024]{0:T(1024)S(1)}, u32[]{:S(2)}) copy-start(f32[1024]{0:T(1024)S(1)} %get-tuple-element.167) | copy-start | bytes 12292
  139.4 12.6 %copy-start.95 = (f32[1024]{0:T(1024)}, f32[1024]{0:T(1024)S(1)}, u32[]{:S(2)}) copy-start(f32[1024]{0:T(1024)S(1)} %get-tuple-element.168) | copy-start | bytes 12292
  139.4 24.6 %copy-start.71 = (f32[1024]{0:T(1024)}, f32[1024]{0:T(1024)S(1)}, u32[]{:S(2)}) copy-start(f32[1024]{0:T(1024)S(1)} %get-tuple-element.159) | copy-start | bytes 12292
  151.0 13.9 %slice-start.5 = ((s8[6291456]{0:T(1024)(128)(4,1)}), s8[4194304]{0:T(1024)(128)(4,1)S(1)}, s32[]{:S(2)}) async-start(s8[6291456]{0:T(1024)(128)(4,1)} %bitcast.362), calls=%async_computation.5 | async-start | bytes 8388608
  152.1 12.7 %slice-start.6 = ((s8[6291456]{0:T(1024)(128)(4,1)}), s8[2097152]{0:T(1024)(128)(4,1)S(1)}, s32[]{:S(2)}) async-start(s8[6291456]{0:T(1024)(128)(4,1)} %bitcast.362), calls=%async_computation.6 | async-start | bytes 4194304
  163.7 133.6 %copy-start.4 = (f32[512,1024]{1,0:T(8,128)}, f32[512,1024]{1,0:T(8,128)S(1)}, u32[]{:S(2)}) copy-start(f32[512,1024]{1,0:T(8,128)S(1)} %get-tuple-element.224) | copy-start | bytes 6291460
  177.8 40.1 %collective-permute-start = (bf16[2,512,16,64]{1,3,2,0:T(8,128)(2,1)}, bf16[2,512,16,64]{1,3,2,0:T(8,128)(2,1)}, u32[]{:S(2)}, u32[]{:S(2)}) collective-permute-start(bf16[2,512,16,64]{1,3,2,0:T(8,128)(2,1)} %pad_maximum_fusion.8), channel_id=1, source_target_pairs={{1,0},{0,1},{3,2},{2,3},{5,4},{4,5},{7,6},{6,7},{9,8},{8,9},{11,10... | collective-permute-start | bytes 6291464 | tf_op jit(solution)/shard_map/ppermute | solution.py:592
  216.2 102.9 %copy-start.126 = (f32[512]{0:T(512)}, f32[512]{0:T(512)S(1)}, u32[]{:S(2)}) copy-start(f32[512]{0:T(512)S(1)} %get-tuple-element.221) | copy-start | bytes 6148
  278.2 14.3 %copy-start.151 = (f32[16,512]{1,0:T(8,128)}, f32[16,512]{1,0:T(8,128)S(1)}, u32[]{:S(2)}) copy-start(f32[16,512]{1,0:T(8,128)S(1)} %get-tuple-element.238) | copy-start | bytes 98308
  294.0 13.3 %slice-start = ((s8[18874368]{0:T(1024)(128)(4,1)}), s8[4194304]{0:T(1024)(128)(4,1)S(1)}, s32[]{:S(2)}) async-start(s8[18874368]{0:T(1024)(128)(4,1)} %bitcast.360), calls=%async_computation | async-start | bytes 8388608
  303.7 17.7 %copy-start.22 = (f32[512,1024]{1,0:T(8,128)}, f32[512,1024]{1,0:T(8,128)S(1)}, u32[]{:S(2)}) copy-start(f32[512,1024]{1,0:T(8,128)S(1)} %fusion.185) | copy-start | bytes 6291460
  310.0 18.4 %copy-start.137 = (f32[512,1024]{1,0:T(8,128)}, f32[512,1024]{1,0:T(8,128)S(1)}, u32[]{:S(2)}) copy-start(f32[512,1024]{1,0:T(8,128)S(1)} %fusion.161) | copy-start | bytes 6291460
  349.1 13.2 %copy-start.152 = (f32[16,512]{1,0:T(8,128)S(1)}, f32[16,512]{1,0:T(8,128)}, u32[]{:S(2)}) copy-start(f32[16,512]{1,0:T(8,128)} %copy-done.151) | copy-start | bytes 98308
  470.3 12.7 %copy-start.46 = (bf16[512,1024]{1,0:T(8,128)(2,1)S(1)}, bf16[512,1024]{1,0:T(8,128)(2,1)}, u32[]{:S(2)}) copy-start(bf16[512,1024]{1,0:T(8,128)(2,1)} %copy-done.45) | copy-start | bytes 3145732
  483.1 25.0 %copy-start.9 = (f32[1,1024,16,64]{1,3,2,0:T(8,128)}, f32[1,1024,16,64]{1,3,2,0:T(8,128)S(1)}, u32[]{:S(2)}) copy-start(f32[1,1024,16,64]{1,3,2,0:T(8,128)S(1)} %fusion.25) | copy-start | bytes 12582916
  510.1 19.5 %collective-permute-start.1 = (bf16[2,512,16,64]{1,3,2,0:T(8,128)(2,1)}, bf16[2,512,16,64]{1,3,2,0:T(8,128)(2,1)S(1)}, u32[]{:S(2)}, u32[]{:S(2)}) collective-permute-start(bf16[2,512,16,64]{1,3,2,0:T(8,128)(2,1)} %fusion.24), channel_id=1, source_target_pairs={{0,1},{1,0},{2,3},{3,2},{4,5},{5,4},{6,7},{7,6},{8,9},{9,8},{10,11... | collective-permute-start | bytes 6291464 | tf_op jit(solution)/shard_map/ppermute | solution.py:596
  561.8 37.4 %collective-permute-start.2 = (f32[16,1024]{1,0:T(8,128)S(1)}, f32[16,1024]{1,0:T(8,128)S(1)}, u32[]{:S(2)}, u32[]{:S(2)}) collective-permute-start(f32[16,1024]{1,0:T(8,128)S(1)} %get-tuple-element.228), channel_id=1, source_target_pairs={{1,0},{3,2},{5,4},{7,6},{9,8},{11,10},{13,12},{15,14},{17,16},{19,... | collective-permute-start | bytes 196616 | tf_op jit(solution)/shard_map/ppermute | solution.py:683
  563.1 36.1 %collective-permute-start.3 = (f32[16,1024]{1,0:T(8,128)S(1)}, f32[16,1024]{1,0:T(8,128)S(1)}, u32[]{:S(2)}, u32[]{:S(2)}) collective-permute-start(f32[16,1024]{1,0:T(8,128)S(1)} %get-tuple-element.229), channel_id=1, source_target_pairs={{0,1},{2,3},{4,5},{6,7},{8,9},{10,11},{12,13},{14,15},{16,17},{18,... | collective-permute-start | bytes 196616 | tf_op jit(solution)/shard_map/ppermute | solution.py:686
  584.7 15.8 %copy-start.83 = (f32[1024]{0:T(1024)S(1)}, f32[1024]{0:T(1024)}, u32[]{:S(2)}) copy-start(f32[1024]{0:T(1024)} %copy-done.82) | copy-start | bytes 12292
  584.7 15.8 %copy-start.85 = (f32[1024]{0:T(1024)S(1)}, f32[1024]{0:T(1024)}, u32[]{:S(2)}) copy-start(f32[1024]{0:T(1024)} %copy-done.84) | copy-start | bytes 12292
  584.7 15.8 %copy-start.87 = (f32[1024]{0:T(1024)S(1)}, f32[1024]{0:T(1024)}, u32[]{:S(2)}) copy-start(f32[1024]{0:T(1024)} %copy-done.86) | copy-start | bytes 12292
  584.7 15.8 %copy-start.89 = (f32[1024]{0:T(1024)S(1)}, f32[1024]{0:T(1024)}, u32[]{:S(2)}) copy-start(f32[1024]{0:T(1024)} %copy-done.88) | copy-start | bytes 12292
  584.7 15.8 %copy-start.91 = (f32[1024]{0:T(1024)S(1)}, f32[1024]{0:T(1024)}, u32[]{:S(2)}) copy-start(f32[1024]{0:T(1024)} %copy-done.90) | copy-start | bytes 12292
  600.5 20.0 %copy-start.53 = (bf16[544,128]{1,0:T(8,128)(2,1)S(1)}, bf16[544,128]{1,0:T(8,128)(2,1)}, u32[]{:S(2)}) copy-start(bf16[544,128]{1,0:T(8,128)(2,1)} %copy-done.52) | copy-start | bytes 417796
  637.3 195.4 %copy-start.17 = (f32[1024,128]{0,1:T(8,128)S(1)}, f32[1024,128]{0,1:T(8,128)}, u32[]{:S(2)}) copy-start(f32[1024,128]{0,1:T(8,128)} %copy-done.16) | copy-start | bytes 1572868
  637.3 195.4 %copy-start.20 = (f32[1024,128]{0,1:T(8,128)S(1)}, f32[1024,128]{0,1:T(8,128)}, u32[]{:S(2)}) copy-start(f32[1024,128]{0,1:T(8,128)} %copy.197) | copy-start | bytes 1572868
  637.3 195.4 %copy-start.21 = (f32[1024,128]{0,1:T(8,128)S(1)}, f32[1024,128]{0,1:T(8,128)}, u32[]{:S(2)}) copy-start(f32[1024,128]{0,1:T(8,128)} %copy.198) | copy-start | bytes 1572868
  (134 other events, 681.8 us)

commit v3 on v1

v3 whole, which is shorter than its diff:
```python
import functools
from typing import Any, NamedTuple

import jax
import jax.numpy as jnp
from jax import lax
from jax.experimental import pallas as pl
from jax.experimental.pallas import tpu as pltpu
from jax.sharding import PartitionSpec as P

HEADS = 16
HEAD_DIM = 64
PHONES = 128
KERNEL = 31
HALF = 15
PAD = 16
TSTEPS = 1000
STEP = 10

SIGMA = 1e-05
BETA_ONE = 0.9
BETA_TWO = 0.999
EPSILON = 1e-08
DECAY = 0.01
RATE = 0.15
CLIP_AT = 0.1
NORM_EPS = 1e-05
SCALE = HEAD_DIM**-0.5
bf = jnp.bfloat16
f32 = jnp.float32


def gelu(v):
    return jax.nn.gelu(v, approximate=True)


def gelu_back(v, dv):
    return jax.vjp(gelu, v)[1](dv)[0]


def dot(left, right):
    return jnp.dot(left, right, preferred_element_type=f32)


def tdot(left, right):
    return lax.dot_general(
        left, right, (((0,), (0,)), ((), ())), preferred_element_type=f32
    )


def rdot(left, right):
    return lax.dot_general(
        left, right, (((1,), (1,)), ((), ())), preferred_element_type=f32
    )


def norm_parts(v):
    centered = v - jnp.mean(v, axis=-1, keepdims=True)
    spread = jnp.mean(centered * centered, axis=-1, keepdims=True)
    r = lax.rsqrt(spread + NORM_EPS)
    return centered * r, r


def norm_back(da, xhat, r, gain):
    dgain = jnp.sum(da * xhat, axis=0)
    dbias = jnp.sum(da, axis=0)
    dx = da * gain
    dv = r * (
        dx
        - jnp.mean(dx, axis=-1, keepdims=True)
        - xhat * jnp.mean(dx * xhat, axis=-1, keepdims=True)
    )
    return dv, dgain, dbias


def adam_update(weight, first, second, grad, factor):
    clipped = grad * factor
    first_new = BETA_ONE * first + (1.0 - BETA_ONE) * clipped
    second_new = BETA_TWO * second + (1.0 - BETA_TWO) * clipped * clipped
    first_hat = first_new / (1.0 - BETA_ONE**STEP)
    second_hat = second_new / (1.0 - BETA_TWO**STEP)
    weight_new = weight - RATE * (first_hat / (jnp.sqrt(second_hat) + EPSILON) + DECAY * weight)
    return (weight_new, first_new, second_new)


MESH = pl.DeviceIdType.MESH
AXES = ("z", "x", "y", "c")


class Wires:
    def __init__(self, ndp, nmp):
        self.sizes = {"z": ndp // 2, "x": 2, "y": nmp // 2, "c": 2}
        dp = lax.axis_index("dp")
        mp = lax.axis_index("mp")
        self.at = {"z": dp // 2, "x": dp % 2, "y": mp // 2, "c": mp % 2}

    def peer(self, axis, k):
        at = dict(self.at)
        at[axis] = lax.rem(at[axis] + k, self.sizes[axis])
        return (at["z"] * 2 + at["x"], at["y"] * 2 + at["c"])

    def owner_mp(self, ky, kc):
        ny = self.sizes["y"]
        return lax.rem(self.at["y"] + ny - ky, ny) * 2 + lax.rem(self.at["c"] + 2 - kc, 2)

    def near(self, k):
        nmp = self.sizes["y"] * self.sizes["c"]
        return (lax.axis_index("dp"), lax.rem(lax.axis_index("mp") + k, nmp))

    def far(self, k):
        ndp = self.sizes["z"] * self.sizes["x"]
        return (lax.rem(lax.axis_index("dp") + k, ndp), lax.axis_index("mp"))

    def align(self, again):
        fars = [self.far(k) for k in range(1, self.sizes["z"] * self.sizes["x"])]
        self.greet([self.near(k) for k in range(1, self.sizes["y"] * self.sizes["c"])] + fars)
        for p in fars:
            pl.semaphore_signal(again, inc=1, device_id=p, device_id_type=MESH)
        pl.semaphore_wait(again, len(fars))

    def greet(self, peers):
        barrier = pltpu.get_barrier_semaphore()
        for p in peers:
            pl.semaphore_signal(barrier, inc=1, device_id=p, device_id_type=MESH)
        pl.semaphore_wait(barrier, len(peers))


def slot_number(sizes, k):
    return ((k["z"] * sizes["x"] + k["x"]) * sizes["y"] + k["y"]) * sizes["c"] + k["c"]


def spread(sizes, order):
    slots = [(dict.fromkeys(AXES, 0), -1)]
    for stage, axis in enumerate(order):
        slots += [
            ({**k, axis: n}, stage) for n in range(1, sizes[axis]) for k, _ in list(slots)
        ]
    return slots


class Gather:
    def __init__(self, wires, order, own, slot, send, recv):
        self.wires, self.order, self.own, self.slot = wires, order, own, slot
        self.send, self.recv = send, recv
        self.slots = spread(wires.sizes, order)
        self.by_number = {slot_number(wires.sizes, k): i for i, (k, _) in enumerate(self.slots)}
        self.started = []

    def forward(self, source, k, stage):
        for later in range(stage + 1, len(self.order)):
            axis = self.order[later]
            for n in range(1, self.wires.sizes[axis]):
                there = {**k, axis: n}
                number = slot_number(self.wires.sizes, there)
                copy = pltpu.make_async_remote_copy(
                    source, self.slot(there, k), self.send.at[number], self.recv.at[number],
                    device_id=self.wires.peer(axis, n), device_id_type=MESH,
                )
                copy.start()
                self.started.append((copy, number))

    def begin(self):
        k, stage = self.slots[0]
        self.forward(self.own, k, stage)

    def arrive(self, number):
        k, stage = self.slots[self.by_number[number]]
        here = self.slot(k, k)
        pltpu.make_async_remote_copy(
            here, here, self.send.at[number], self.recv.at[number],
            device_id=self.wires.peer("c", 1), device_id_type=MESH,
        ).wait_recv()
        self.forward(here, k, stage)

    def finish(self):
        for copy, _ in self.started:
            copy.wait_send()


FIRST = ("z", "x", "y", "c")
OTHER = ("z", "y", "x", "c")


def total(ref):
    rows = 8

    def body(i, part):
        x = ref[pl.ds(i * rows, rows)]
        return part + x * x

    part = lax.fori_loop(0, ref.shape[0] // rows, body, jnp.zeros((rows, ref.shape[1]), f32))
    return jnp.sum(part)


BLOCK = 256
TILE = 64
FAR = 1e12


def distances(dist, base, other_base, size):
    rows = dist.shape[1]

    def body(i, _):
        here = pl.ds(pl.multiple_of(i * TILE, TILE), TILE)
        down = lax.broadcasted_iota(jnp.int32, (TILE, rows), 0) + i * TILE
        key = jnp.where(down < rows, base + down, other_base + down - rows)
        query = base + lax.broadcasted_iota(jnp.int32, (TILE, rows), 1)
        dist[here] = jnp.where(key < size, jnp.abs(key - query).astype(f32), FAR)
        return 0

    lax.fori_loop(0, dist.shape[0] // TILE, body, 0)


def key_blocks(packed, other, m, col):
    rows = packed.shape[1]
    twin = m + 1 - 2 * (m % 2)
    for part, (ref, index) in enumerate(((packed, m), (other, twin))):
        for start in range(0, rows, BLOCK):
            k = ref[index, start : start + BLOCK, col + HEAD_DIM : col + 2 * HEAD_DIM]
            v = ref[index, start : start + BLOCK, col + 2 * HEAD_DIM : col + 3 * HEAD_DIM]
            yield part, start, part * rows + start, k, v


def attend(packed, other, dist, slopes, mixed, mixed_t, lse, score, m):
    heads = packed.shape[2] // (3 * HEAD_DIM)
    for j in range(heads):
        col = j * 3 * HEAD_DIM
        q = packed[m, :, col : col + HEAD_DIM] * bf(SCALE)
        slope = slopes[m * heads + j]
        top = None
        for _, _, at, k, _ in key_blocks(packed, other, m, col):
            s = rdot(k, q) - slope * dist[at : at + BLOCK]
            score[at : at + BLOCK] = s
            peak = jnp.max(s, axis=0, keepdims=True)
            top = peak if top is None else jnp.maximum(top, peak)
        total_e = jnp.zeros_like(top)
        acc = None
        for _, _, at, _, v in key_blocks(packed, other, m, col):
            e = jnp.exp(score[at : at + BLOCK] - top)
            total_e = total_e + jnp.sum(e, axis=0, keepdims=True)
            part = tdot(v, e.astype(bf))
            acc = part if acc is None else acc + part
        out = acc / total_e
        row = (m * heads + j) * HEAD_DIM
        mixed_t[pl.ds(pl.multiple_of(row, HEAD_DIM), HEAD_DIM)] = out
        mixed[m, :, j * HEAD_DIM : (j + 1) * HEAD_DIM] = out.T.astype(bf)
        lse[m * heads + j] = top + jnp.log(total_e)
        yield


def attend_back(packed, other, dist, slopes, mixed_t, lse, dmixed, down, dother, m):
    heads = packed.shape[2] // (3 * HEAD_DIM)
    for j in range(heads):
        col = j * 3 * HEAD_DIM
        q = packed[m, :, col : col + HEAD_DIM] * bf(SCALE)
        slope = slopes[m * heads + j]
        row = (m * heads + j) * HEAD_DIM
        mt = mixed_t[pl.ds(pl.multiple_of(row, HEAD_DIM), HEAD_DIM)]
        dm = dmixed[m, :, j * HEAD_DIM : (j + 1) * HEAD_DIM]
        delta = jnp.sum(dm.astype(f32).T * mt, axis=0, keepdims=True)
        level = lse[m * heads + j]
        dq = None
        for part, start, at, k, v in key_blocks(packed, other, m, col):
            p = jnp.exp(rdot(k, q) - slope * dist[at : at + BLOCK] - level)
            dv = dot(p.astype(bf), dm)
            t = (p * (rdot(v, dm) - delta)).astype(bf)
            dk = dot(t, q)
            more = tdot(k, t)
            dq = more if dq is None else dq + more
            here = slice(start, start + BLOCK)
            ref = dother if part else down.at[m]
            ref[here, col + HEAD_DIM : col + 2 * HEAD_DIM] = dk.astype(ref.dtype)
            ref[here, col + 2 * HEAD_DIM : col + 3 * HEAD_DIM] = dv.astype(ref.dtype)
        down[m, :, col : col + HEAD_DIM] = (dq * SCALE).T.astype(down.dtype)
        yield


def windows(x, count):
    for j in range(8):
        moved = x if j == 0 else pltpu.roll(x, x.shape[0] - j, 0)
        for far in range(0, count + 1, 8):
            if 1 <= far + j <= count:
                yield far + j, moved[far : far + TILE]


def convolve(hm, chan, conv, column):
    lanes = slice(column, column + 128)

    def body(r, _):
        start = pl.multiple_of(r * TILE, TILE)
        x = hm[pl.ds(start, TILE + 2 * PAD), lanes]
        acc = jnp.broadcast_to(chan[KERNEL + 7, lanes][None], (TILE, 128))
        for offset, moved in windows(x, KERNEL):
            acc = acc + chan[offset - 1, lanes][None] * moved
        conv[pl.ds(start, TILE), lanes] = acc
        return 0

    lax.fori_loop(0, conv.shape[0] // TILE, body, 0)


def convolve_back(dconv, hm, chan, back, gtaps, column):
    lanes = slice(column, column + 128)

    def body(r, _):
        start = pl.multiple_of(r * TILE, TILE)
        x = dconv[pl.ds(start, TILE + 2 * PAD), lanes]
        acc = jnp.zeros((TILE, 128), f32)
        for offset, moved in windows(x, KERNEL):
            acc = acc + chan[KERNEL - offset, lanes][None] * moved
        back[pl.ds(start, TILE), lanes] = acc
        here = x[PAD : PAD + TILE]
        y = hm[pl.ds(start, TILE + 2 * PAD), lanes]
        for offset, moved in windows(y, KERNEL):
            part = here * moved
            part = sum(part[i : i + 8] for i in range(8, TILE, 8)) + part[:8]
            rows_at = slice((offset - 1) * 8, offset * 8)
            gtaps[rows_at, lanes] = gtaps[rows_at, lanes] + part
        return 0

    lax.fori_loop(0, back.shape[0] // TILE, body, 0)


VMEM = pl.BlockSpec(memory_space=pltpu.VMEM)
SMEM = pl.BlockSpec(memory_space=pltpu.SMEM)


class Reduce:
    def __init__(self, wires, order, source, landing, out, send, recv):
        self.wires, self.order, self.source, self.landing = wires, order, source, landing
        self.out, self.send, self.recv = out, send, recv
        self.where = {}
        self.started = []
        sizes = {a: wires.sizes[a] if a in order else 1 for a in AXES}
        slots = [k for k, _ in spread(sizes, order[::-1])]
        self.stages = []
        for axis in order:
            self.stages.append([k for k in slots if k[axis]])
            slots = [k for k in slots if not k[axis]]
        self.by_number = {
            self.number(k): (stage, k) for stage, ks in enumerate(self.stages) for k in ks
        }
        self.summed = set()

    def number(self, k):
        return slot_number(self.wires.sizes, k)

    def now(self, k):
        n = self.number(k)
        return self.landing(self.where[n]) if n in self.where else self.source(k)

    def leave(self, stage, k):
        axis = self.order[stage]
        n = self.wires.sizes[axis]
        number = self.number(k)
        source = self.now(k)
        pltpu.make_async_remote_copy(
            source, self.landing(k), self.send.at[number], self.recv.at[number],
            device_id=self.wires.peer(axis, (n - k[axis]) % n), device_id_type=MESH,
        ).start()
        self.started.append((k, number))

    def keep(self):
        add_rows(self.out, self.source(dict.fromkeys(AXES, 0)), None)

    def depart(self, number):
        self.leave(0, self.by_number[number][1])

    def terms(self, stage, kept):
        return {
            self.number({**kept, axis: n})
            for axis in self.order[: stage + 1]
            for n in range(1, self.wires.sizes[axis])
        }

    def arrive(self, number):
        stage, k = self.by_number[number]
        self.summed.add(number)
        here = self.landing(k)
        axis = self.order[stage]
        pltpu.make_async_remote_copy(
            here, here, self.send.at[number], self.recv.at[number],
            device_id=self.wires.peer(axis, 1), device_id_type=MESH,
        ).wait_recv()
        kept = {**k, axis: 0}
        if not any(kept.values()):
            add_rows(self.out, self.out, here)
            return
        add_rows(here, self.now(kept), here)
        self.where[self.number(kept)] = k
        last = k[axis] == self.wires.sizes[axis] - 1
        if last and stage + 1 < len(self.order) and kept[self.order[stage + 1]]:
            assert self.terms(stage, kept) <= self.summed
            self.leave(stage + 1, kept)

    def finish(self):
        for k, number in self.started:
            here = self.landing(k)
            pltpu.make_async_remote_copy(
                here, here, self.send.at[number], self.recv.at[number],
                device_id=self.wires.peer("c", 1), device_id_type=MESH,
            ).wait_send()


class Crossing:
    def __init__(self, *parts):
        self.parts = parts

    def make(self):
        (src, *s), (dst, *d), send, recv, i, wires = self.parts
        return pltpu.make_async_remote_copy(
            src.at[s[0]] if s else src, dst.at[d[0]] if d else dst, send.at[i], recv.at[i],
            device_id=wires.peer("c", 1), device_id_type=MESH,
        )

    def wait_send(self):
        self.make().wait_send()

    def wait_recv(self):
        self.make().wait_recv()


def add_rows(out, left, right):
    step = 16

    def body(i, _):
        here = pl.ds(pl.multiple_of(i * step, step), step)
        value = left[here].astype(f32)
        if right is not None:
            value = value + right[here].astype(f32)
        out[here] = value.astype(out.dtype)
        return 0

    lax.fori_loop(0, out.shape[0] // step, body, 0)


def gelu_slope(v):
    cube = 0.044715 * v * v * v
    t = jnp.tanh(0.7978845608028654 * (v + cube))
    inner = 0.7978845608028654 * (1.0 + 3.0 * 0.044715 * v * v)
    return 0.5 * (1.0 + t) + 0.5 * v * (1.0 - t * t) * inner


THIN_CHAN = 384
THIN_HEAD = 512
THIN = 640


class BackIn(NamedTuple):
    places: Any
    slopes: Any
    loss: Any
    g_up: Any
    g_down: Any
    dattn: Any
    mixed: Any
    extra: Any
    g_head: Any
    chan: Any
    packed: Any
    other: Any
    mixed_t: Any
    lse: Any
    dmixed: Any
    w_qkv: Any
    first: Any
    conv: Any
    dsecond: Any
    hm: Any
    features: Any


class BackRefs(NamedTuple):
    places: Any
    slopes: Any
    loss: Any
    g_up: Any
    g_down: Any
    dattn: Any
    mixed: Any
    extra: Any
    g_head: Any
    chan: Any
    packed: Any
    other: Any
    mixed_t: Any
    lse: Any
    dmixed: Any
    w_qkv: Any
    first: Any
    conv: Any
    dsecond: Any
    hm: Any
    features: Any
    o_thin: Any
    o_up: Any
    o_down: Any
    o_qkv: Any
    o_out: Any
    sums: Any
    g_qkv: Any
    g_out: Any
    thin: Any
    l_up0: Any
    l_up1: Any
    l_down0: Any
    l_down1: Any
    l_qkv0: Any
    l_qkv1: Any
    l_out0: Any
    l_out1: Any
    l_thin: Any
    down: Any
    dother: Any
    l_other: Any
    a1: Any
    l_a1: Any
    l_dattn: Any
    l_mixed: Any
    l_dpack: Any
    halo: Any
    edge: Any
    parts: Any
    w_buf: Any
    rows_buf: Any
    send: Any
    recv: Any
    c_send: Any
    c_recv: Any
    local: Any
    near_send: Any
    near_recv: Any
    far_send: Any
    far_recv: Any
    again: Any


COLS = 256


def by_tiles(count, size, body):
    def step(i, _):
        body(pl.ds(pl.multiple_of(i * size, size), size))
        return 0

    lax.fori_loop(0, count // size, step, 0)


def fold(x):
    return jnp.sum(x, axis=0, keepdims=True)


def norm_turn(da, xhat, scale, gain):
    dx = da * gain
    return scale * (
        dx
        - jnp.mean(dx, axis=-1, keepdims=True)
        - xhat * jnp.mean(dx * xhat, axis=-1, keepdims=True)
    )


FORE_TURNS = (
    (
        1, 8, 4, 2, 9, 16, 5, 3, 24, 17, 25, 12, 10, 6, 20, 13, 11, 28, 18, 7, 21, 26, 29, 19, 14, 27, 22,
        15, 30, 23, 31, 33, 65, 36, 34, 68, 66, 40, 48,
    ),
    (56,),
    (),
    (72,),
    (37, 35),
    (69, 67),
    (41,),
    (49,),
    (38,),
    (97, 70),
    (129,),
    (80, 42, 44, 57),
    (73, 88, 50, 52),
    (),
    (39, 71),
    (98,),
    (100, 81, 43, 45),
    (),
    (89, 51, 53),
    (130,),
    (132,),
    (104, 58),
    (
        60, 74, 76, 82, 84, 59, 61, 75, 77, 83, 46, 85, 92, 90, 47, 93, 91, 54, 55, 78, 86, 79, 87, 62, 94,
        63, 95, 99, 101, 112, 131, 120, 133, 105, 134, 108, 136, 102, 144, 106, 152,
    ),
    (),
    (),
    (),
    (113,),
    (121, 135, 109, 137, 103, 145, 107, 116, 153, 114),
    (),
    (124,),
    (122, 161, 193),
    (140,),
    (117, 115, 110),
    (),
    (148, 125, 138, 168, 123),
    (141,),
    (156, 176, 146, 111),
    (184, 164),
    (149, 154, 139, 169),
    (196,),
    (162, 157, 177, 147),
    (142, 200, 185, 194, 165),
    (155, 172, 208),
    (118, 143, 126, 150, 119, 127, 151, 158, 159, 197, 163, 180, 216, 201, 195, 173, 209, 170, 188),
    (178,),
    (186,),
    (204, 181, 166, 217, 171, 189),
    (198, 202, 179),
    (212, 174, 187),
    (
        220, 205, 210, 167, 199, 182, 203, 206, 213, 218, 175, 221, 211, 183, 207, 219, 214, 190, 215, 222,
        191, 223,
    ),
)
BACK_TURNS = (
    (34, 100, 42, 108, 50, 116, 58, 124, 38, 102, 46, 110),
    (54, 118),
    (62, 126, 162, 228, 2, 68),
    (170, 236, 10, 76),
    (178, 244, 18, 84),
    (186, 252, 26, 92, 166, 230, 6, 70),
    (14, 78),
    (22, 86),
    (30, 94),
    (130, 196),
    (174, 238, 138, 204, 182, 246, 146, 212),
    (190, 254, 154, 220),
    (290, 356, 298, 364, 306, 372, 134, 198),
    (314, 380, 66, 4, 294, 358, 74, 12, 302, 366),
    (310, 374, 318, 382, 82, 20),
    (90, 28),
    (72, 142, 206, 8, 150, 214),
    (158, 222, 258, 324, 266, 332),
    (274, 340, 80),
    (194, 132, 282, 348),
    (262, 326, 270, 334, 278, 342, 16, 286, 350),
    (88, 202, 140),
    (418, 484, 426, 492, 434, 500, 442, 508, 422, 486, 430, 494, 438, 502, 446, 510, 24, 210, 148),
    (218, 156, 322, 260),
    (330, 268, 338, 276, 346, 284, 200),
    (),
    (386, 452, 136, 394, 460),
    (402, 468),
    (410, 476, 208),
    (390, 454),
    (398, 462, 144, 406, 470),
    (414, 478, 216),
    (388, 450, 152),
    (328, 264, 396, 458),
    (336, 404, 466, 272, 344),
    (
        545, 553, 561, 569, 549, 557, 565, 573, 547, 555, 563, 571, 551, 559, 567, 575, 280, 412, 474, 392,
        456, 513, 521, 529, 537, 517, 525, 533, 541, 515, 523, 531, 539, 519, 527, 535, 543, 400, 514, 522,
        530, 464, 538, 518, 408, 526, 534, 516, 542, 472, 524, 532, 540, 520, 528, 536,
    ),
)


class ForeIn(NamedTuple):
    places: Any
    slopes: Any
    thin_own: Any
    near_own: Any
    mid_own: Any
    down_own: Any
    features: Any


class ForeOut(NamedTuple):
    thin: Any
    near: Any
    mid: Any
    down: Any
    hm: Any
    conv: Any
    first: Any
    packed: Any
    other: Any
    mixed: Any
    mixed_t: Any
    lse: Any
    chan: Any
    second: Any
    a2: Any
    active: Any
    slope: Any


class ForeRefs(NamedTuple):
    places: Any
    slopes: Any
    thin_own: Any
    near_own: Any
    mid_own: Any
    down_own: Any
    features: Any
    o_thin: Any
    o_near: Any
    mid: Any
    down: Any
    o_hm: Any
    o_conv: Any
    o_first: Any
    o_packed: Any
    o_other: Any
    o_mixed: Any
    o_mixed_t: Any
    o_lse: Any
    o_chan: Any
    o_second: Any
    o_a2: Any
    o_active: Any
    o_slope: Any
    thin: Any
    near: Any
    hm: Any
    conv: Any
    first: Any
    packed: Any
    other: Any
    mixed: Any
    mixed_t: Any
    lse: Any
    chan: Any
    second: Any
    a2: Any
    active: Any
    slope: Any
    a1: Any
    dist: Any
    score: Any
    w: Any
    send: Any
    recv: Any
    local: Any
    c_send: Any
    c_recv: Any
    again: Any


def fore_kernel(ndp, nmp, *refs):
    r = ForeRefs(*refs)
    wires = Wires(ndp, nmp)
    wires.align(r.again)
    sizes = wires.sizes
    thin_rows = r.thin_own.shape[0]
    rows, model = r.first.shape
    size = r.places[2]

    def thin_slot(k, sent):
        block = (k["z"] * sizes["x"] + k["x"]) * nmp + wires.owner_mp(sent["y"], sent["c"])
        return r.thin.at[pl.ds(pl.multiple_of(block * thin_rows, thin_rows), thin_rows)]

    flows = [Gather(wires, FIRST, r.thin_own, thin_slot, r.send.at[0], r.recv.at[0])]

    def wide_flow(own, out, half, order):
        height = own.shape[0] // 2

        def slot(k, sent):
            start = (k["z"] * sizes["x"] + k["x"]) * 2 * height + half * height
            return out.at[k["y"] * sizes["c"] + k["c"], pl.ds(start, height)]

        n = len(flows)
        part = own.at[pl.ds(half * height, height)]
        flows.append(Gather(wires, order, part, slot, r.send.at[n], r.recv.at[n]))
        return flows[-1]

    near = [wide_flow(r.near_own, r.near, h, o) for h, o in enumerate((FIRST, OTHER))]
    mid = [wide_flow(r.mid_own, r.mid, h, o) for h, o in enumerate((FIRST, OTHER))]
    down = [wide_flow(r.down_own, r.down, h, o) for h, o in enumerate((FIRST, OTHER))]
    zero = dict.fromkeys(AXES, 0)
    kept = [
        pltpu.make_async_copy(f.own, f.slot(zero, zero), r.local.at[i])
        for i, f in enumerate(flows)
    ]
    for copy in kept:
        copy.start()
    for f in flows[:1] + near:
        f.begin()
    turns = iter(FORE_TURNS)
    slots = ndp * nmp
    saves = []

    def save(src, dst):
        copy = pltpu.make_async_copy(src, dst, r.local.at[len(flows) + nmp + len(saves)])
        copy.start()
        saves.append(copy)

    def turn():
        for code in next(turns):
            flows[code // slots].arrive(code % slots)

    turn()
    for f in mid:
        f.begin()
    for copy in kept:
        copy.wait()

    for i in range(0, model, 128):
        cols = r.thin[i : i + 128, THIN_CHAN:THIN_HEAD].astype(f32)
        r.chan[:, i : i + 128] = cols.T
    save(r.chan, r.o_chan)
    save(r.thin, r.o_thin)
    distances(r.dist, r.places[0], r.places[1], size)
    turn()

    for column in range(0, model, 128):
        cols = slice(column, column + 128)
        h = rdot(r.features[...], r.thin[cols, :THIN_CHAN])
        h = h + r.chan[KERNEL + 6, cols][None]
        place = r.places[0] - PAD + lax.broadcasted_iota(jnp.int32, (h.shape[0], 1), 0)
        r.first[:, cols] = h[PAD : PAD + rows]
        r.hm[:, cols] = jnp.where((place >= 0) & (place < size), h, 0.0)
        turn()
    for c in range(0, model, 128):
        convolve(r.hm, r.chan, r.conv, c)
        turn()

    def norm(i, _):
        here = pl.ds(pl.multiple_of(i * TILE, TILE), TILE)
        v = r.conv[here]
        inner = 0.7978845608028654 * v * (1.0 + 0.044715 * v * v)
        first = r.first[here] + v * (0.5 + 0.5 * jnp.tanh(inner))
        r.first[here] = first
        xhat, _ = norm_parts(first)
        r.a1[here] = (xhat * r.chan[KERNEL][None] + r.chan[KERNEL + 1][None]).astype(bf)

        return 0

    save(r.hm, r.o_hm)
    save(r.conv, r.o_conv)
    for i in range(0, rows // TILE, 2):
        lax.fori_loop(i, i + 2, norm, 0)
        turn()
    save(r.first, r.o_first)
    turn()
    crossings = []
    width = r.packed.shape[2]
    for m in range(nmp):
        def expand(cols):
            r.packed[m, :, cols] = dot(r.a1[...], r.near[m, :, cols]).astype(bf)

        by_tiles(width, COLS, expand)
        copy = pltpu.make_async_remote_copy(
            r.packed.at[m], r.other.at[m], r.c_send.at[m], r.c_recv.at[m],
            device_id=wires.peer("c", 1), device_id_type=MESH,
        )
        copy.start()
        crossings.append(copy)
        turn()
    for f in down:
        f.begin()
    save(r.near, r.o_near)
    save(r.packed, r.o_packed)
    for m in range(nmp):
        crossings[m + 1 - 2 * (m % 2)].wait_recv()
        for _ in attend(
            r.packed, r.other, r.dist, r.slopes, r.mixed, r.mixed_t, r.lse,
            r.score, m,
        ):
            turn()
    turn()
    for src, dst in (
        (r.other, r.o_other), (r.mixed, r.o_mixed), (r.mixed_t, r.o_mixed_t), (r.lse, r.o_lse)
    ):
        save(src, dst)
    loads = [
        pltpu.make_async_copy(r.mid.at[m], r.w.at[m], r.local.at[len(flows) + m])
        for m in range(nmp)
    ]
    for copy in loads:
        copy.start()
    c_out = r.mixed.shape[2]
    hid = r.active.shape[2]
    w_out = [r.w.at[m, :, pl.ds(0, c_out)] for m in range(nmp)]
    w_up = [r.w.at[m, :, pl.ds(c_out, hid)] for m in range(nmp)]
    for copy in loads:
        copy.wait()

    def project(cols):
        acc = r.first[:, cols]
        for m in range(nmp):
            acc = acc + rdot(r.mixed[m], w_out[m][cols, :])
        r.second[:, cols] = acc

    by_tiles(model, COLS, project)

    def second_norm(here):
        xhat, _ = norm_parts(r.second[here])
        gain, bias = r.chan[KERNEL + 2][None], r.chan[KERNEL + 3][None]
        r.a2[here] = (xhat * gain + bias).astype(bf)

    by_tiles(rows, TILE, second_norm)
    save(r.second, r.o_second)
    save(r.a2, r.o_a2)
    turn()
    for m in range(nmp):

        def gelu_pair(v, cols):
            square = v * v
            t = jnp.tanh(0.7978845608028654 * v * (1.0 + 0.044715 * square))
            half = 0.5 + 0.5 * t
            r.active[m, :, cols] = (v * half).astype(bf)
            inner = 0.3989422804014327 * (1.0 + 0.134145 * square)
            r.slope[m, :, cols] = (half + v * (1.0 - t * t) * inner).astype(bf)

        def expand(i, _):
            cols = [pl.ds(pl.multiple_of((2 * i + n) * COLS, COLS), COLS) for n in range(2)]
            values = [dot(r.a2[...], w_up[m][:, c]) for c in cols]
            for v, c in zip(values, cols):
                gelu_pair(v, c)
            return 0

        lax.fori_loop(0, hid // COLS // 2, expand, 0)
        save(r.active.at[m], r.o_active.at[m])
        save(r.slope.at[m], r.o_slope.at[m])
        turn()
    turn()
    assert next(turns, None) is None
    for copy in saves:
        copy.wait()
    for f in flows:
        f.finish()
    for copy in crossings:
        copy.wait_send()


def fore_all(ndp, nmp, given):
    model = given.near_own.shape[0] * ndp
    width = given.near_own.shape[1]
    hid = given.down_own.shape[1]
    wide = HEADS * HEAD_DIM
    rows = given.features.shape[0] - 2 * PAD
    struct = jax.ShapeDtypeStruct
    dma = pltpu.SemaphoreType.DMA
    anywhere = pl.BlockSpec(memory_space=pl.ANY)
    outs = [
        struct((model, THIN), bf),
        struct((nmp, model, width), bf),
        struct((nmp, model, given.mid_own.shape[1]), bf),
        struct((nmp, model, hid), bf),
        struct((rows + 2 * PAD, model), f32),
        struct((rows, model), f32),
        struct((rows, model), f32),
        struct((nmp, rows, width), bf),
        struct((nmp, rows, width), bf),
        struct((nmp, rows, wide // nmp), bf),
        struct((wide, rows), f32),
        struct((HEADS, 1, rows), f32),
        struct((128, model), f32),
        struct((rows, model), f32),
        struct((rows, model), bf),
        struct((nmp, rows, hid), bf),
        struct((nmp, rows, hid), bf),
    ]
    outs = pl.pallas_call(
        functools.partial(fore_kernel, ndp, nmp),
        name="fore",
        out_shape=outs,
        in_specs=[SMEM] * 2 + [anywhere] * 4 + [VMEM],
        out_specs=[anywhere] * len(outs),
        scratch_shapes=[pltpu.VMEM(o.shape, o.dtype) for o in outs[:2] + outs[4:]]
        + [
            pltpu.VMEM((rows, model), bf),
            pltpu.VMEM((2 * rows, rows), f32),
            pltpu.VMEM((2 * rows, rows), f32),
            pltpu.VMEM((nmp, model, given.mid_own.shape[1]), bf),
            dma((7, ndp * nmp)),
            dma((7, ndp * nmp)),
            dma((7 + nmp + 13 + 2 * nmp,)),
            dma((nmp,)),
            dma((nmp,)),
            pltpu.SemaphoreType.REGULAR,
        ],
        compiler_params=pltpu.CompilerParams(
            collective_id=0, has_side_effects=True, vmem_limit_bytes=62 << 20
        ),
    )(*given)
    return ForeOut(*outs)


class MiddleIn(NamedTuple):
    second: Any
    a2: Any
    active: Any
    slope: Any
    chan: Any
    w_head: Any
    target: Any
    weights: Any
    mid: Any
    down: Any


class MiddleOut(NamedTuple):
    g_up: Any
    g_down: Any
    dsecond: Any
    dattn: Any
    dmixed: Any
    extra: Any
    g_head: Any
    loss: Any


class MiddleRefs(NamedTuple):
    second: Any
    a2: Any
    active: Any
    slope: Any
    chan: Any
    w_head: Any
    target: Any
    weights: Any
    mid: Any
    down: Any
    g_up: Any
    g_down: Any
    dsecond: Any
    dattn: Any
    dmixed: Any
    extra: Any
    g_head: Any
    loss: Any
    ffn: Any
    l_a2: Any
    dffn: Any
    l_dffn: Any
    l_active: Any
    l_dhid: Any
    dhid: Any
    a3: Any
    stage: Any
    w: Any
    w_down: Any
    c_send: Any
    c_recv: Any
    local: Any


def middle_kernel(ndp, nmp, *refs):
    r = MiddleRefs(*refs)
    wires = Wires(ndp, nmp)
    partner = wires.peer("c", 1)
    wires.greet([partner])
    rows, model = r.second.shape
    ny = nmp // 2
    theirs = list(range(1, nmp, 2))
    mine = list(range(0, nmp, 2))
    hid = r.active.shape[2]
    c_out = r.mid.shape[2] - hid
    w_out = [r.w.at[m, :, pl.ds(0, c_out)] for m in range(nmp)]
    w_up = [r.w.at[m, :, pl.ds(c_out, hid)] for m in range(nmp)]
    loads = [
        [
            pltpu.make_async_copy(src.at[m], dst.at[m], r.local.at[i * nmp + m])
            for m in range(nmp)
        ]
        for i, (src, dst) in enumerate(((r.down, r.w_down), (r.mid, r.w)))
    ]
    for group in loads:
        for m in theirs + mine:
            group[m].start()
    w_down = [r.w_down.at[m] for m in range(nmp)]
    crossings = []

    def cross(src, dst):
        i = len(crossings)
        copy = pltpu.make_async_remote_copy(
            src, dst, r.c_send.at[i], r.c_recv.at[i],
            device_id=partner, device_id_type=MESH,
        )
        copy.start()
        crossings.append(copy)
        return copy

    def row(i):
        return r.chan[KERNEL + i][None]

    got_a2 = cross(r.a2, r.l_a2)
    got_active = [cross(r.active.at[m], r.l_active.at[m // 2]) for m in theirs]
    for m in theirs + mine:
        loads[0][m].wait()

        def shrink(cols):
            part = rdot(r.active[m], w_down[m][cols, :])
            r.ffn[:, cols] = part if m == theirs[0] else r.ffn[:, cols] + part

        by_tiles(model, COLS, shrink)

    def third_norm(here):
        xhat, _ = norm_parts(r.second[here] + r.ffn[here])
        r.a3[here] = (xhat * row(4) + row(5)).astype(bf)

    by_tiles(rows, TILE, third_norm)
    error = dot(r.a3[...], r.w_head[...]) - r.target[...]
    weighted = r.weights[...] * error
    lanes = lax.broadcasted_iota(jnp.int32, (8, 128), 1)
    r.loss[...] = jnp.where(lanes == 0, jnp.sum(weighted * error), 0.0)
    dpred = (2.0 * weighted).astype(bf)
    r.g_head[...] = tdot(r.a3[...], dpred).astype(bf)
    r.dsecond[...] = rdot(dpred, r.w_head[...])

    zero = jnp.zeros((1, model), f32)

    def third_back(i, acc):
        here = pl.ds(pl.multiple_of(i * TILE, TILE), TILE)
        xhat, scale = norm_parts(r.second[here] + r.ffn[here])
        da = r.dsecond[here]
        dv = norm_turn(da, xhat, scale, row(4))
        r.ffn[here] = dv
        r.dffn[here] = dv.astype(bf)
        return acc[0] + fold(da * xhat), acc[1] + fold(da)

    dgain, dbias = lax.fori_loop(0, rows // TILE, third_back, (zero, zero))
    r.extra[...] = jnp.zeros_like(r.extra)
    r.extra[2:3] = dgain
    r.extra[3:4] = dbias
    got_dffn = cross(r.dffn, r.l_dffn)
    got_dhid = []
    stored = []

    def store(out, y, left, right, left_other, right_other):
        slot = len(stored) % 2
        if len(stored) >= 2:
            stored[-2].wait()

        def body(cols):
            part = tdot(left[:, cols], right[...]) + tdot(left_other[:, cols], right_other[...])
            r.stage[slot, cols] = part.astype(bf)

        by_tiles(model, COLS, body)
        copy = pltpu.make_async_copy(r.stage.at[slot], out.at[y], r.local.at[2 * nmp + len(stored)])
        copy.start()
        stored.append(copy)

    got_a2.wait_recv()
    for m in theirs + mine:
        loads[1][m].wait()

        def contract(cols):
            dact = dot(r.dffn[...], w_down[m][:, cols])
            r.dhid[m, :, cols] = (dact * r.slope[m, :, cols].astype(f32)).astype(bf)

        by_tiles(hid, COLS, contract)
        if m in theirs:
            got_dhid.append(cross(r.dhid.at[m], r.l_dhid.at[m // 2]))

        def gather_da2(cols):
            part = rdot(r.dhid[m], w_up[m][cols, :])
            r.dsecond[:, cols] = part if m == theirs[0] else r.dsecond[:, cols] + part

        by_tiles(model, COLS, gather_da2)
    got_dffn.wait_recv()
    for y in range(ny):
        got_active[y].wait_recv()
        store(r.g_down, y, r.dffn, r.active.at[2 * y], r.l_dffn, r.l_active.at[y])
    for y in range(ny):
        got_dhid[y].wait_recv()
        store(r.g_up, y, r.a2, r.dhid.at[2 * y], r.l_a2, r.l_dhid.at[y])

    def second_back(i, acc):
        here = pl.ds(pl.multiple_of(i * TILE, TILE), TILE)
        xhat, scale = norm_parts(r.second[here])
        da = r.dsecond[here]
        dsecond = r.ffn[here] + norm_turn(da, xhat, scale, row(2))
        r.dsecond[here] = dsecond
        r.dattn[here] = dsecond.astype(bf)
        return acc[0] + fold(da * xhat), acc[1] + fold(da)

    dgain, dbias = lax.fori_loop(0, rows // TILE, second_back, (zero, zero))
    r.extra[0:1] = dgain
    r.extra[1:2] = dbias
    for m in range(nmp):
        r.dmixed[m] = dot(r.dattn[...], w_out[m][...]).astype(bf)
    for copy in stored[-2:]:
        copy.wait()
    for copy in crossings:
        copy.wait_send()


def middle_all(ndp, nmp, given):
    rows, model = given.second.shape
    ny = nmp // 2
    hid = given.active.shape[2]
    c_out = given.mid.shape[2] - hid
    dma = pltpu.SemaphoreType.DMA
    anywhere = pl.BlockSpec(memory_space=pl.ANY)
    struct = jax.ShapeDtypeStruct
    outs = [
        struct((ny, model, hid), bf),
        struct((ny, model, hid), bf),
        struct((rows, model), f32),
        struct((rows, model), bf),
        struct((nmp, rows, c_out), bf),
        struct((8, model), f32),
        struct((model, 128), bf),
        struct((8, 128), f32),
    ]
    flat, tall = pltpu.VMEM((rows, model), f32), pltpu.VMEM((rows, model), bf)
    scratch = [
        flat,
        tall,
        tall,
        tall,
        pltpu.VMEM((ny, rows, hid), bf),
        pltpu.VMEM((ny, rows, hid), bf),
        pltpu.VMEM((nmp, rows, hid), bf),
        tall,
        pltpu.VMEM((2, model, hid), bf),
        pltpu.VMEM(given.mid.shape, bf),
        pltpu.VMEM(given.down.shape, bf),
        dma((8,)),
        dma((8,)),
        dma((2 * nmp + 2 * ny,)),
    ]
    outs = pl.pallas_call(
        functools.partial(middle_kernel, ndp, nmp),
        name="middle",
        out_shape=outs,
        in_specs=[VMEM] * 8 + [anywhere] * 2,
        out_specs=[anywhere] * 2 + [VMEM] * 6,
        scratch_shapes=scratch,
        compiler_params=pltpu.CompilerParams(
            collective_id=2, has_side_effects=True, vmem_limit_bytes=62 << 20
        ),
    )(*given)
    return MiddleOut(*outs)


def back_kernel(ndp, nmp, *refs):
    r = BackRefs(*refs)
    wires = Wires(ndp, nmp)
    sizes = wires.sizes
    rows, model = r.dattn.shape
    ny = sizes["y"]
    seq = wires.at["c"]
    nears = [wires.near(k) for k in range(1, nmp)]
    fars = [wires.far(k) for k in range(1, ndp)]
    wires.align(r.again)
    pending = []
    size = r.places[2]

    count = iter(range(16))

    def cross(src, dst):
        i = next(count)
        copy = Crossing(src, dst, r.c_send, r.c_recv, i, wires)
        copy.make().start()
        pending.append(copy)
        return copy

    def sent(copy):
        copy.wait_send()
        pending[:] = [c for c in pending if c is not copy]

    locals_used = []

    def fetch(src, dst):
        copy = pltpu.make_async_copy(src, dst, r.local.at[len(locals_used)])
        copy.start()
        locals_used.append(copy)
        return copy

    flows = []

    def wide_flow(term, out, box, half, order):
        height = term.shape[1] // ndp // 2
        n = len(flows)

        def source(k):
            start = (k["z"] * sizes["x"] + k["x"]) * 2 * height + half * height
            return term.at[k["y"], pl.ds(start, height)]

        def landing(k):
            return box.at[slot_number(sizes, k) // sizes["c"] - 1]

        here = out.at[pl.ds(half * height, height)]
        flows.append(
            Reduce(wires, order, source, landing, here, r.send.at[n], r.recv.at[n])
        )
        return flows[-1]

    def both(term, out, *boxes):
        orders = (("y", "x", "z"), ("x", "y", "z"))
        return [wide_flow(term, out, boxes[h], h, order) for h, order in enumerate(orders)]

    def thin_source(k):
        height = r.o_thin.shape[0]
        block = (k["z"] * sizes["x"] + k["x"]) * nmp + wires.owner_mp(k["y"], k["c"])
        return r.thin.at[pl.ds(pl.multiple_of(block * height, height), height)]

    down_flows = both(r.g_down, r.o_down, r.l_down0, r.l_down1)
    up_flows = both(r.g_up, r.o_up, r.l_up0, r.l_up1)
    out_flows = both(r.g_out, r.o_out, r.l_out0, r.l_out1)
    qkv_flows = both(r.g_qkv, r.o_qkv, r.l_qkv0, r.l_qkv1)
    n = len(flows)
    thin_flow = Reduce(
        wires, ("c", "y", "x", "z"), thin_source,
        lambda k: r.l_thin.at[slot_number(sizes, k) - 1],
        r.o_thin, r.send.at[n], r.recv.at[n],
    )
    flows.append(thin_flow)
    turns = iter(BACK_TURNS)
    slots = ndp * nmp

    def turn():
        for code in next(turns):
            flow = flows[code // (2 * slots)]
            if code // slots % 2:
                flow.depart(code % slots)
            else:
                flow.arrive(code % slots)

    mine = [m for m in range(nmp) if m % 2 == 0]
    theirs = [m for m in range(nmp) if m % 2]
    for f in down_flows + up_flows:
        f.keep()
    turn()
    got_dattn = cross((r.dattn,), (r.l_dattn,))
    got_mixed = [cross((r.mixed, m), (r.l_mixed, m // 2)) for m in theirs]

    got_other = {}
    loads = {m: fetch(r.w_qkv.at[m], r.w_buf.at[m]) for m in range(2)}

    def attention(packed, other, mixed_t, dmixed, dist):
        copies = [
            fetch(src, ref)
            for src, ref in (
                (r.packed, packed), (r.other, other), (r.mixed_t, mixed_t), (r.dmixed, dmixed)
            )
        ]
        distances(dist, r.places[0], r.places[1], size)
        turn()
        got_dattn.wait_recv()
        for copy in got_mixed:
            copy.wait_recv()
        for y in range(ny):
            g = tdot(r.dattn[...], r.mixed[2 * y])
            r.g_out[y] = (g + tdot(r.l_dattn[...], r.l_mixed[y])).astype(bf)
        for f in out_flows:
            f.keep()
        for copy in copies:
            copy.wait()
        leaving = []
        for m in theirs + mine:
            slot = len(leaving) % 2
            if len(leaving) >= 2:
                sent(leaving[-2])
            for _ in attend_back(
                packed, other, dist, r.slopes, mixed_t, r.lse, dmixed,
                r.down, r.dother.at[slot], m,
            ):
                turn()
            twin = m + 1 - 2 * (m % 2)
            leaving.append(cross((r.dother, slot), (r.l_other, twin)))
            got_other[twin] = leaving[-1]

    chunks, _, width = r.packed.shape
    pl.run_scoped(
        attention,
        pltpu.VMEM(r.packed.shape, bf),
        pltpu.VMEM(r.other.shape, bf),
        pltpu.VMEM(r.mixed_t.shape, f32),
        pltpu.VMEM(r.dmixed.shape, bf),
        pltpu.VMEM((2 * rows, rows), f32),
    )

    lane = lax.broadcasted_iota(jnp.int32, (TILE, width), 1)
    is_query = lax.rem(lane, 3 * HEAD_DIM) < HEAD_DIM

    def front(first, conv, back, hm, features, dconv, gtaps):
        copies = [
            fetch(src, ref)
            for src, ref in (
                (r.first, first), (r.conv, conv), (r.dsecond, back), (r.hm, hm), (r.features, features)
            )
        ]
        copies[0].wait()
        gain = r.chan[KERNEL][None]
        bias = r.chan[KERNEL + 1][None]

        def act(i, _):
            here = pl.ds(pl.multiple_of(i * TILE, TILE), TILE)
            xhat, _ = norm_parts(first[here])
            r.a1[here] = (xhat * gain + bias).astype(bf)
            return 0

        lax.fori_loop(0, rows // TILE, act, 0)
        got_a1 = cross((r.a1,), (r.l_a1,))
        turn()

        def combine(m):
            got_other[m].wait_recv()

            def body(i, _):
                here = pl.ds(pl.multiple_of(i * TILE, TILE), TILE)
                own = r.down[m, here].astype(f32)
                more = own + r.l_other[m, here].astype(f32)
                r.down[m, here] = jnp.where(is_query, own, more).astype(bf)
                return 0

            lax.fori_loop(0, rows // TILE, body, 0)

        got_pack = []
        for m in theirs:
            combine(m)
            got_pack.append(cross((r.down, m), (r.l_dpack, m // 2)))
        for m in mine:
            combine(m)
        turn()
        got_a1.wait_recv()
        for y in range(ny):
            got_pack[y].wait_recv()
            g = tdot(r.a1[...], r.down[2 * y])
            r.g_qkv[y] = (g + tdot(r.l_a1[...], r.l_dpack[y])).astype(bf)
            turn()
        for f in qkv_flows:
            f.keep()
        inner = pl.ds(PAD, rows)
        for m in range(chunks):
            loads[m].wait()
            part = rdot(r.down[m], r.w_buf[m % 2])
            dconv[inner] = part if m == 0 else dconv[inner] + part
            if m + 2 < chunks:
                loads[m + 2] = fetch(r.w_qkv.at[m + 2], r.w_buf.at[m % 2])
            turn()
        for copy in copies[1:]:
            copy.wait()
        r.rows_buf[...] = jnp.zeros_like(r.rows_buf)
        r.rows_buf[KERNEL + 2 : KERNEL + 6] = r.extra[0:4]

        def norm(i, sums_in):
            here = pl.ds(pl.multiple_of(i * TILE, TILE), TILE)
            xhat, scale = norm_parts(first[here])
            shifted = pl.ds(pl.multiple_of(i * TILE + PAD, PAD), TILE)
            da = dconv[shifted]
            dx = da * gain
            dv = scale * (
                dx
                - jnp.mean(dx, axis=-1, keepdims=True)
                - xhat * jnp.mean(dx * xhat, axis=-1, keepdims=True)
            )
            dfirst = back[here] + dv
            first[here] = dfirst
            dc = dfirst * gelu_slope(conv[here])
            dconv[shifted] = dc
            return tuple(a + fold(b) for a, b in zip(sums_in, (da * xhat, da, dc)))

        zero = jnp.zeros((1, model), f32)
        dgain, dbias, dcsum = lax.fori_loop(0, rows // TILE, norm, (zero, zero, zero))
        r.rows_buf[KERNEL : KERNEL + 1] = dgain
        r.rows_buf[KERNEL + 1 : KERNEL + 2] = dbias
        r.rows_buf[KERNEL + 7 : KERNEL + 8] = dcsum
        r.edge[0] = dconv[PAD : 2 * PAD]
        r.edge[1] = dconv[rows : rows + PAD]
        got_edge = cross((r.edge,), (r.halo,))
        turn()
        got_edge.wait_recv()
        dconv[0:PAD] = jnp.where(seq == 0, 0.0, r.halo[1])
        dconv[rows + PAD :] = jnp.where(seq == 0, r.halo[0], 0.0)
        gtaps[...] = jnp.zeros_like(gtaps)
        for c in range(0, model, 128):
            convolve_back(dconv, hm, r.chan, back, gtaps, c)
            turn()

        def finish(i, acc):
            here = pl.ds(pl.multiple_of(i * TILE, TILE), TILE)
            place = r.places[0] + i * TILE + lax.broadcasted_iota(jnp.int32, (TILE, 1), 0)
            dstart = first[here] + jnp.where(place < size, back[here], 0.0)
            r.a1[here] = dstart.astype(bf)
            return acc + fold(dstart)

        sent(got_a1)
        r.rows_buf[KERNEL + 6 : KERNEL + 7] = lax.fori_loop(0, rows // TILE, finish, zero)
        for k in range(KERNEL):
            r.rows_buf[k : k + 1] = fold(gtaps[8 * k : 8 * k + 8])
        r.thin[:, :THIN_CHAN] = tdot(r.a1[...], features[...]).astype(bf)
        for i in range(0, model, 128):
            r.thin[i : i + 128, THIN_CHAN:THIN_HEAD] = r.rows_buf[:, i : i + 128].T.astype(bf)
        r.thin[:, THIN_HEAD:] = r.g_head[...]

    pl.run_scoped(
        front,
        pltpu.VMEM((rows, model), f32),
        pltpu.VMEM((rows, model), f32),
        pltpu.VMEM((rows, model), f32),
        pltpu.VMEM((rows + 2 * PAD, model), f32),
        pltpu.VMEM(r.features.shape, bf),
        pltpu.VMEM((rows + 2 * PAD, model), f32),
        pltpu.VMEM((8 * KERNEL, model), f32),
    )
    thin_flow.keep()
    turn()
    assert next(turns, None) is None
    for f in flows:
        f.finish()
    for copy in pending:
        copy.wait_send()

    squares = None
    for out in (r.o_thin, r.o_up, r.o_down, r.o_qkv, r.o_out):
        part = total(out)
        squares = part if squares is None else squares + part
    lanes = lax.broadcasted_iota(jnp.int32, (8, 128), 1)
    block = jnp.where(lanes == 1, squares, r.loss[...])
    parts = r.parts
    for peers, sends, recvs, lower in (
        (nears, r.near_send, r.near_recv, 0),
        (fars, r.far_send, r.far_recv, nmp),
    ):
        parts[lower] = block
        copies = []
        for i, p in enumerate(peers):
            copy = pltpu.make_async_remote_copy(
                parts.at[lower], parts.at[lower + 1 + i], sends.at[i], recvs.at[i],
                device_id=p, device_id_type=MESH,
            )
            copy.start()
            copies.append(copy)
        for copy in copies:
            copy.wait()
        for i in range(len(peers)):
            block = block + parts[lower + 1 + i]
    r.sums[...] = block


def back_all(ndp, nmp, given):
    rows, model = given.dattn.shape
    ny = nmp // 2
    width = given.packed.shape[2]
    c_out = given.mixed.shape[2]
    c_up = given.g_up.shape[2]
    height = model // ndp
    pairs = (ndp * ny - 1, height // 2)
    dma = pltpu.SemaphoreType.DMA
    wide = (c_up, given.g_down.shape[2], width, c_out)
    outs = [jax.ShapeDtypeStruct((height // nmp, THIN), f32)]
    outs += [jax.ShapeDtypeStruct((height, n), f32) for n in wide]
    outs += [jax.ShapeDtypeStruct((8, 128), f32)]
    scratch = [
        pltpu.VMEM((ny, model, width), bf),
        pltpu.VMEM((ny, model, c_out), bf),
        pltpu.VMEM((model, THIN), bf),
    ]
    for n in wide:
        scratch += [pltpu.VMEM((*pairs, n), bf)] * 2
    scratch += [
        pltpu.VMEM((ndp * nmp - 1, height // nmp, THIN), bf),
        pltpu.VMEM((nmp, rows, width), bf),
        pltpu.VMEM((2, rows, width), bf),
        pltpu.VMEM((nmp, rows, width), bf),
        pltpu.VMEM((rows, model), bf),
        pltpu.VMEM((rows, model), bf),
        pltpu.VMEM((rows, model), bf),
        pltpu.VMEM((ny, rows, c_out), bf),
        pltpu.VMEM((ny, rows, width), bf),
        pltpu.VMEM((2, PAD, model), f32),
        pltpu.VMEM((2, PAD, model), f32),
        pltpu.VMEM((nmp + ndp, 8, 128), f32),
        pltpu.VMEM((2, model, width), bf),
        pltpu.VMEM((128, model), f32),
        dma((9, ndp * nmp)),
        dma((9, ndp * nmp)),
        dma((16,)),
        dma((16,)),
        dma((16,)),
        dma((nmp - 1,)),
        dma((nmp - 1,)),
        dma((ndp - 1,)),
        dma((ndp - 1,)),
        pltpu.SemaphoreType.REGULAR,
    ]
    anywhere = pl.BlockSpec(memory_space=pl.ANY)
    specs = [SMEM] * 2 + [VMEM] * 8 + [anywhere] * 3 + [VMEM] * 1 + [anywhere] * 7
    return pl.pallas_call(
        functools.partial(back_kernel, ndp, nmp),
        name="back",
        out_shape=outs,
        in_specs=specs,
        out_specs=[VMEM] * len(outs),
        scratch_shapes=scratch,
        compiler_params=pltpu.CompilerParams(
            collective_id=1, has_side_effects=True, vmem_limit_bytes=62 << 20
        ),
    )(*given)


def shards(
    clean_mel,
    noise_mel,
    lengths,
    span_start,
    span_end,
    phone_ids,
    flow_steps,
    in_table,
    channel_rows,
    attn_qkv,
    attn_out,
    ffn_up,
    ffn_down,
    mel_head,
    table_first,
    channel_first,
    qkv_first,
    merge_first,
    upward_first,
    downward_first,
    head_first,
    table_second,
    channel_second,
    qkv_second,
    merge_second,
    upward_second,
    downward_second,
    head_second,
):
    micro, units, length, mel = clean_mel.shape
    nmp = lax.axis_size("mp")
    seqs = nmp // micro
    rows = length // seqs
    mp = lax.axis_index("mp")
    batch = mp // seqs
    seq = mp % seqs
    base = seq * rows
    width = in_table.shape[0]
    nch = channel_rows.shape[0]

    c_qkv = attn_qkv.shape[1]
    c_out = attn_out.shape[0]
    c_up = ffn_up.shape[1]

    ndp = lax.axis_size("dp")
    spans = jnp.sum(span_end - span_start, axis=1)
    digits = jnp.stack([spans // 32, spans % 32], axis=1).reshape(1, -1)
    digits = jnp.broadcast_to(digits, (mel_head.shape[0], 2 * micro))

    def columns(x, size):
        return jnp.pad(x.astype(bf), ((0, 0), (0, size - x.shape[1])))

    thin = jnp.concatenate(
        [
            columns(in_table.T, THIN_CHAN),
            columns(channel_rows.T, THIN_HEAD - THIN_CHAN),
            columns(jnp.concatenate([mel_head, digits.astype(f32)], axis=1), THIN - THIN_HEAD),
        ],
        axis=1,
    )
    mid = jnp.concatenate([attn_out.T, ffn_up], axis=1).astype(bf)
    own = (ndp, nmp, seqs) == (8, 4, 2)
    def mine(x):
        return lax.dynamic_index_in_dim(x, batch, 0, keepdims=False)[0]

    def widen(x):
        x = jnp.pad(mine(x), [(PAD, PAD)] + [(0, 0)] * (x.ndim - 3))
        return lax.dynamic_slice_in_dim(x, base, rows + 2 * PAD, 0)

    size = mine(lengths)
    first_frame = mine(span_start)
    last_frame = mine(span_end)
    place = base - PAD + jnp.arange(rows + 2 * PAD)
    valid_ext = ((place >= 0) & (place < size)).astype(f32)[:, None]
    masked_ext = ((place >= first_frame) & (place < last_frame)).astype(f32)[:, None]
    inside = slice(PAD, PAD + rows)
    valid = valid_ext[inside]
    masked = masked_ext[inside]
    tau = mine(flow_steps).astype(f32) / TSTEPS
    clean = widen(clean_mel).astype(f32)
    noise = widen(noise_mel).astype(f32)
    noisy = (1.0 - (1.0 - SIGMA) * tau) * noise + tau * clean
    context = clean * (valid_ext * (1.0 - masked_ext))
    target = (clean - (1.0 - SIGMA) * noise)[inside]
    onehot = (widen(phone_ids)[:, None] == jnp.arange(PHONES)).astype(bf)
    features_ext = jnp.concatenate([noisy.astype(bf), context.astype(bf), onehot], axis=-1)
    features = features_ext[inside]

    wires = Wires(ndp, nmp)
    owners = [wires.owner_mp(m // 2, m % 2) if own else m for m in range(nmp)]
    owners = jnp.stack(owners) if own else jnp.arange(nmp)
    heads = (owners[:, None] * (HEADS // nmp) + jnp.arange(HEADS // nmp)).reshape(-1)
    slopes = jnp.exp2(-8.0 * (heads + 1).astype(f32) / HEADS)
    if own:
        places = jnp.stack([base, (1 - seq) * rows, size]).astype(jnp.int32)
        fore = fore_all(
            ndp,
            nmp,
            ForeIn(
                places=places,
                slopes=slopes,
                thin_own=thin,
                near_own=attn_qkv.astype(bf),
                mid_own=mid,
                down_own=ffn_down.T.astype(bf),
                features=columns(features_ext, THIN_CHAN),
            ),
        )
        thin = fore.thin
    else:
        thin = lax.all_gather(thin, ("dp", "mp"), axis=0, tiled=True)
        w_qkv = lax.all_gather(attn_qkv.astype(bf), ("mp", "dp"), axis=0, tiled=True)
        w_qkv = w_qkv.reshape(nmp, -1, c_qkv)
        rest = jnp.concatenate([mid, ffn_down.T.astype(bf)], axis=1)
        rest = lax.all_gather(rest, ("mp", "dp"), axis=0, tiled=True)
        rest = rest.reshape(nmp, -1, rest.shape[1])
        owners = jnp.arange(nmp)
    model = thin.shape[0]
    digits = thin[:, THIN_HEAD + mel : THIN_HEAD + mel + 2 * micro]
    digits = jnp.sum(digits.reshape(ndp, -1, 2 * micro)[:, 0].astype(f32), axis=0)
    count = lax.dynamic_slice_in_dim(digits, 2 * batch, 2, 0)
    count = count[0] * 32.0 + count[1]

    if own:
        lanes = jnp.arange(128) < mel
        middle = middle_all(
            ndp,
            nmp,
            MiddleIn(
                second=fore.second,
                a2=fore.a2,
                active=fore.active,
                slope=fore.slope,
                chan=fore.chan,
                w_head=jnp.where(lanes, thin[:, THIN_HEAD:], 0),
                target=jnp.pad(target, ((0, 0), (0, 128 - mel))),
                weights=jnp.broadcast_to(masked / count, (rows, 128)),
                mid=fore.mid,
                down=fore.down,
            ),
        )
        given = BackIn(
            places=places,
            slopes=slopes,
            loss=middle.loss,
            g_up=middle.g_up,
            g_down=middle.g_down,
            dattn=middle.dattn,
            mixed=fore.mixed,
            extra=middle.extra,
            g_head=middle.g_head,
            chan=fore.chan,
            packed=fore.packed,
            other=fore.other,
            mixed_t=fore.mixed_t,
            lse=fore.lse,
            dmixed=middle.dmixed,
            w_qkv=fore.near,
            first=fore.first,
            conv=fore.conv,
            dsecond=middle.dsecond,
            hm=fore.hm,
            features=columns(features, THIN_CHAN),
        )
        g_thin, g_up, g_down, g_qkv, g_out, sums = back_all(ndp, nmp, given)
    else:
        w_out = rest[:, :, :c_out]
        w_up = rest[:, :, c_out : c_out + c_up]
        w_down = rest[:, :, c_out + c_up :]
        w_in = thin[:, :width]
        channel = thin[:, THIN_CHAN : THIN_CHAN + nch].T.astype(f32)
        w_head = thin[:, THIN_HEAD : THIN_HEAD + mel]
        taps = channel[:KERNEL]
        vecs = channel[KERNEL:]

        start_ext = rdot(features_ext, w_in) + vecs[6]
        hm = start_ext * valid_ext
        conv = jnp.zeros((rows, model), f32) + vecs[7]
        for k in range(KERNEL):
            conv = conv + taps[k] * hm[k + 1 : k + 1 + rows]
        first = start_ext[inside] + gelu(conv)
        x_one, r_one = norm_parts(first)
        act_one = (x_one * vecs[0] + vecs[1]).astype(bf)

        groups = [[g * seqs + s for s in range(seqs)] for g in range(micro)]

        def shift(x, i):
            pairs = [(g[(s + i) % seqs], g[s]) for g in groups for s in range(seqs)]
            return lax.ppermute(x, "mp", pairs)

        def unshift(x, i):
            pairs = [(g[s], g[(s + i) % seqs]) for g in groups for s in range(seqs)]
            return lax.ppermute(x, "mp", pairs)

        packed = jnp.einsum("rd,mdc->rmc", act_one, w_qkv, preferred_element_type=f32).astype(bf)
        packed = packed.reshape(rows, HEADS, 3, HEAD_DIM)
        query, key, value = packed[:, :, 0], packed[:, :, 1], packed[:, :, 2]
        both = jnp.stack([key, value])
        both = jnp.concatenate([both] + [shift(both, i) for i in range(1, seqs)], axis=1)
        keys, values = both[0], both[1]
        blocks = (seq + jnp.arange(seqs)) % seqs
        key_place = (blocks[:, None] * rows + jnp.arange(rows)).reshape(-1)
        query_place = base + jnp.arange(rows)
        distance = jnp.abs(query_place[:, None] - key_place[None, :]).astype(f32)
        raw = jnp.einsum("qhd,khd->hqk", query, keys, preferred_element_type=f32)
        score = raw * SCALE - slopes[:, None, None] * distance
        score = jnp.where((key_place < size)[None, None, :], score, -1000000000.0)
        top = jnp.max(score, axis=-1, keepdims=True)
        prob = jnp.exp(score - top)
        prob = prob / jnp.sum(prob, axis=-1, keepdims=True)
        prob_low = prob.astype(bf)
        mixed = jnp.einsum("hqk,khd->qhd", prob_low, values, preferred_element_type=f32)
        mixed = mixed.astype(bf).reshape(rows, nmp, c_out)
        mixed = [mixed[:, m] for m in range(nmp)]
        attn = jnp.zeros((rows, model), f32)
        for m in range(nmp):
            attn = attn + rdot(mixed[m], w_out[m])
        second = first + attn

        x_two, r_two = norm_parts(second)
        act_two = (x_two * vecs[2] + vecs[3]).astype(bf)
        ffn = jnp.zeros((rows, model), f32)
        hidden = []
        active = []
        for m in range(nmp):
            hidden.append(dot(act_two, w_up[m]))
            active.append(gelu(hidden[m]).astype(bf))
            ffn = ffn + rdot(active[m], w_down[m])
        third = second + ffn

        x_three, r_three = norm_parts(third)
        act_three = (x_three * vecs[4] + vecs[5]).astype(bf)
        error = dot(act_three, w_head) - target
        weight_rows = masked / count
        loss_local = jnp.sum(weight_rows * error * error)
        dpred = (2.0 * weight_rows * error).astype(bf)
        g_head = tdot(act_three, dpred)
        dthird, dg3, db3 = norm_back(rdot(dpred, w_head), x_three, r_three, vecs[4])

        dffn = dthird.astype(bf)
        da2 = jnp.zeros((rows, model), f32)
        dhids = []
        for m in range(nmp):
            dhid = gelu_back(hidden[m], dot(dffn, w_down[m])).astype(bf)
            dhids.append(dhid)
            da2 = da2 + rdot(dhid, w_up[m])
        dnorm, dg2, db2 = norm_back(da2, x_two, r_two, vecs[2])
        dsecond = dthird + dnorm

        dattn = dsecond.astype(bf)
        g_out = [tdot(dattn, mixed[m]).astype(bf) for m in range(nmp)]
        dmixed = [dot(dattn, w_out[m]).astype(bf) for m in range(nmp)]
        dmixed = jnp.stack(dmixed, axis=1).reshape(rows, HEADS, HEAD_DIM)
        dvalues = jnp.einsum("hqk,qhd->khd", prob_low, dmixed, preferred_element_type=f32)
        dprob = jnp.einsum("qhd,khd->hqk", dmixed, values, preferred_element_type=f32)
        dscore = prob * (dprob - jnp.sum(prob * dprob, axis=-1, keepdims=True))
        draw = (dscore * SCALE).astype(bf)
        dquery = jnp.einsum("hqk,khd->qhd", draw, keys, preferred_element_type=f32)
        dkeys = jnp.einsum("hqk,qhd->khd", draw, query, preferred_element_type=f32)
        dboth = jnp.stack([dkeys, dvalues])
        parts = [dboth[:, i * rows : (i + 1) * rows] for i in range(seqs)]
        dboth = parts[0]
        for i in range(1, seqs):
            dboth = dboth + unshift(parts[i].astype(bf), i).astype(f32)
        dpacked = jnp.stack([dquery, dboth[0], dboth[1]], axis=2).astype(bf)
        dpacked = dpacked.reshape(rows, nmp, c_qkv)
        dpacked = [dpacked[:, m] for m in range(nmp)]
        g_qkv = [tdot(act_one, dpacked[m]).astype(bf) for m in range(nmp)]
        da1 = jnp.zeros((rows, model), f32)
        for m in range(nmp):
            da1 = da1 + rdot(dpacked[m], w_qkv[m])

        dnorm, dg1, db1 = norm_back(da1, x_one, r_one, vecs[0])
        dfirst = dsecond + dnorm
        dconv = gelu_back(conv, dfirst)
        right = lax.ppermute(
            dconv[:PAD], "mp", [(g[s + 1], g[s]) for g in groups for s in range(seqs - 1)]
        )
        left = lax.ppermute(
            dconv[rows - PAD :], "mp", [(g[s], g[s + 1]) for g in groups for s in range(seqs - 1)]
        )
        dconv_ext = jnp.concatenate([left, dconv, right], axis=0)
        back = jnp.zeros((rows, model), f32)
        g_taps = []
        for k in range(KERNEL):
            back = back + taps[k] * dconv_ext[2 * PAD - 1 - k : 2 * PAD - 1 - k + rows]
            g_taps.append(jnp.sum(dconv * hm[k + 1 : k + 1 + rows], axis=0))
        dstart = dfirst + valid * back
        g_in = tdot(dstart.astype(bf), features)
        g_rows = g_taps + [dg1, db1, dg2, db2, dg3, db3, jnp.sum(dstart, axis=0), jnp.sum(dconv, axis=0)]
        g_chan = jnp.stack(g_rows, axis=1)

        g_thin = jnp.concatenate(
            [
                columns(g_in, THIN_CHAN),
                columns(g_chan, THIN_HEAD - THIN_CHAN),
                columns(g_head, THIN - THIN_HEAD),
            ],
            axis=1,
        )
        g_up = [tdot(act_two, dhids[m]).astype(bf) for m in range(nmp)]
        g_down = [tdot(dffn, active[m]).astype(bf) for m in range(nmp)]
        terms = [g_thin, jnp.stack(g_up), jnp.stack(g_down), jnp.stack(g_qkv), jnp.stack(g_out)]
        g_thin = lax.psum_scatter(g_thin, ("dp", "mp"), scatter_dimension=0, tiled=True)
        sums = [g_thin.astype(f32)] + [
            lax.psum_scatter(
                t.reshape(-1, t.shape[2]), ("mp", "dp"), scatter_dimension=0, tiled=True
            ).astype(f32)
            for t in terms[1:]
        ]
        g_thin, g_up, g_down, g_qkv, g_out = sums
        squares = sum(jnp.sum(g * g) for g in sums)
        sums = lax.psum(jnp.stack([loss_local, squares])[None], ("dp", "mp"))
    sums = sums[0]
    loss = sums[0]
    grad_norm = jnp.sqrt(sums[1])
    factor = CLIP_AT / jnp.maximum(grad_norm, CLIP_AT)

    tw, tm, tv = adam_update(in_table, table_first, table_second, g_thin[:, :width].T, factor)
    cw, cm, cv = adam_update(
        channel_rows, channel_first, channel_second, g_thin[:, THIN_CHAN : THIN_CHAN + nch].T, factor
    )
    hw, hm_, hv = adam_update(mel_head, head_first, head_second, g_thin[:, THIN_HEAD : THIN_HEAD + mel], factor)
    qw, qm, qv = adam_update(attn_qkv, qkv_first, qkv_second, g_qkv, factor)
    ow, om, ov = adam_update(attn_out, merge_first, merge_second, g_out.T, factor)
    uw, um, uv = adam_update(ffn_up, upward_first, upward_second, g_up, factor)
    dw, dm, dv = adam_update(ffn_down, downward_first, downward_second, g_down.T, factor)
    return (
        loss, grad_norm,
        tw, tm, tv, cw, cm, cv, qw, qm, qv, ow, om, ov, uw, um, uv, dw, dm, dv, hw, hm_, hv,
    )


def solution(mesh):
    wide = P(None, ("dp", "mp"))
    tall = P(("dp", "mp"), None)
    down = P("dp", "mp")
    flat = P("mp", "dp")
    weights = (wide, wide, down, flat, down, flat, tall)
    pair = P(None, "dp")
    data = (P(None, "dp", None, None), P(None, "dp", None, None), pair, pair, pair)
    data = data + (P(None, "dp", None), pair)
    return jax.shard_map(
        shards,
        mesh=mesh,
        in_specs=data + weights * 3,
        out_specs=(P(), P()) + tuple(w for w in weights for _ in range(3)),
        check_vma=False,
    )
```

time: 1280 us -> 408 us (0.32)
  waiting for transfers between devices: 612 us -> 0 us
  Pallas kernels: 0 us -> 354 us
  matrix products: 241 us -> 0 us
  other arithmetic: 148 us -> 20.4 us
  local copies, waits for them, and re-layouts: 134 us -> 21.6 us
  blocking collectives: 104 us -> 0 us
  between operations: 22.2 us -> 6.05 us
    reduce_scatter x3 -> x0, waiting for transfers between devices: 603 us -> none  [the longest x1 358 us: shards(): lax.psum_scatter(g_rest, ('mp', 'dp'), scatter_dimension=0, tiled=True)]
    pallas_call x0 -> x3, Pallas kernels: none -> 354 us  [the longest x1 157 us: back_all(): pl.pallas_call(functools.partial(back_kernel, ndp, nmp), name='back', out...]
    dot_general x56 -> x0, matrix products: 241 us -> none  [the longest x1 54.8 us: shards(): dkeys = jnp.einsum('hqk,qhd->khd', draw, query, preferred_element_type=f32)]
    another operation x44 -> x2, local copies, waits for them, and re-layouts: 58.8 us -> 0.19 us  [the longest x39 23.2 us: shards(): g_chan = jnp.stack(g_rows, axis=1)]
    psum x2 -> x0, blocking collectives: 56.1 us -> none  [the longest x1 38.6 us: shards(): sums = lax.psum(jnp.stack([loss_local, squares]), ('dp', 'mp'))]
    reduce_sum x11 -> x1, other arithmetic: 48.3 us -> 0.03 us  [shards(): jnp.sum(digits.reshape(ndp, -1, 2 * micro)[:, 0].astype(f32), axis=0)]
    all_gather x1 -> x0, blocking collectives: 47.6 us -> none  [shards(): thin = lax.all_gather(thin, ('dp', 'mp'), axis=0, tiled=True)]
    sub x1, other arithmetic: 40 us -> 0.04 us  [shards(): target = (clean - (1.0 - SIGMA) * noise)[inside]]
  transfers between devices with their start and end apart: 9 -> 0, of which waited for: 4 -> 0; matrix products, arithmetic and copies ran while one was open for 22% -> 0% of each run, Pallas kernels for 0% -> 0%
where the time goes in v3:
time: 408 us; the launch traced here: 402 us
  Pallas kernels  354 us (87%)
  local copies, waits for them, and re-layouts  21.6 us (5%)
  other arithmetic  20.4 us (5%)
  between operations  6.05 us (1%)
    pallas_call x1, Pallas kernels, back_all(): pl.pallas_call(functools.partial(back_kernel, ndp, nmp), name='back', out...  157 us
    pallas_call x1, Pallas kernels, fore_all(): pl.pallas_call(functools.partial(fore_kernel, ndp, nmp), name='fore', out...  143 us
    pallas_call x1, Pallas kernels, middle_all(): pl.pallas_call(functools.partial(middle_kernel, ndp, nmp), name='middle',...  53.2 us
    unnamed x68, local copies, waits for them, and re-layouts  11.7 us
    sub x7, other arithmetic, adam_update(): weight - RATE * (first_hat / (jnp.sqrt(second_hat) + EPSILON) + DECAY * w...  9.17 us

profile of v3, /device:TPU:0, one launch (start us, length us, event | category | flops | bytes accessed | tf_op | source)
XLA Modules:
  0.0 401.6 jit_solution(12705625925525095687)
XLA Ops:
  0.8 1.1 constant_dynamic-slice_fusion.3
  2.2 1.3 constant_dynamic-slice_fusion.6
  3.5 1.3 constant_dynamic-slice_fusion.1
  4.8 1.9 subtract_select_fusion
  8.7 0.8 pad.41.refs_6_
  10.3 1.2 pad_add_fusion.refs_0_
  12.7 0.7 convert_bitcast_fusion.refs_5_
  14.3 0.7 pad_maximum_fusion.1.refs_4_
  15.7 143.4 %fore.1 = (bf16[1024,640]{1,0:T(8,128)(2,1)}, bf16[4,1024,768]{2,1,0:T(8,128)(2,1)}, bf16[4,1024,1280]{2,1,0:T(8,128)(2,1)}, bf16[4,1024,1024]{2,1,0:T(8,128)(2,...) custom-call(s32[3]{0:T(128)} %pad_add_fusion.refs_0_, ...), custom_call_target="tpu_custom_call" | custom-call | tf_op jit(solution)/shard_map/fore/pallas_call | solution.py:963
  159.1 1.1 slice.48
  162.2 1.3 fusion.27
  163.5 0.8 broadcast_in_dim.15.refs_7_
  164.4 1.7 slice_select_fusion.refs_5_
  166.9 53.2 %middle.1 = (bf16[2,1024,1024]{2,1,0:T(8,128)(2,1)}, bf16[2,1024,1024]{2,1,0:T(8,128)(2,1)}, f32[512,1024]{1,0:T(8,128)}, bf16[512,1024]{1,0:T(8,128)(2,1)}, bf1...) custom-call(f32[512,1024]{1,0:T(8,128)} %get-tuple-element.54.refs_0_, ...), custom_call_target="tpu_custom_call" | custom-call | tf_op jit(solution)/shard_map/middle/pallas_call | solution.py:1224
  220.1 0.8 pad.43.refs_20_
  220.9 157.0 %back.1 = (f32[32,640]{1,0:T(8,128)}, f32[128,1024]{1,0:T(8,128)}, f32[128,1024]{1,0:T(8,128)}, f32[128,768]{1,0:T(8,128)}, f32[128,256]{1,0:T(8,128)}, /*index=5*/f32[8,128]{1,0:T(8,128)}) custom-call(s32[3]{0:T(128)} %pad_add_fusion.refs_0_, f32[16]{0:T(128)} %reshape.139.refs_1_, f32[8,128]{1,0:T(8,128)} %get-tuple-element.62.refs_2_, ...), custom_call_target="tpu_custom_call" | custom-call | tf_op jit(solution)/shard_map/back/pallas_call | solution.py:1583
  377.9 1.3 fusion.40
  380.0 1.4 multiply_subtract_fusion.5
  381.4 1.2 copy.60
  382.6 2.0 copy.61
  384.7 1.7 multiply_subtract_fusion
  386.3 1.0 copy.67
  387.3 1.0 copy.68
  388.3 1.0 copy.69
  389.4 2.6 multiply_subtract_fusion.1
  392.0 1.1 copy.56
  393.1 1.0 copy.57
  394.1 1.0 multiply_subtract_fusion.3
  395.2 0.8 copy.64
  395.9 0.8 copy.65
  396.7 0.8 copy.66
  397.5 1.2 multiply_subtract_fusion.2
  (94 shorter events, 7.4 us)
Async XLA Ops:
  0.7 7.5 %copy-start = (s32[2,1,1024]{2,1,0:T(1,128)S(1)}, s32[2,1,1024]{2,1,0:T(1,128)}, u32[]{:S(2)}) copy-start(s32[2,1,1024]{2,1,0:T(1,128)} %param.33) | copy-start | bytes 24580
  0.7 10.8 %copy-start.27 = (s32[2,1]{0,1:T(1,128)S(1)}, s32[2,1]{0,1:T(1,128)}, u32[]{:S(2)}) copy-start(s32[2,1]{0,1:T(1,128)} %param.31) | copy-start | bytes 28
  0.7 10.8 %copy-start.26 = (s32[2,1]{0,1:T(1,128)S(1)}, s32[2,1]{0,1:T(1,128)}, u32[]{:S(2)}) copy-start(s32[2,1]{0,1:T(1,128)} %param.32) | copy-start | bytes 28
  0.7 11.1 %copy-start.17 = (f32[32,80]{1,0:T(8,128)S(1)}, f32[32,80]{1,0:T(8,128)}, u32[]{:S(2)}) copy-start(f32[32,80]{1,0:T(8,128)} %param.41) | copy-start | bytes 30724
  0.7 11.1 %copy-start.13 = (f32[288,32]{0,1:T(8,128)S(1)}, f32[288,32]{0,1:T(8,128)}, u32[]{:S(2)}) copy-start(f32[288,32]{0,1:T(8,128)} %param.35) | copy-start | bytes 110596
  0.7 11.1 %copy-start.18 = (f32[39,32]{0,1:T(8,128)S(1)}, f32[39,32]{0,1:T(8,128)}, u32[]{:S(2)}) copy-start(f32[39,32]{0,1:T(8,128)} %param.36) | copy-start | bytes 14980
  0.7 11.8 %copy-start.7 = (f32[1024,128]{1,0:T(8,128)S(1)}, f32[1024,128]{1,0:T(8,128)}, u32[]{:S(2)}) copy-start(f32[1024,128]{1,0:T(8,128)} %param.40) | copy-start | bytes 1572868
  0.8 12.7 %copy-start.15 = (f32[256,128]{1,0:T(8,128)S(1)}, f32[256,128]{1,0:T(8,128)}, u32[]{:S(2)}) copy-start(f32[256,128]{1,0:T(8,128)} %param.38) | copy-start | bytes 393220
  1.9 12.3 %copy-start.2 = (f32[128,1024]{1,0:T(8,128)S(1)}, f32[128,1024]{1,0:T(8,128)}, u32[]{:S(2)}) copy-start(f32[128,1024]{1,0:T(8,128)} %param.39) | copy-start | bytes 1572868
  8.2 6.8 %copy-start.3 = (f32[128,768]{1,0:T(8,128)S(1)}, f32[128,768]{1,0:T(8,128)}, u32[]{:S(2)}) copy-start(f32[128,768]{1,0:T(8,128)} %param.37) | copy-start | bytes 1179652
  13.5 0.7 copy-start.5
  220.9 159.1 %copy-start.22 = (f32[32,80]{1,0:T(8,128)S(1)}, f32[32,80]{1,0:T(8,128)}, u32[]{:S(2)}) copy-start(f32[32,80]{1,0:T(8,128)} %param.48) | copy-start | bytes 30724
  220.9 159.1 %copy-start.23 = (f32[32,80]{1,0:T(8,128)S(1)}, f32[32,80]{1,0:T(8,128)}, u32[]{:S(2)}) copy-start(f32[32,80]{1,0:T(8,128)} %param.55) | copy-start | bytes 30724
  386.3 3.0 copy-start.8
  386.3 3.0 copy-start.9
  387.3 6.8 %copy-start.6 = (f32[256,128]{0,1:T(8,128)S(1)}, f32[256,128]{0,1:T(8,128)}, u32[]{:S(2)}) copy-start(f32[256,128]{0,1:T(8,128)} %copy-done.5) | copy-start | bytes 393220
  389.3 8.1 %copy-start.4 = (f32[128,768]{1,0:T(8,128)S(1)}, f32[128,768]{1,0:T(8,128)}, u32[]{:S(2)}) copy-start(f32[128,768]{1,0:T(8,128)} %param.37) | copy-start | bytes 1179652
  389.3 8.1 %copy-start.10 = (f32[128,768]{1,0:T(8,128)S(1)}, f32[128,768]{1,0:T(8,128)}, u32[]{:S(2)}) copy-start(f32[128,768]{1,0:T(8,128)} %param.44) | copy-start | bytes 1179652
  389.3 8.1 %copy-start.11 = (f32[128,768]{1,0:T(8,128)S(1)}, f32[128,768]{1,0:T(8,128)}, u32[]{:S(2)}) copy-start(f32[128,768]{1,0:T(8,128)} %param.51) | copy-start | bytes 1179652
  389.3 8.1 %copy-start.12 = (f32[128,768]{1,0:T(8,128)S(1)}, f32[128,768]{1,0:T(8,128)}, u32[]{:S(2)}) copy-start(f32[128,768]{1,0:T(8,128)} %get-tuple-element.81) | copy-start | bytes 1179652
  389.3 10.7 %copy-start.1 = (s32[2,1,1024]{2,1,0:T(1,128)S(1)}, s32[2,1,1024]{2,1,0:T(1,128)}, u32[]{:S(2)}) copy-start(s32[2,1,1024]{2,1,0:T(1,128)} %param.33) | copy-start | bytes 24580
  392.0 6.7 %copy-start.16 = (f32[32,640]{1,0:T(8,128)S(1)}, f32[32,640]{1,0:T(8,128)}, u32[]{:S(2)}) copy-start(f32[32,640]{1,0:T(8,128)} %get-tuple-element.80) | copy-start | bytes 245764
  392.0 6.7 %copy-start.19 = (f32[39,32]{0,1:T(8,128)S(1)}, f32[39,32]{0,1:T(8,128)}, u32[]{:S(2)}) copy-start(f32[39,32]{0,1:T(8,128)} %param.36) | copy-start | bytes 14980
  392.0 6.7 %copy-start.24 = (f32[39,32]{0,1:T(8,128)S(1)}, f32[39,32]{0,1:T(8,128)}, u32[]{:S(2)}) copy-start(f32[39,32]{0,1:T(8,128)} %param.43) | copy-start | bytes 14980
  392.0 6.7 %copy-start.25 = (f32[39,32]{0,1:T(8,128)S(1)}, f32[39,32]{0,1:T(8,128)}, u32[]{:S(2)}) copy-start(f32[39,32]{0,1:T(8,128)} %param.50) | copy-start | bytes 14980
  392.0 7.3 %copy-start.14 = (f32[288,32]{0,1:T(8,128)S(1)}, f32[288,32]{0,1:T(8,128)}, u32[]{:S(2)}) copy-start(f32[288,32]{0,1:T(8,128)} %param.35) | copy-start | bytes 110596
  392.0 7.3 %copy-start.20 = (f32[288,32]{0,1:T(8,128)S(1)}, f32[288,32]{0,1:T(8,128)}, u32[]{:S(2)}) copy-start(f32[288,32]{0,1:T(8,128)} %param.42) | copy-start | bytes 110596
  392.0 7.3 %copy-start.21 = (f32[288,32]{0,1:T(8,128)S(1)}, f32[288,32]{0,1:T(8,128)}, u32[]{:S(2)}) copy-start(f32[288,32]{0,1:T(8,128)} %param.49) | copy-start | bytes 110596

commit v4 on v3

--- a/solution.py
+++ b/solution.py
@@ -987,14 +987,14 @@
 
 
 class MiddleIn(NamedTuple):
+    places: Any
     second: Any
     a2: Any
     active: Any
     slope: Any
     chan: Any
-    w_head: Any
+    thin: Any
     target: Any
-    weights: Any
     mid: Any
     down: Any
 
@@ -1011,14 +1011,14 @@
 
 
 class MiddleRefs(NamedTuple):
+    places: Any
     second: Any
     a2: Any
     active: Any
     slope: Any
     chan: Any
-    w_head: Any
+    thin: Any
     target: Any
-    weights: Any
     mid: Any
     down: Any
     g_up: Any
@@ -1100,13 +1100,26 @@
         r.a3[here] = (xhat * row(4) + row(5)).astype(bf)
 
     by_tiles(rows, TILE, third_norm)
-    error = dot(r.a3[...], r.w_head[...]) - r.target[...]
-    weighted = r.weights[...] * error
-    lanes = lax.broadcasted_iota(jnp.int32, (8, 128), 1)
+    mel = r.places[6]
+    lanes = lax.broadcasted_iota(jnp.int32, (16, 128), 1)
+    digits = jnp.zeros((16, 128), f32)
+    for d in range(ndp):
+        start = d * (model // ndp)
+        digits = digits + r.thin[start : start + 16, THIN_HEAD:].astype(f32)
+    first_digit = mel + 2 * r.places[5]
+    scale = jnp.where(lanes == first_digit, 32.0, jnp.where(lanes == first_digit + 1, 1.0, 0.0))
+    count = jnp.sum(digits[0:1] * scale[0:1], axis=1, keepdims=True)
+    place = r.places[0] + lax.broadcasted_iota(jnp.int32, (rows, 1), 0)
+    weights = jnp.where((place >= r.places[3]) & (place < r.places[4]), 1.0, 0.0) / count
+    head_lanes = lax.broadcasted_iota(jnp.int32, (model, 128), 1)
+    head = jnp.where(head_lanes < mel, r.thin[:, THIN_HEAD:].astype(f32), 0.0).astype(bf)
+    error = dot(r.a3[...], head) - r.target[...]
+    weighted = weights * error
+    lanes = lanes[:8]
     r.loss[...] = jnp.where(lanes == 0, jnp.sum(weighted * error), 0.0)
     dpred = (2.0 * weighted).astype(bf)
     r.g_head[...] = tdot(r.a3[...], dpred).astype(bf)
-    r.dsecond[...] = rdot(dpred, r.w_head[...])
+    r.dsecond[...] = rdot(dpred, head)
 
     zero = jnp.zeros((1, model), f32)
 
@@ -1225,7 +1238,7 @@
         functools.partial(middle_kernel, ndp, nmp),
         name="middle",
         out_shape=outs,
-        in_specs=[VMEM] * 8 + [anywhere] * 2,
+        in_specs=[SMEM] + [VMEM] * 7 + [anywhere] * 2,
         out_specs=[anywhere] * 2 + [VMEM] * 6,
         scratch_shapes=scratch,
         compiler_params=pltpu.CompilerParams(
@@ -1380,7 +1393,8 @@
         copies = [
             fetch(src, ref)
             for src, ref in (
-                (r.first, first), (r.conv, conv), (r.dsecond, back), (r.hm, hm), (r.features, features)
+                (r.first, first), (r.conv, conv), (r.dsecond, back), (r.hm, hm),
+                (r.features.at[pl.ds(PAD, rows)], features),
             )
         ]
         copies[0].wait()
@@ -1493,7 +1507,7 @@
         pltpu.VMEM((rows, model), f32),
         pltpu.VMEM((rows, model), f32),
         pltpu.VMEM((rows + 2 * PAD, model), f32),
-        pltpu.VMEM(r.features.shape, bf),
+        pltpu.VMEM((rows, r.features.shape[1]), bf),
         pltpu.VMEM((rows + 2 * PAD, model), f32),
         pltpu.VMEM((8 * KERNEL, model), f32),
     )
@@ -1593,6 +1607,47 @@
     )(*given)
 
 
+def step_kernel(sums, g_thin, g_qkv, g_out, g_up, g_down, *refs):
+    weights, firsts, seconds = refs[:7], refs[7:14], refs[14:21]
+    loss, grad_norm = refs[21:23]
+    outs = refs[23:]
+    norm = jnp.sqrt(sums[0:1, 1:2])
+    loss[...] = sums[0:1, 0:1]
+    grad_norm[...] = norm
+    factor = CLIP_AT / jnp.maximum(norm, CLIP_AT)
+
+    def update(i, here, grad):
+        new = adam_update(weights[i][here], firsts[i][here], seconds[i][here], grad, factor)
+        for n in range(3):
+            outs[3 * i + n][here] = new[n]
+
+    inputs, channels = weights[0].shape[1], weights[1].shape[1]
+    mel = weights[6].shape[1]
+    every = slice(None)
+    update(0, every, g_thin[:, :THIN_CHAN][:, :inputs])
+    update(1, every, g_thin[:, THIN_CHAN:THIN_HEAD][:, :channels])
+    update(6, every, g_thin[:, THIN_HEAD:][:, :mel])
+    for i, grad in ((2, g_qkv), (4, g_up)):
+        by_tiles(grad.shape[0], 16, lambda here, i=i, grad=grad: update(i, here, grad[here]))
+    for i, grad in ((3, g_out), (5, g_down)):
+        by_tiles(grad.shape[1], 128, lambda here, i=i, grad=grad: update(i, here, grad[:, here].T))
+
+
+def step_all(sums, grads, state):
+    state = [x.T if i % 7 < 2 else x for i, x in enumerate(state)]
+    one = jax.ShapeDtypeStruct((1, 1), f32)
+    outs = [jax.ShapeDtypeStruct(state[i].shape, f32) for i in range(7) for _ in range(3)]
+    loss, norm, *new = pl.pallas_call(
+        step_kernel,
+        name="step",
+        out_shape=[one, one] + outs,
+        in_specs=[VMEM] * 27,
+        out_specs=[VMEM] * 23,
+        compiler_params=pltpu.CompilerParams(vmem_limit_bytes=62 << 20),
+    )(sums, *grads, *state)
+    return (loss[0, 0], norm[0, 0], *[x.T for x in new[:6]], *new[6:])
+
+
 def shards(
     clean_mel,
     noise_mel,
@@ -1688,7 +1743,9 @@
     heads = (owners[:, None] * (HEADS // nmp) + jnp.arange(HEADS // nmp)).reshape(-1)
     slopes = jnp.exp2(-8.0 * (heads + 1).astype(f32) / HEADS)
     if own:
-        places = jnp.stack([base, (1 - seq) * rows, size]).astype(jnp.int32)
+        numbers = [base, (1 - seq) * rows, size, first_frame, last_frame, batch, mel]
+        places = jnp.stack([jnp.asarray(n, jnp.int32) for n in numbers])
+        features_wide = columns(features_ext, THIN_CHAN)
         fore = fore_all(
             ndp,
             nmp,
@@ -1699,7 +1756,7 @@
                 near_own=attn_qkv.astype(bf),
                 mid_own=mid,
                 down_own=ffn_down.T.astype(bf),
-                features=columns(features_ext, THIN_CHAN),
+                features=features_wide,
             ),
         )
         thin = fore.thin
@@ -1712,25 +1769,19 @@
         rest = rest.reshape(nmp, -1, rest.shape[1])
         owners = jnp.arange(nmp)
     model = thin.shape[0]
-    digits = thin[:, THIN_HEAD + mel : THIN_HEAD + mel + 2 * micro]
-    digits = jnp.sum(digits.reshape(ndp, -1, 2 * micro)[:, 0].astype(f32), axis=0)
-    count = lax.dynamic_slice_in_dim(digits, 2 * batch, 2, 0)
-    count = count[0] * 32.0 + count[1]
-
     if own:
-        lanes = jnp.arange(128) < mel
         middle = middle_all(
             ndp,
             nmp,
             MiddleIn(
+                places=places,
                 second=fore.second,
                 a2=fore.a2,
                 active=fore.active,
                 slope=fore.slope,
                 chan=fore.chan,
-                w_head=jnp.where(lanes, thin[:, THIN_HEAD:], 0),
+                thin=fore.thin,
                 target=jnp.pad(target, ((0, 0), (0, 128 - mel))),
-                weights=jnp.broadcast_to(masked / count, (rows, 128)),
                 mid=fore.mid,
                 down=fore.down,
             ),
@@ -1756,10 +1807,21 @@
             conv=fore.conv,
             dsecond=middle.dsecond,
             hm=fore.hm,
-            features=columns(features, THIN_CHAN),
+            features=features_wide,
         )
         g_thin, g_up, g_down, g_qkv, g_out, sums = back_all(ndp, nmp, given)
+        state = (
+            in_table, channel_rows, attn_qkv, attn_out, ffn_up, ffn_down, mel_head,
+            table_first, channel_first, qkv_first, merge_first, upward_first, downward_first,
+            head_first, table_second, channel_second, qkv_second, merge_second, upward_second,
+            downward_second, head_second,
+        )
+        return step_all(sums, (g_thin, g_qkv, g_out, g_up, g_down), state)
     else:
+        digits = thin[:, THIN_HEAD + mel : THIN_HEAD + mel + 2 * micro]
+        digits = jnp.sum(digits.reshape(ndp, -1, 2 * micro)[:, 0].astype(f32), axis=0)
+        count = lax.dynamic_slice_in_dim(digits, 2 * batch, 2, 0)
+        count = count[0] * 32.0 + count[1]
         w_out = rest[:, :, :c_out]
         w_up = rest[:, :, c_out : c_out + c_up]
         w_down = rest[:, :, c_out + c_up :]

time: 408 us -> 390 us (0.956)
  local copies, waits for them, and re-layouts: 21.6 us -> 7.72 us
  other arithmetic: 20.4 us -> 11.9 us
  Pallas kernels: 354 us -> 362 us
    unnamed x68 -> x12, local copies, waits for them, and re-layouts: 11.7 us -> 1.87 us
    sub x7 -> x0, other arithmetic: 9.17 us -> none  [adam_update(): weight - RATE * (first_hat / (jnp.sqrt(second_hat) + EPSILON) + DECAY * w...]
    pallas_call x0 -> x1, Pallas kernels: none -> 7.82 us  [step_all(): pl.pallas_call(step_kernel, name='step', out_shape=[one, one] + outs, in_...]
where the time goes in v4:
time: 390 us; the launch traced here: 384 us
  Pallas kernels  362 us (93%)
  other arithmetic  11.9 us (3%)
  local copies, waits for them, and re-layouts  7.72 us (2%)
    pallas_call x1, Pallas kernels, back_all(): pl.pallas_call(functools.partial(back_kernel, ndp, nmp), name='back', out...  157 us
    pallas_call x1, Pallas kernels, fore_all(): pl.pallas_call(functools.partial(fore_kernel, ndp, nmp), name='fore', out...  144 us
    pallas_call x1, Pallas kernels, middle_all(): pl.pallas_call(functools.partial(middle_kernel, ndp, nmp), name='middle',...  53.6 us
    pallas_call x1, Pallas kernels, step_all(): pl.pallas_call(step_kernel, name='step', out_shape=[one, one] + outs, in_...  7.82 us

profile of v4, /device:TPU:0, one launch (start us, length us, event | category | flops | bytes accessed | tf_op | source)
XLA Modules:
  0.0 384.1 jit_solution(16004313668776979889)
XLA Ops:
  0.7 0.0 copy-start
  0.8 0.1 add_multiply_fusion
  0.8 1.3 constant_dynamic-slice_fusion.6
  3.5 0.7 and_select_fusion.1
  4.2 0.1 copy.51
  4.3 0.1 reshape.125
  4.4 0.1 pad.48.clone
  4.5 1.3 constant_dynamic-slice_fusion.4
  5.7 2.5 stack.35.refs_0_
  8.3 0.1 multiply_exponential_fusion
  8.3 0.6 reshape.123.refs_1_
  8.9 1.9 subtract_select_fusion
  10.9 0.1 pad_dynamic-slice_fusion.2
  11.0 0.7 bitcast_convert_fusion
  11.7 0.7 convert.14
  12.5 0.8 bitcast_convert_fusion.1
  13.3 0.6 fusion.13.refs_2_
  13.9 1.0 copy.52
  14.9 0.1 fusion.5
  15.0 1.7 convert_element_type.73.refs_3_
  16.7 1.1 convert.17
  17.8 0.7 pad_maximum_fusion.refs_4_
  18.6 0.8 copy.53
  19.4 0.2 copy.55
  19.6 0.2 copy.54
  19.8 0.2 add_convert_fusion
  20.0 1.0 fusion.4.refs_6_.refs_20_
  21.1 0.7 pad.38.refs_7_
  21.8 143.6 %fore.1 = (bf16[1024,640]{1,0:T(8,128)(2,1)}, bf16[4,1024,768]{2,1,0:T(8,128)(2,1)}, bf16[4,1024,1280]{2,1,0:T(8,128)(2,1)}, bf16[4,1024,1024]{2,1,0:T(8,128)(2,...) custom-call(s32[7]{0:T(128)} %stack.35.refs_0_, ...), custom_call_target="tpu_custom_call" | custom-call | tf_op jit(solution)/shard_map/fore/pallas_call | solution.py:963
  165.4 53.6 %middle.1 = (bf16[2,1024,1024]{2,1,0:T(8,128)(2,1)}, bf16[2,1024,1024]{2,1,0:T(8,128)(2,1)}, f32[512,1024]{1,0:T(8,128)}, bf16[512,1024]{1,0:T(8,128)(2,1)}, bf1...) custom-call(s32[7]{0:T(128)} %stack.35.refs_0_, ...), custom_call_target="tpu_custom_call" | custom-call | tf_op jit(solution)/shard_map/middle/pallas_call | solution.py:1237
  219.0 156.7 %back.1 = (f32[32,640]{1,0:T(8,128)}, f32[128,1024]{1,0:T(8,128)}, f32[128,1024]{1,0:T(8,128)}, f32[128,768]{1,0:T(8,128)}, f32[128,256]{1,0:T(8,128)}, /*index=5*/f32[8,128]{1,0:T(8,128)}) custom-call(s32[7]{0:T(128)} %stack.35.refs_0_, f32[16]{0:T(128)} %reshape.123.refs_1_, f32[8,128]{1,0:T(8,128)} %get-tuple-element.85.refs_2_, ...), custom_call_target="tpu_custom_call" | custom-call | tf_op jit(solution)/shard_map/back/pallas_call | solution.py:1597
  375.8 7.8 %step.1 = (f32[1,1]{1,0:T(1,128)}, f32[1,1]{1,0:T(1,128)}, f32[32,288]{1,0:T(8,128)}, f32[32,288]{1,0:T(8,128)}, f32[32,288]{1,0:T(8,128)}, /*index=5*/f32[32,39...) custom-call(f32[8,128]{1,0:T(8,128)} %get-tuple-element.102.sums, ...), custom_call_target="tpu_custom_call" | custom-call | tf_op jit(solution)/shard_map/step/pallas_call | solution.py:1640
  (17 shorter events, 0.2 us)
Async XLA Ops:
  0.7 10.2 %copy-start = (s32[2,1,1024]{2,1,0:T(1,128)S(1)}, s32[2,1,1024]{2,1,0:T(1,128)}, u32[]{:S(2)}) copy-start(s32[2,1,1024]{2,1,0:T(1,128)} %param.33) | copy-start | bytes 24580
  0.7 17.9 %copy-start.2 = (f32[1024,128]{1,0:T(8,128)S(1)}, f32[1024,128]{1,0:T(8,128)}, u32[]{:S(2)}) copy-start(f32[1024,128]{1,0:T(8,128)} %refs_5_.1) | copy-start | bytes 1572868
  0.7 18.7 %copy-start.4 = (bf16[2,1,1024,80]{2,3,1,0:T(8,128)(2,1)S(1)}, bf16[2,1,1024,80]{2,3,1,0:T(8,128)(2,1)}, u32[]{:S(2)}) copy-start(bf16[2,1,1024,80]{2,3,1,0:T(8,128)(2,1)} %param.29) | copy-start | bytes 983044
  0.7 18.7 %copy-start.3 = (bf16[2,1,1024,80]{2,3,1,0:T(8,128)(2,1)S(1)}, bf16[2,1,1024,80]{2,3,1,0:T(8,128)(2,1)}, u32[]{:S(2)}) copy-start(bf16[2,1,1024,80]{2,3,1,0:T(8,128)(2,1)} %param.28) | copy-start | bytes 983044
  375.8 7.8 %copy-start.1 = (s32[2,1,1024]{2,1,0:T(1,128)S(1)}, s32[2,1,1024]{2,1,0:T(1,128)}, u32[]{:S(2)}) copy-start(s32[2,1,1024]{2,1,0:T(1,128)} %param.33) | copy-start | bytes 24580

commit v5 on v4

--- a/solution.py
+++ b/solution.py
@@ -563,102 +563,100 @@
         1, 8, 4, 2, 9, 16, 5, 3, 24, 17, 25, 12, 10, 6, 20, 13, 11, 28, 18, 7, 21, 26, 29, 19, 14, 27, 22,
         15, 30, 23, 31, 33, 65, 36, 34, 68, 66, 40, 48,
     ),
-    (56,),
+    (56, 72, 37, 35, 69, 67, 41, 49, 38),
+    (97, 70, 129),
     (),
-    (72,),
-    (37, 35),
-    (69, 67),
-    (41,),
-    (49,),
-    (38,),
-    (97, 70),
-    (129,),
-    (80, 42, 44, 57),
-    (73, 88, 50, 52),
+    (80, 42, 44),
     (),
-    (39, 71),
+    (88, 50),
+    (52, 57, 73),
+    (39,),
+    (71,),
     (98,),
     (100, 81, 43, 45),
+    (89, 51),
+    (53, 130),
+    (132, 104),
+    (58, 99, 60),
+    (101, 74),
+    (76, 112),
+    (131, 82, 84, 120, 133, 105),
+    (46, 59, 92, 61),
+    (75, 90),
+    (77, 113),
+    (
+        54, 83, 85, 47, 93, 91, 55, 78, 79, 62, 63, 86, 87, 94, 95, 134, 121, 136, 108, 102, 144, 106, 152,
+        116, 114, 124,
+    ),
+    (122,),
     (),
-    (89, 51, 53),
-    (130,),
-    (132,),
-    (104, 58),
-    (
-        60, 74, 76, 82, 84, 59, 61, 75, 77, 83, 46, 85, 92, 90, 47, 93, 91, 54, 55, 78, 86, 79, 87, 62, 94,
-        63, 95, 99, 101, 112, 131, 120, 133, 105, 134, 108, 136, 102, 144, 106, 152,
-    ),
+    (135, 137),
+    (109, 103, 145, 107, 153, 117, 115, 125),
+    (138, 140, 123),
+    (110, 148),
     (),
+    (161, 146, 156, 193),
+    (139, 141, 164),
+    (154, 111, 149, 168),
+    (196, 118),
+    (147, 157, 176, 142, 184, 165),
+    (126, 155),
+    (169, 150),
+    (162, 197, 119),
+    (177, 143, 185, 194, 158, 200),
+    (127, 166, 172, 208, 151),
+    (216, 163),
+    (170, 180, 195, 159),
+    (201, 178, 188, 167, 173),
     (),
-    (),
-    (113,),
-    (121, 135, 109, 137, 103, 145, 107, 116, 153, 114),
-    (),
-    (124,),
-    (122, 161, 193),
-    (140,),
-    (117, 115, 110),
-    (),
-    (148, 125, 138, 168, 123),
-    (141,),
-    (156, 176, 146, 111),
-    (184, 164),
-    (149, 154, 139, 169),
-    (196,),
-    (162, 157, 177, 147),
-    (142, 200, 185, 194, 165),
-    (155, 172, 208),
-    (118, 143, 126, 150, 119, 127, 151, 158, 159, 197, 163, 180, 216, 201, 195, 173, 209, 170, 188),
-    (178,),
-    (186,),
-    (204, 181, 166, 217, 171, 189),
-    (198, 202, 179),
-    (212, 174, 187),
-    (
-        220, 205, 210, 167, 199, 182, 203, 206, 213, 218, 175, 221, 211, 183, 207, 219, 214, 190, 215, 222,
-        191, 223,
-    ),
+    (209, 186, 198, 217, 171, 181, 202, 204, 179, 189),
+    (174, 212, 210, 220),
+    (187, 199, 203, 205, 218, 206, 182),
+    (175, 213, 211, 221, 190, 214),
+    (219, 207, 183, 222),
+    (191, 215, 223),
 )
 BACK_TURNS = (
-    (34, 100, 42, 108, 50, 116, 58, 124, 38, 102, 46, 110),
-    (54, 118),
-    (62, 126, 162, 228, 2, 68),
+    (34, 100, 42, 108, 50, 116, 58, 124, 38, 102),
+    (46, 110),
+    (54, 118, 62, 126),
+    (162, 228, 2, 68),
     (170, 236, 10, 76),
-    (178, 244, 18, 84),
-    (186, 252, 26, 92, 166, 230, 6, 70),
+    (178, 244, 18, 186, 252, 84, 26, 92),
+    (166, 230, 6, 70),
     (14, 78),
     (22, 86),
     (30, 94),
-    (130, 196),
-    (174, 238, 138, 204, 182, 246, 146, 212),
+    (130, 174, 238, 196, 138, 204),
+    (182, 246, 146, 212),
     (190, 254, 154, 220),
-    (290, 356, 298, 364, 306, 372, 134, 198),
-    (314, 380, 66, 4, 294, 358, 74, 12, 302, 366),
-    (310, 374, 318, 382, 82, 20),
+    (290, 356, 298, 364, 306, 372, 314, 380, 134, 294, 198, 66, 4),
+    (358, 302, 366, 74, 12, 310, 374),
+    (318, 382, 82, 20),
     (90, 28),
-    (72, 142, 206, 8, 150, 214),
-    (158, 222, 258, 324, 266, 332),
-    (274, 340, 80),
-    (194, 132, 282, 348),
-    (262, 326, 270, 334, 278, 342, 16, 286, 350),
-    (88, 202, 140),
-    (418, 484, 426, 492, 434, 500, 442, 508, 422, 486, 430, 494, 438, 502, 446, 510, 24, 210, 148),
-    (218, 156, 322, 260),
-    (330, 268, 338, 276, 346, 284, 200),
+    (142, 206, 72, 150, 214),
     (),
-    (386, 452, 136, 394, 460),
+    (8, 158, 222, 258, 324, 266, 332, 274, 340, 282, 348),
+    (262,),
+    (80, 132, 194, 326, 270, 334, 278, 342, 286, 350),
+    (418, 484, 426, 492, 434, 500, 442, 508, 422, 486, 430, 494, 16, 202, 140, 438, 502),
+    (88, 210, 446, 510, 148),
+    (),
+    (24, 218, 156, 322, 260, 330, 268),
+    (338, 276, 346, 284, 386, 452, 200),
+    (394, 460, 136),
     (402, 468),
-    (410, 476, 208),
-    (390, 454),
-    (398, 462, 144, 406, 470),
-    (414, 478, 216),
-    (388, 450, 152),
-    (328, 264, 396, 458),
-    (336, 404, 466, 272, 344),
+    (410, 476),
+    (390, 454, 208),
+    (398, 462),
+    (406, 470, 144, 414, 478),
+    (),
+    (216, 388, 450),
     (
-        545, 553, 561, 569, 549, 557, 565, 573, 547, 555, 563, 571, 551, 559, 567, 575, 280, 412, 474, 392,
-        456, 513, 521, 529, 537, 517, 525, 533, 541, 515, 523, 531, 539, 519, 527, 535, 543, 400, 514, 522,
-        530, 464, 538, 518, 408, 526, 534, 516, 542, 472, 524, 532, 540, 520, 528, 536,
+        545, 553, 561, 569, 549, 557, 565, 573, 547, 555, 563, 571, 551, 559, 567, 575, 152, 328, 396, 264,
+        458, 336, 404, 466, 272, 344, 412, 280, 474, 513, 521, 529, 537, 517, 525, 533, 541, 515, 523, 531,
+        539, 519, 527, 535, 543, 392, 456, 514, 522, 530, 538, 518, 400, 526, 534, 516, 542, 524, 532, 540,
+        464, 408, 472, 520, 528, 536,
     ),
 )
 
@@ -1093,7 +1091,7 @@
             part = rdot(r.active[m], w_down[m][cols, :])
             r.ffn[:, cols] = part if m == theirs[0] else r.ffn[:, cols] + part
 
-        by_tiles(model, COLS, shrink)
+        by_tiles(model, 4 * COLS, shrink)
 
     def third_norm(here):
         xhat, _ = norm_parts(r.second[here] + r.ffn[here])
@@ -1149,7 +1147,7 @@
             part = tdot(left[:, cols], right[...]) + tdot(left_other[:, cols], right_other[...])
             r.stage[slot, cols] = part.astype(bf)
 
-        by_tiles(model, COLS, body)
+        by_tiles(model, 4 * COLS, body)
         copy = pltpu.make_async_copy(r.stage.at[slot], out.at[y], r.local.at[2 * nmp + len(stored)])
         copy.start()
         stored.append(copy)
@@ -1162,7 +1160,7 @@
             dact = dot(r.dffn[...], w_down[m][:, cols])
             r.dhid[m, :, cols] = (dact * r.slope[m, :, cols].astype(f32)).astype(bf)
 
-        by_tiles(hid, COLS, contract)
+        by_tiles(hid, 4 * COLS, contract)
         if m in theirs:
             got_dhid.append(cross(r.dhid.at[m], r.l_dhid.at[m // 2]))
 
@@ -1170,7 +1168,7 @@
             part = rdot(r.dhid[m], w_up[m][cols, :])
             r.dsecond[:, cols] = part if m == theirs[0] else r.dsecond[:, cols] + part
 
-        by_tiles(model, COLS, gather_da2)
+        by_tiles(model, 4 * COLS, gather_da2)
     got_dffn.wait_recv()
     for y in range(ny):
         got_active[y].wait_recv()

time: 390 us -> 364 us (0.933)
  Pallas kernels: 362 us -> 336 us
    pallas_call x1, Pallas kernels: 53.6 us -> 43.4 us  [middle_all(): pl.pallas_call(functools.partial(middle_kernel, ndp, nmp), name='middle',...]
    pallas_call x1, Pallas kernels: 144 us -> 136 us  [fore_all(): pl.pallas_call(functools.partial(fore_kernel, ndp, nmp), name='fore', out...]
    pallas_call x1, Pallas kernels: 157 us -> 149 us  [back_all(): pl.pallas_call(functools.partial(back_kernel, ndp, nmp), name='back', out...]
where the time goes in v5:
time: 364 us; the launch traced here: 358 us
  Pallas kernels  336 us (92%)
  other arithmetic  11.9 us (3%)
  local copies, waits for them, and re-layouts  7.72 us (2%)
    pallas_call x1, Pallas kernels, back_all(): pl.pallas_call(functools.partial(back_kernel, ndp, nmp), name='back', out...  149 us
    pallas_call x1, Pallas kernels, fore_all(): pl.pallas_call(functools.partial(fore_kernel, ndp, nmp), name='fore', out...  136 us
    pallas_call x1, Pallas kernels, middle_all(): pl.pallas_call(functools.partial(middle_kernel, ndp, nmp), name='middle',...  43.4 us
    pallas_call x1, Pallas kernels, step_all(): pl.pallas_call(step_kernel, name='step', out_shape=[one, one] + outs, in_...  7.82 us

profile of v5, /device:TPU:0, one launch (start us, length us, event | category | flops | bytes accessed | tf_op | source)
XLA Modules:
  0.0 357.6 jit_solution(9344221059565968342)
XLA Ops:
  0.7 0.0 copy-start
  0.8 0.1 add_multiply_fusion
  0.8 1.3 constant_dynamic-slice_fusion.6
  3.5 0.7 and_select_fusion.1
  4.2 0.1 copy.51
  4.3 0.1 reshape.125
  4.4 0.1 pad.48.clone
  4.5 1.3 constant_dynamic-slice_fusion.4
  5.7 2.5 stack.35.refs_0_
  8.3 0.1 multiply_exponential_fusion
  8.3 0.6 reshape.123.refs_1_
  8.9 1.9 subtract_select_fusion
  10.9 0.1 pad_dynamic-slice_fusion.2
  11.0 0.7 bitcast_convert_fusion
  11.7 0.7 convert.14
  12.5 0.8 bitcast_convert_fusion.1
  13.3 0.6 fusion.13.refs_2_
  13.9 1.0 copy.52
  14.9 0.1 fusion.5
  15.0 1.7 convert_element_type.73.refs_3_
  16.7 1.1 convert.17
  17.8 0.7 pad_maximum_fusion.refs_4_
  18.6 0.8 copy.53
  19.4 0.2 copy.55
  19.6 0.2 copy.54
  19.8 0.2 add_convert_fusion
  20.0 1.0 fusion.4.refs_6_.refs_20_
  21.1 0.7 pad.38.refs_7_
  21.8 135.6 %fore.1 = (bf16[1024,640]{1,0:T(8,128)(2,1)}, bf16[4,1024,768]{2,1,0:T(8,128)(2,1)}, bf16[4,1024,1280]{2,1,0:T(8,128)(2,1)}, bf16[4,1024,1024]{2,1,0:T(8,128)(2,...) custom-call(s32[7]{0:T(128)} %stack.35.refs_0_, ...), custom_call_target="tpu_custom_call" | custom-call | tf_op jit(solution)/shard_map/fore/pallas_call | solution.py:961
  157.4 43.4 %middle.1 = (bf16[2,1024,1024]{2,1,0:T(8,128)(2,1)}, bf16[2,1024,1024]{2,1,0:T(8,128)(2,1)}, f32[512,1024]{1,0:T(8,128)}, bf16[512,1024]{1,0:T(8,128)(2,1)}, bf1...) custom-call(s32[7]{0:T(128)} %stack.35.refs_0_, ...), custom_call_target="tpu_custom_call" | custom-call | tf_op jit(solution)/shard_map/middle/pallas_call | solution.py:1235
  200.7 148.7 %back.1 = (f32[32,640]{1,0:T(8,128)}, f32[128,1024]{1,0:T(8,128)}, f32[128,1024]{1,0:T(8,128)}, f32[128,768]{1,0:T(8,128)}, f32[128,256]{1,0:T(8,128)}, /*index=5*/f32[8,128]{1,0:T(8,128)}) custom-call(s32[7]{0:T(128)} %stack.35.refs_0_, f32[16]{0:T(128)} %reshape.123.refs_1_, f32[8,128]{1,0:T(8,128)} %get-tuple-element.85.refs_2_, ...), custom_call_target="tpu_custom_call" | custom-call | tf_op jit(solution)/shard_map/back/pallas_call | solution.py:1595
  349.5 7.8 %step.1 = (f32[1,1]{1,0:T(1,128)}, f32[1,1]{1,0:T(1,128)}, f32[32,288]{1,0:T(8,128)}, f32[32,288]{1,0:T(8,128)}, f32[32,288]{1,0:T(8,128)}, /*index=5*/f32[32,39...) custom-call(f32[8,128]{1,0:T(8,128)} %get-tuple-element.102.sums, ...), custom_call_target="tpu_custom_call" | custom-call | tf_op jit(solution)/shard_map/step/pallas_call | solution.py:1638
  (17 shorter events, 0.2 us)
Async XLA Ops:
  0.7 10.2 %copy-start = (s32[2,1,1024]{2,1,0:T(1,128)S(1)}, s32[2,1,1024]{2,1,0:T(1,128)}, u32[]{:S(2)}) copy-start(s32[2,1,1024]{2,1,0:T(1,128)} %param.33) | copy-start | bytes 24580
  0.7 17.9 %copy-start.2 = (f32[1024,128]{1,0:T(8,128)S(1)}, f32[1024,128]{1,0:T(8,128)}, u32[]{:S(2)}) copy-start(f32[1024,128]{1,0:T(8,128)} %refs_5_.1) | copy-start | bytes 1572868
  0.7 18.7 %copy-start.4 = (bf16[2,1,1024,80]{2,3,1,0:T(8,128)(2,1)S(1)}, bf16[2,1,1024,80]{2,3,1,0:T(8,128)(2,1)}, u32[]{:S(2)}) copy-start(bf16[2,1,1024,80]{2,3,1,0:T(8,128)(2,1)} %param.29) | copy-start | bytes 983044
  0.7 18.7 %copy-start.3 = (bf16[2,1,1024,80]{2,3,1,0:T(8,128)(2,1)S(1)}, bf16[2,1,1024,80]{2,3,1,0:T(8,128)(2,1)}, u32[]{:S(2)}) copy-start(bf16[2,1,1024,80]{2,3,1,0:T(8,128)(2,1)} %param.28) | copy-start | bytes 983044
  349.5 7.8 %copy-start.1 = (s32[2,1,1024]{2,1,0:T(1,128)S(1)}, s32[2,1,1024]{2,1,0:T(1,128)}, u32[]{:S(2)}) copy-start(s32[2,1,1024]{2,1,0:T(1,128)} %param.33) | copy-start | bytes 24580

commit v6 on v5

--- a/solution.py
+++ b/solution.py
@@ -620,43 +620,43 @@
     (34, 100, 42, 108, 50, 116, 58, 124, 38, 102),
     (46, 110),
     (54, 118, 62, 126),
-    (162, 228, 2, 68),
-    (170, 236, 10, 76),
-    (178, 244, 18, 186, 252, 84, 26, 92),
-    (166, 230, 6, 70),
+    (162, 228),
+    (170, 236, 2, 68),
+    (178, 244, 10, 76),
+    (186, 252, 18, 84, 166, 230),
+    (174, 238, 26, 92, 6, 70),
     (14, 78),
     (22, 86),
     (30, 94),
-    (130, 174, 238, 196, 138, 204),
-    (182, 246, 146, 212),
-    (190, 254, 154, 220),
-    (290, 356, 298, 364, 306, 372, 314, 380, 134, 294, 198, 66, 4),
-    (358, 302, 366, 74, 12, 310, 374),
-    (318, 382, 82, 20),
+    (130, 182, 246, 196, 138, 204),
+    (190, 254, 146, 212),
+    (290, 356, 298, 364, 306, 372, 154, 220, 314, 380),
+    (294, 358, 302, 366, 310, 374, 318, 382, 134, 198, 142, 206),
+    (66, 4),
+    (74, 12),
+    (82, 20),
     (90, 28),
-    (142, 206, 72, 150, 214),
+    (150, 214),
+    (158, 222, 258, 324),
+    (266, 332, 274, 340, 282, 348, 72, 262, 326, 270, 334),
+    (418, 484, 426, 492, 434, 500, 442, 508, 422, 486, 430, 494, 278, 342, 286, 350, 8),
+    (194, 132, 438, 502),
     (),
-    (8, 158, 222, 258, 324, 266, 332, 274, 340, 282, 348),
-    (262,),
-    (80, 132, 194, 326, 270, 334, 278, 342, 286, 350),
-    (418, 484, 426, 492, 434, 500, 442, 508, 422, 486, 430, 494, 16, 202, 140, 438, 502),
-    (88, 210, 446, 510, 148),
-    (),
-    (24, 218, 156, 322, 260, 330, 268),
-    (338, 276, 346, 284, 386, 452, 200),
-    (394, 460, 136),
-    (402, 468),
-    (410, 476),
-    (390, 454, 208),
-    (398, 462),
-    (406, 470, 144, 414, 478),
-    (),
-    (216, 388, 450),
+    (446, 510, 202, 140, 80),
+    (210, 148),
+    (218, 156, 16, 322, 260, 330, 268),
+    (88, 386, 452),
+    (394, 460, 24),
+    (402, 468, 200),
+    (410, 476, 136, 390, 454),
+    (398, 462, 338, 276),
+    (346, 284, 208),
+    (406, 470, 414, 478),
     (
-        545, 553, 561, 569, 549, 557, 565, 573, 547, 555, 563, 571, 551, 559, 567, 575, 152, 328, 396, 264,
-        458, 336, 404, 466, 272, 344, 412, 280, 474, 513, 521, 529, 537, 517, 525, 533, 541, 515, 523, 531,
-        539, 519, 527, 535, 543, 392, 456, 514, 522, 530, 538, 518, 400, 526, 534, 516, 542, 524, 532, 540,
-        464, 408, 472, 520, 528, 536,
+        545, 553, 561, 569, 549, 557, 565, 573, 547, 555, 563, 571, 551, 559, 567, 575, 144, 388, 450, 216,
+        396, 458, 152, 328, 264, 336, 404, 466, 272, 344, 513, 521, 529, 412, 537, 517, 525, 474, 280, 533,
+        541, 515, 523, 531, 539, 519, 527, 535, 543, 392, 456, 514, 522, 530, 538, 518, 400, 526, 534, 516,
+        542, 524, 532, 464, 540, 408, 472, 520, 528, 536,
     ),
 )
 
@@ -845,7 +845,7 @@
         def expand(cols):
             r.packed[m, :, cols] = dot(r.a1[...], r.near[m, :, cols]).astype(bf)
 
-        by_tiles(width, COLS, expand)
+        by_tiles(width, 3 * COLS, expand)
         copy = pltpu.make_async_remote_copy(
             r.packed.at[m], r.other.at[m], r.c_send.at[m], r.c_recv.at[m],
             device_id=wires.peer("c", 1), device_id_type=MESH,
@@ -888,7 +888,7 @@
             acc = acc + rdot(r.mixed[m], w_out[m][cols, :])
         r.second[:, cols] = acc
 
-    by_tiles(model, COLS, project)
+    by_tiles(model, 4 * COLS, project)
 
     def second_norm(here):
         xhat, _ = norm_parts(r.second[here])

time: 364 us -> 362 us (level)
  no operation moved by 1% of the time
where the time goes in v6:
time: 362 us; the launch traced here: 357 us
  Pallas kernels  334 us (92%)
  other arithmetic  11.9 us (3%)
  local copies, waits for them, and re-layouts  7.72 us (2%)
    pallas_call x1, Pallas kernels, back_all(): pl.pallas_call(functools.partial(back_kernel, ndp, nmp), name='back', out...  147 us
    pallas_call x1, Pallas kernels, fore_all(): pl.pallas_call(functools.partial(fore_kernel, ndp, nmp), name='fore', out...  136 us
    pallas_call x1, Pallas kernels, middle_all(): pl.pallas_call(functools.partial(middle_kernel, ndp, nmp), name='middle',...  43.6 us
    pallas_call x1, Pallas kernels, step_all(): pl.pallas_call(step_kernel, name='step', out_shape=[one, one] + outs, in_...  7.82 us

profile of v6, /device:TPU:0, one launch (start us, length us, event | category | flops | bytes accessed | tf_op | source)
XLA Modules:
  0.0 356.6 jit_solution(1014886843401051539)
XLA Ops:
  0.7 0.0 copy-start
  0.8 0.1 add_multiply_fusion
  0.8 1.3 constant_dynamic-slice_fusion.6
  3.5 0.7 and_select_fusion.1
  4.2 0.1 copy.51
  4.3 0.1 reshape.125
  4.4 0.1 pad.48.clone
  4.5 1.3 constant_dynamic-slice_fusion.4
  5.7 2.5 stack.35.refs_0_
  8.3 0.1 multiply_exponential_fusion
  8.3 0.6 reshape.123.refs_1_
  8.9 1.9 subtract_select_fusion
  10.9 0.1 pad_dynamic-slice_fusion.2
  11.0 0.7 bitcast_convert_fusion
  11.7 0.7 convert.14
  12.5 0.8 bitcast_convert_fusion.1
  13.3 0.6 fusion.13.refs_2_
  13.9 1.0 copy.52
  14.9 0.1 fusion.5
  15.0 1.7 convert_element_type.73.refs_3_
  16.7 1.1 convert.17
  17.8 0.7 pad_maximum_fusion.refs_4_
  18.6 0.8 copy.53
  19.4 0.2 copy.55
  19.6 0.2 copy.54
  19.8 0.2 add_convert_fusion
  20.0 1.0 fusion.4.refs_6_.refs_20_
  21.1 0.7 pad.38.refs_7_
  21.8 135.7 %fore.1 = (bf16[1024,640]{1,0:T(8,128)(2,1)}, bf16[4,1024,768]{2,1,0:T(8,128)(2,1)}, bf16[4,1024,1280]{2,1,0:T(8,128)(2,1)}, bf16[4,1024,1024]{2,1,0:T(8,128)(2,...) custom-call(s32[7]{0:T(128)} %stack.35.refs_0_, ...), custom_call_target="tpu_custom_call" | custom-call | tf_op jit(solution)/shard_map/fore/pallas_call | solution.py:961
  157.5 43.6 %middle.1 = (bf16[2,1024,1024]{2,1,0:T(8,128)(2,1)}, bf16[2,1024,1024]{2,1,0:T(8,128)(2,1)}, f32[512,1024]{1,0:T(8,128)}, bf16[512,1024]{1,0:T(8,128)(2,1)}, bf1...) custom-call(s32[7]{0:T(128)} %stack.35.refs_0_, ...), custom_call_target="tpu_custom_call" | custom-call | tf_op jit(solution)/shard_map/middle/pallas_call | solution.py:1235
  201.1 147.2 %back.1 = (f32[32,640]{1,0:T(8,128)}, f32[128,1024]{1,0:T(8,128)}, f32[128,1024]{1,0:T(8,128)}, f32[128,768]{1,0:T(8,128)}, f32[128,256]{1,0:T(8,128)}, /*index=5*/f32[8,128]{1,0:T(8,128)}) custom-call(s32[7]{0:T(128)} %stack.35.refs_0_, f32[16]{0:T(128)} %reshape.123.refs_1_, f32[8,128]{1,0:T(8,128)} %get-tuple-element.85.refs_2_, ...), custom_call_target="tpu_custom_call" | custom-call | tf_op jit(solution)/shard_map/back/pallas_call | solution.py:1595
  348.3 7.8 %step.1 = (f32[1,1]{1,0:T(1,128)}, f32[1,1]{1,0:T(1,128)}, f32[32,288]{1,0:T(8,128)}, f32[32,288]{1,0:T(8,128)}, f32[32,288]{1,0:T(8,128)}, /*index=5*/f32[32,39...) custom-call(f32[8,128]{1,0:T(8,128)} %get-tuple-element.102.sums, ...), custom_call_target="tpu_custom_call" | custom-call | tf_op jit(solution)/shard_map/step/pallas_call | solution.py:1638
  (17 shorter events, 0.2 us)
Async XLA Ops:
  0.7 10.2 %copy-start = (s32[2,1,1024]{2,1,0:T(1,128)S(1)}, s32[2,1,1024]{2,1,0:T(1,128)}, u32[]{:S(2)}) copy-start(s32[2,1,1024]{2,1,0:T(1,128)} %param.33) | copy-start | bytes 24580
  0.7 17.9 %copy-start.2 = (f32[1024,128]{1,0:T(8,128)S(1)}, f32[1024,128]{1,0:T(8,128)}, u32[]{:S(2)}) copy-start(f32[1024,128]{1,0:T(8,128)} %refs_5_.1) | copy-start | bytes 1572868
  0.7 18.7 %copy-start.4 = (bf16[2,1,1024,80]{2,3,1,0:T(8,128)(2,1)S(1)}, bf16[2,1,1024,80]{2,3,1,0:T(8,128)(2,1)}, u32[]{:S(2)}) copy-start(bf16[2,1,1024,80]{2,3,1,0:T(8,128)(2,1)} %param.29) | copy-start | bytes 983044
  0.7 18.7 %copy-start.3 = (bf16[2,1,1024,80]{2,3,1,0:T(8,128)(2,1)S(1)}, bf16[2,1,1024,80]{2,3,1,0:T(8,128)(2,1)}, u32[]{:S(2)}) copy-start(bf16[2,1,1024,80]{2,3,1,0:T(8,128)(2,1)} %param.28) | copy-start | bytes 983044
  348.3 7.8 %copy-start.1 = (s32[2,1,1024]{2,1,0:T(1,128)S(1)}, s32[2,1,1024]{2,1,0:T(1,128)}, u32[]{:S(2)}) copy-start(s32[2,1,1024]{2,1,0:T(1,128)} %param.33) | copy-start | bytes 24580
